TPU v7x, 256 devices: a whole 4x4x8 slice. The times are simulated.
256 devices in a mesh: row: 32 (over x, z_hi, core), col: 8 (over z_lo, y).
Axes of the slice: x: 4, y: 4, z: 8 (z_hi: 4, z_lo: 2; z = z_hi * 2 + z_lo), core: 2. Of those that a mesh axis runs over, the one named last changes fastest.
Arguments:
- pair_acts: bfloat16 [384, 384, 128], P('row', 'col'), may hold values from -6 to 6
- token_valid: int32 [384], replicated, may hold values from 0 to 1, as said below
- norm_gain: float32 [128], replicated, may hold values from 0.5 to 1.5
- proj_weight: bfloat16 [128, 640], replicated, may hold values from -0.5 to 0.5
- out_gain: float32 [128], replicated, may hold values from 0.5 to 1.5
- out_weight: bfloat16 [128, 128], replicated, may hold values from -0.5 to 0.5
- out_cotangent: bfloat16 [384, 384, 128], P('row', 'col'), may hold values from -6 to 6
Outputs:
- update: bfloat16 [384, 384, 128], P('row', 'col')
- grad_pair: bfloat16 [384, 384, 128], P('row', 'col')
- grad_weight: float32 [128, 640], replicated
Inputs may be any that keep to these rules, and one draw needn't show every extreme that they name: `token_valid`: in every aligned block of 12 tokens the valid tokens come before the padding, and at least half of the block is valid.
All inputs are finite; a program needn't handle non-finite values.
Results may differ from a plain program's by a relative error of at most 0.018.
Values may be sent and summed in bfloat16 or wider, within the bound.
No kernel may reach another device: no remote copies, remote signals or barrier semaphores. Data moves between devices by JAX's collectives and lax.ppermute only.
A program may use at most 128 MiB of HBM per device.

v0:
```python
import jax
import jax.numpy as jnp
from jax import lax
from jax.sharding import PartitionSpec as P

EPSILON = 1e-05


def normalize(values):
    center = jnp.mean(values, axis=-1, keepdims=True)
    shifted = values - center
    inv_std = lax.rsqrt(jnp.mean(shifted * shifted, axis=-1, keepdims=True) + EPSILON)
    return (shifted * inv_std, inv_std)


def norm_grad(upstream, scaled, inv_std):
    first = jnp.mean(upstream, axis=-1, keepdims=True)
    second = jnp.mean(upstream * scaled, axis=-1, keepdims=True)
    return inv_std * (upstream - first - scaled * second)


def per_device(pair_acts, token_valid, norm_gain, proj_weight, out_gain, out_weight, out_cotangent):
    num_rows = pair_acts.shape[0]
    num_cols = pair_acts.shape[1]
    channels = pair_acts.shape[2]
    hidden_dim = out_weight.shape[0]
    width_all = proj_weight.shape[1]
    full_len = token_valid.shape[0]
    validity = token_valid.astype(jnp.float32)
    valid_rows = lax.dynamic_slice_in_dim(validity, lax.axis_index("row") * num_rows, num_rows)
    valid_cols = lax.dynamic_slice_in_dim(validity, lax.axis_index("col") * num_cols, num_cols)
    pair_mask = (valid_rows[:, None] * valid_cols[None, :])[:, :, None]
    scaled_in, inv_in = normalize(pair_acts.astype(jnp.float32))
    normed = (scaled_in * norm_gain).astype(jnp.bfloat16)
    normed_flat = normed.reshape(-1, channels)
    projected = jnp.dot(normed_flat, proj_weight, preferred_element_type=jnp.float32).reshape(
        num_rows, num_cols, width_all
    )
    left_sig = jax.nn.sigmoid(projected[:, :, 0:hidden_dim])
    left_val = projected[:, :, hidden_dim : 2 * hidden_dim]
    right_sig = jax.nn.sigmoid(projected[:, :, 2 * hidden_dim : 3 * hidden_dim])
    right_val = projected[:, :, 3 * hidden_dim : 4 * hidden_dim]
    gate_sig = jax.nn.sigmoid(projected[:, :, 4 * hidden_dim :])
    left_side = (left_sig * left_val * pair_mask).astype(jnp.bfloat16)
    right_side = (right_sig * right_val * pair_mask).astype(jnp.bfloat16)
    tri_part = jnp.einsum(
        "ikh,jkh->ijh",
        left_side,
        lax.all_gather(right_side, "row", axis=0, tiled=True),
        preferred_element_type=jnp.float32,
    )
    tri_sum = lax.psum_scatter(tri_part, "col", scatter_dimension=1, tiled=True)
    scaled_out, inv_out = normalize(tri_sum)
    normed_out = (scaled_out * out_gain).astype(jnp.bfloat16)
    out_proj = jnp.dot(
        normed_out.reshape(-1, hidden_dim), out_weight, preferred_element_type=jnp.float32
    ).reshape(num_rows, num_cols, channels)
    gate_mask = gate_sig * pair_mask
    update = (gate_mask * out_proj).astype(jnp.bfloat16)
    cotangent = out_cotangent.astype(jnp.float32)
    back_out = (cotangent * gate_mask).astype(jnp.bfloat16)
    back_norm = (
        jnp.dot(
            back_out.reshape(-1, channels), out_weight.T, preferred_element_type=jnp.float32
        ).reshape(num_rows, num_cols, hidden_dim)
        * out_gain
    )
    back_tri = norm_grad(back_norm, scaled_out, inv_out).astype(jnp.bfloat16)
    back_whole = lax.all_gather(back_tri, "col", axis=1, tiled=True)
    columns = back_whole
    back_left = jnp.einsum(
        "ijh,jkh->ikh",
        columns,
        lax.all_gather(right_side, "row", axis=0, tiled=True),
        preferred_element_type=jnp.float32,
    )
    columns = back_whole
    back_right = lax.psum_scatter(
        jnp.einsum("ijh,ikh->jkh", columns, left_side, preferred_element_type=jnp.float32).astype(
            jnp.bfloat16
        ),
        "row",
        scatter_dimension=0,
        tiled=True,
    ).astype(jnp.float32)
    back_left = back_left * pair_mask
    back_right = back_right * pair_mask
    back_gate = cotangent * pair_mask * out_proj * gate_sig * (1.0 - gate_sig)
    back_proj = jnp.concatenate(
        [
            back_left * left_val * left_sig * (1.0 - left_sig),
            back_left * left_sig,
            back_right * right_val * right_sig * (1.0 - right_sig),
            back_right * right_sig,
            back_gate,
        ],
        axis=-1,
    ).astype(jnp.bfloat16)
    back_flat = back_proj.reshape(-1, width_all)
    back_normed = (
        jnp.dot(back_flat, proj_weight.T, preferred_element_type=jnp.float32).reshape(
            num_rows, num_cols, channels
        )
        * norm_gain
    )
    grad_pair = norm_grad(back_normed, scaled_in, inv_in).astype(jnp.bfloat16)
    weight_term = (
        lax.dot_general(
            normed_flat, back_flat, (((0,), (0,)), ((), ())), preferred_element_type=jnp.float32
        )
        / full_len
    )
    grad_weight = lax.psum(weight_term, ("row", "col"))
    return (update, grad_pair, grad_weight)


def solution(mesh):
    placed = (P("row", "col", None), P(), P(), P(), P(), P(), P("row", "col", None))
    return jax.shard_map(
        per_device,
        mesh=mesh,
        in_specs=placed,
        out_specs=(P("row", "col", None), P("row", "col", None), P()),
        check_vma=False,
    )
```

profile of v0, /device:TPU:1, one launch (start us, length us, event | category | flops | bytes accessed | tf_op | source)
XLA Modules:
  0.0 579.7 jit_solution(7344521318242436571)
XLA Ops:
  7.2 0.0 copy-start
  7.2 0.0 all-gather.3.cloned.1.call-start
  7.2 0.7 convert_element_type.47
  7.9 0.1 dynamic_slice.7
  8.0 0.1 dynamic_slice.6
  8.1 1.1 convert_reduce_fusion
  9.2 1.2 fusion.11
  10.4 0.1 broadcast_multiply_fusion
  10.5 0.0 copy-done
  10.5 1.3 fusion.27
  11.8 0.8 multiply_convert_fusion.7
  12.6 0.0 all-gather.3.cloned.1.call-update
  12.7 0.0 reduce-scatter.3.cloned.1.call-start
  12.7 0.4 copy.47
  13.2 0.0 copy-start.1
  13.2 66.5 %all-gather.3.cloned.1.call-done = bf16[384,48,128]{2,1,0:T(8,128)(2,1)} async-done(((bf16[12,48,128]{2,1,0:T(8,128)(2,1)}), bf16[384,48,128]{2,1,0:T(8,128)(2,1)}) %all-gather.3.cloned.1.call-update) | async-done | bytes 4718608 | tf_op jit(solution)/shard_map/all_gather | solution.py:49
  79.7 17.9 %copy.46 = bf16[384,48,128]{1,0,2:T(8,128)(2,1)} copy(bf16[384,48,128]{2,1,0:T(8,128)(2,1)} %all-gather.3.cloned.1.call-done) | data formatting | bytes 9437184 | tf_op jit(solution)/shard_map/all_gather | solution.py:49
  97.6 0.0 copy-done.1
  97.6 10.7 %convolution_bitcast_fusion = f32[12,384,128]{1,0,2:T(8,128)} fusion(bf16[384,48,128]{1,0,2:T(8,128)(2,1)} %copy.46, bf16[12,48,128]{1,0,2:T(8,128)(2,1)S(1)} %copy.47), kind=kOutput, calls=%fused_computation.1 | convolution fusion | flops 56623104 | bytes 7225344 | tf_op jit(solution)/shard_map/ikh,jkh->ijh/dot_general | solution.py:46
  108.3 3.6 copy.48
  111.9 0.0 copy-start.7
  111.9 0.0 copy-start.8
  111.9 0.0 reduce-scatter.3.cloned.1.call-update
  112.0 0.0 all-gather.5.cloned.1.call-start
  112.0 42.4 %reduce-scatter.3.cloned.1.call-done = f32[12,48,128]{2,0,1:T(8,128)} async-done(((f32[12,384,128]{2,0,1:T(8,128)}), f32[12,48,128]{2,0,1:T(8,128)}) %reduce-scatter.3.cloned.1.call-update) | async-done | bytes 294928 | tf_op jit(solution)/shard_map/reduce_scatter | solution.py:52
  154.4 0.0 copy-start.3
  154.4 1.2 reduce_sum.74
  155.7 0.1 copy.49
  155.7 1.3 multiply_reduce_fusion.1
  157.0 0.0 copy-done.4
  157.1 0.0 copy-done.7
  157.1 0.0 copy-done.8
  157.1 1.5 fusion.45
  158.6 0.0 copy-done.3
  158.6 1.0 multiply_convert_fusion.4
  159.6 0.0 all-gather.5.cloned.1.call-update
  159.7 0.0 reduce-scatter.5.cloned.1.call-start
  159.7 40.4 %all-gather.5.cloned.1.call-done = bf16[12,384,128]{2,1,0:T(8,128)(2,1)} async-done(((bf16[12,48,128]{2,1,0:T(8,128)(2,1)}), bf16[12,384,128]{2,1,0:T(8,128)(2,1)}) %all-gather.5.cloned.1.call-update) | async-done | bytes 1179664 | tf_op jit(solution)/shard_map/all_gather | solution.py:69
  200.1 2.2 copy.52
  202.3 4.8 fusion.47
  207.1 7.5 %copy.56 = bf16[128,48,384]{0,1,2:T(8,128)(2,1)} copy(bf16[128,48,384]{2,1,0:T(8,128)(2,1)} %fusion.47) | data formatting | bytes 9437184 | tf_op jit(solution)/shard_map/ijh,ikh->jkh/dot_general | solution.py:79
  214.7 0.0 reduce-scatter.5.cloned.1.call-update
  214.7 0.2 all-reduce.2.cloned.1.call-start
  214.9 2.0 multiply_convert_fusion.5
  216.9 7.8 %fusion.46 = f32[128,48,12]{1,2,0:T(8,128)} fusion(bf16[384,48,128]{1,0,2:T(8,128)(2,1)} %copy.46, bf16[12,384,128]{1,0,2:T(8,128)(2,1)S(1)} %copy.52), kind=kOutput, calls=%fused_computation.77 | convolution fusion | flops 56623104 | bytes 6193152 | tf_op jit(solution)/shard_map/ijh,jkh->ikh/dot_general | solution.py:71
  224.8 1.5 copy.53
  226.3 0.0 copy-start.5
  226.3 0.1 fusion.30
  226.5 0.0 copy-start.2
  226.5 0.0 copy-start.6
  226.5 0.2 fusion.31
  226.7 93.1 %reduce-scatter.5.cloned.1.call-done = bf16[12,48,128]{2,1,0:T(8,128)(2,1)} async-done(((bf16[384,48,128]{2,1,0:T(8,128)(2,1)}), bf16[12,48,128]{2,1,0:T(8,128)(2,1)}) %reduce-scatter.5.cloned.1.call-update) | async-done | bytes 147472 | tf_op jit(solution)/shard_map/reduce_scatter | solution.py:78
  319.7 1.1 fusion.32
  320.9 1.1 fusion.33
  321.9 0.0 copy-done.5
  322.0 0.2 fusion.34
  322.2 0.0 copy-done.2
  322.2 0.0 copy-done.6
  322.2 0.5 fusion.44
  322.7 1.3 fusion
  324.0 0.0 all-reduce.2.cloned.1.call-update
  324.0 1.0 fusion.10
  325.1 246.4 %all-reduce.2.cloned.1.call-done = f32[128,640]{1,0:T(8,128)} async-done(((f32[128,640]{1,0:T(8,128)}), f32[128,640]{1,0:T(8,128)}) %all-reduce.2.cloned.1.call-update) | async-done | bytes 327696 | tf_op jit(solution)/shard_map/psum | solution.py:113
  571.5 1.7 copy.74
  (8 shorter events, 0.0 us)
Async XLA Ops:
  7.2 3.3 copy-start
  7.2 72.5 %all-gather.3.cloned.1.call-start = ((), (), s32[]{:S(2)}) async-start(), calls=%async_computation.2 | async-start | bytes 4866048 | tf_op jit(solution)/shard_map/all_gather | solution.py:49
  12.7 141.8 %reduce-scatter.3.cloned.1.call-start = ((), (), s32[]{:S(2)}) async-start(), calls=%async_computation.3 | async-start | bytes 3538944 | tf_op jit(solution)/shard_map/reduce_scatter | solution.py:52
  13.2 84.4 %copy-start.1 = (bf16[12,48,128]{1,0,2:T(8,128)(2,1)}, bf16[12,48,128]{1,0,2:T(8,128)(2,1)S(1)}, u32[]{:S(2)}) copy-start(bf16[12,48,128]{1,0,2:T(8,128)(2,1)S(1)} %copy.47) | copy-start | bytes 442372
  111.9 45.1 %copy-start.4 = (bf16[12,48,128]{2,1,0:T(8,128)(2,1)S(1)}, bf16[12,48,128]{2,1,0:T(8,128)(2,1)}, u32[]{:S(2)}) copy-start(bf16[12,48,128]{2,1,0:T(8,128)(2,1)} %param.13) | copy-start | bytes 442372
  111.9 45.1 %copy-start.7 = (bf16[128,128]{1,0:T(8,128)(2,1)S(1)}, bf16[128,128]{1,0:T(8,128)(2,1)}, u32[]{:S(2)}) copy-start(bf16[128,128]{1,0:T(8,128)(2,1)} %param.12) | copy-start | bytes 98308
  111.9 45.1 %copy-start.8 = (f32[128]{0:T(128)S(1)}, f32[128]{0:T(128)}, u32[]{:S(2)}) copy-start(f32[128]{0:T(128)} %param.11) | copy-start | bytes 1540
  112.0 88.2 %all-gather.5.cloned.1.call-start = ((), (), s32[]{:S(2)}) async-start(), calls=%async_computation.4 | async-start | bytes 1327104 | tf_op jit(solution)/shard_map/all_gather | solution.py:69
  154.4 4.2 copy-start.3
  159.7 160.1 %reduce-scatter.5.cloned.1.call-start = ((), (), s32[]{:S(2)}) async-start(), calls=%async_computation.5 | async-start | bytes 4866048 | tf_op jit(solution)/shard_map/reduce_scatter | solution.py:78
  214.7 356.8 %all-reduce.2.cloned.1.call-start = ((), (), s32[]{:S(2)}) async-start(), calls=%async_computation.6 | async-start | bytes 655360 | tf_op jit(solution)/shard_map/psum | solution.py:113
  226.3 95.7 %copy-start.5 = (bf16[12,48,128]{2,1,0:T(8,128)(2,1)S(1)}, bf16[12,48,128]{2,1,0:T(8,128)(2,1)}, u32[]{:S(2)}) copy-start(bf16[12,48,128]{2,1,0:T(8,128)(2,1)} %param.13) | copy-start | bytes 442372
  226.5 95.7 %copy-start.2 = (bf16[12,48,128]{2,1,0:T(8,128)(2,1)S(1)}, bf16[12,48,128]{2,1,0:T(8,128)(2,1)}, u32[]{:S(2)}) copy-start(bf16[12,48,128]{2,1,0:T(8,128)(2,1)} %param.7) | copy-start | bytes 442372
  226.5 95.7 %copy-start.6 = (f32[128]{0:T(128)S(1)}, f32[128]{0:T(128)}, u32[]{:S(2)}) copy-start(f32[128]{0:T(128)} %param.9) | copy-start | bytes 1540
Sparse Core Ops, SparseCore 0:
  12.8 66.8 all-gather.2
  112.1 42.2 reduce-scatter.2
  159.8 40.3 all-gather.4
  214.8 104.8 reduce-scatter.4
  326.6 244.8 all-reduce.1
where the time goes:
time: 581 us; the launch traced here: 580 us
  waiting for transfers between devices  489 us (84%)
  local copies, waits for them, and re-layouts  35.2 us (6%)
  matrix products  30 us (5%)
  between operations  14 us (2%)
  other arithmetic  11.2 us (2%)
    psum x1, waiting for transfers between devices, per_device(): grad_weight = lax.psum(weight_term, ('row', 'col'))  246 us
    reduce_scatter x1, waiting for transfers between devices, per_device(): lax.psum_scatter(jnp.einsum('ijh,ikh->jkh', columns, left_side, preferred...  93.1 us
    all_gather x1, waiting for transfers between devices, per_device(): lax.all_gather(right_side, 'row', axis=0, tiled=True)  66.5 us
    reduce_scatter x1, waiting for transfers between devices, per_device(): tri_sum = lax.psum_scatter(tri_part, 'col', scatter_dimension=1, tiled=True)  42.4 us
    all_gather x1, waiting for transfers between devices, per_device(): back_whole = lax.all_gather(back_tri, 'col', axis=1, tiled=True)  40.4 us
    all_gather x1, local copies, waits for them, and re-layouts, per_device(): lax.all_gather(right_side, 'row', axis=0, tiled=True)  17.9 us
  transfers between devices with their start and end apart: 5, of which 5 were waited for; matrix products, arithmetic and copies ran while one was open for 2% of the time, Pallas kernels for 0%

commit v1 on v0

v1 whole, which is shorter than its diff:
```python
import jax
import jax.numpy as jnp
from jax import lax
from jax.sharding import PartitionSpec as P

EPSILON = 1e-05
BF16 = jnp.bfloat16
F32 = jnp.float32
AXES = ("row", "col")


def normalize(values):
    center = jnp.mean(values, axis=-1, keepdims=True)
    shifted = values - center
    inv_std = lax.rsqrt(jnp.mean(shifted * shifted, axis=-1, keepdims=True) + EPSILON)
    return (shifted * inv_std, inv_std)


def norm_grad(upstream, scaled, inv_std):
    first = jnp.mean(upstream, axis=-1, keepdims=True)
    second = jnp.mean(upstream * scaled, axis=-1, keepdims=True)
    return inv_std * (upstream - first - scaled * second)


def exchange(chunks):
    return lax.all_to_all(chunks, AXES, 0, 0, tiled=True)


def other_core(values, num_rows):
    return lax.ppermute(values, "row", [(i, i ^ 1) for i in range(num_rows)])


def gather_plane(chunks, rows, cols, part, wide):
    return (
        chunks.reshape(rows, cols, part, wide).transpose(2, 0, 1, 3).reshape(part * rows, cols * wide)
    )


def scatter_plane(plane, rows, cols, part, wide):
    return (
        plane.reshape(part, rows, cols, wide).transpose(1, 2, 0, 3).reshape(rows * cols, part * wide)
    )


def make_per_device(num_r, num_c):
    def per_device(pair_acts, token_valid, norm_gain, proj_weight, out_gain, out_weight, out_cotangent):
        na, nb, channels = pair_acts.shape
        hidden = out_weight.shape[0]
        width_all = proj_weight.shape[1]
        full_len = token_valid.shape[0]
        pairs = na * nb
        half_a = na // 2
        chips = num_r // 2
        core = lax.axis_index("row") % 2
        validity = token_valid.astype(F32)
        valid_rows = lax.dynamic_slice_in_dim(validity, lax.axis_index("row") * na, na)
        valid_cols = lax.dynamic_slice_in_dim(validity, lax.axis_index("col") * nb, nb)
        pair_mask = (valid_rows[:, None] * valid_cols[None, :]).reshape(pairs, 1)

        scaled_in, inv_in = normalize(pair_acts.reshape(pairs, channels).astype(F32))
        normed = (scaled_in * norm_gain).astype(BF16)
        projected = jnp.dot(normed, proj_weight, preferred_element_type=F32)
        left_sig = jax.nn.sigmoid(projected[:, 0:hidden])
        left_val = projected[:, hidden : 2 * hidden]
        right_sig = jax.nn.sigmoid(projected[:, 2 * hidden : 3 * hidden])
        right_val = projected[:, 3 * hidden : 4 * hidden]
        gate_sig = jax.nn.sigmoid(projected[:, 4 * hidden :])
        left_side = (left_sig * left_val * pair_mask).astype(BF16)
        right_side = (right_sig * right_val * pair_mask).astype(BF16)

        sides = jnp.stack(
            [left_side.T.reshape(chips, num_c, pairs), right_side.T.reshape(chips, num_c, pairs)], axis=1
        )
        mine = gather_plane(exchange(sides.reshape(num_r * num_c, pairs)), num_r, num_c, na, nb)
        theirs = other_core(mine, num_r)
        left = jnp.where(core == 0, mine, theirs)
        right = jnp.where(core == 0, theirs, mine)
        right_nat = right.reshape(na, num_r, full_len).transpose(1, 0, 2).reshape(full_len, full_len)
        left_half = lax.dynamic_slice_in_dim(left, core * (full_len // 2), full_len // 2)
        tri = lax.dot_general(
            left_half, right_nat, (((1,), (1,)), ((), ())), preferred_element_type=F32
        ).astype(BF16)
        tri = exchange(scatter_plane(tri, num_r, num_c, half_a, nb))
        tri_sum = (
            tri.reshape(chips, 2, num_c, pairs // 2)
            .transpose(1, 3, 0, 2)
            .reshape(pairs, hidden)
            .astype(F32)
        )

        scaled_out, inv_out = normalize(tri_sum)
        normed_out = (scaled_out * out_gain).astype(BF16)
        out_proj = jnp.dot(normed_out, out_weight, preferred_element_type=F32)
        gate_mask = gate_sig * pair_mask
        update = (gate_mask * out_proj).astype(BF16)
        cotangent = out_cotangent.reshape(pairs, channels).astype(F32)
        back_out = (cotangent * gate_mask).astype(BF16)
        back_norm = jnp.dot(back_out, out_weight.T, preferred_element_type=F32) * out_gain
        back_tri = norm_grad(back_norm, scaled_out, inv_out).astype(BF16)

        back = back_tri.reshape(2, pairs // 2, chips, num_c).transpose(2, 0, 3, 1)
        back = exchange(back.reshape(num_r * num_c, pairs // 2))
        back_half = gather_plane(back, num_r, num_c, half_a, nb)
        back_other = other_core(back_half, num_r)
        back_plane = jnp.concatenate(
            [
                jnp.where(core == 0, back_half, back_other),
                jnp.where(core == 0, back_other, back_half),
            ]
        )
        back_perm = (
            back_plane.reshape(full_len, num_r, na).transpose(0, 2, 1).reshape(full_len, full_len)
        )
        back_side = jnp.dot(
            jnp.where(core == 0, back_perm, back_perm.T),
            jnp.where(core == 0, right, left),
            preferred_element_type=F32,
        ).astype(BF16)
        back_sides = exchange(scatter_plane(back_side, num_r, num_c, na, nb))
        back_sides = back_sides.reshape(chips, 2, num_c, pairs)
        back_left = back_sides[:, 0].reshape(hidden, pairs).T.astype(F32) * pair_mask
        back_right = back_sides[:, 1].reshape(hidden, pairs).T.astype(F32) * pair_mask

        back_gate = cotangent * pair_mask * out_proj * gate_sig * (1.0 - gate_sig)
        back_proj = jnp.concatenate(
            [
                back_left * left_val * left_sig * (1.0 - left_sig),
                back_left * left_sig,
                back_right * right_val * right_sig * (1.0 - right_sig),
                back_right * right_sig,
                back_gate,
            ],
            axis=-1,
        ).astype(BF16)
        weight_term = lax.dot_general(
            normed, back_proj, (((0,), (0,)), ((), ())), preferred_element_type=F32
        ).astype(BF16)
        parts = exchange(weight_term.reshape(num_r * num_c, -1))
        total = jnp.sum(parts.astype(F32), axis=0) / full_len
        spread = jnp.broadcast_to(total.astype(BF16), (num_r * num_c,) + total.shape)
        grad_weight = exchange(spread).reshape(channels, width_all).astype(F32)

        back_normed = jnp.dot(back_proj, proj_weight.T, preferred_element_type=F32) * norm_gain
        grad_pair = norm_grad(back_normed, scaled_in, inv_in).astype(BF16)
        return (
            update.reshape(na, nb, channels),
            grad_pair.reshape(na, nb, channels),
            grad_weight,
        )

    return per_device


def solution(mesh):
    placed = (P("row", "col", None), P(), P(), P(), P(), P(), P("row", "col", None))
    return jax.shard_map(
        make_per_device(mesh.shape["row"], mesh.shape["col"]),
        mesh=mesh,
        in_specs=placed,
        out_specs=(P("row", "col", None), P("row", "col", None), P()),
        check_vma=False,
    )
```

time: 581 us -> 198 us (0.34)
  waiting for transfers between devices: 489 us -> 49.7 us
  blocking collectives: 0 us -> 76.1 us
  matrix products: 30 us -> 5.05 us
  starting transfers between devices: 0.39 us -> 18.6 us
  between operations: 14 us -> 1.26 us
  other arithmetic: 11.2 us -> 22.8 us
  local copies, waits for them, and re-layouts: 35.2 us -> 23.9 us
    psum x1 -> x0, waiting for transfers between devices: 246 us -> none  [per_device(): grad_weight = lax.psum(weight_term, ('row', 'col'))]
    reduce_scatter x2 -> x0, waiting for transfers between devices: 135 us -> none  [the longest x1 93.1 us: per_device(): lax.psum_scatter(jnp.einsum('ijh,ikh->jkh', columns, left_side, preferred...]
    all_gather x2 -> x0, waiting for transfers between devices: 107 us -> none  [the longest x1 66.5 us: per_device(): lax.all_gather(right_side, 'row', axis=0, tiled=True)]
    all_to_all x0 -> x3, blocking collectives: none -> 76.1 us  [exchange(): return lax.all_to_all(chunks, AXES, 0, 0, tiled=True)]
    all_to_all x0 -> x3, waiting for transfers between devices: none -> 47.5 us  [exchange(): return lax.all_to_all(chunks, AXES, 0, 0, tiled=True)]
    dot_general x8 -> x7, matrix products: 30 us -> 5.05 us  [the longest x1 1.5 us: per_device(): jnp.dot(back_out, out_weight.T, preferred_element_type=F32) * out_gain]
    all_gather x2 -> x0, local copies, waits for them, and re-layouts: 20.1 us -> none  [the longest x1 17.9 us: per_device(): lax.all_gather(right_side, 'row', axis=0, tiled=True)]
    all_to_all x0 -> x3, starting transfers between devices: none -> 17.1 us  [exchange(): return lax.all_to_all(chunks, AXES, 0, 0, tiled=True)]
  transfers between devices with their start and end apart: 5 -> 5, of which waited for: 5 -> 5; matrix products, arithmetic and copies ran while one was open for 2% -> 1% of each run, Pallas kernels for 0% -> 0%
where the time goes in v1:
time: 198 us; the launch traced here: 197 us
  blocking collectives  76.1 us (38%)
  waiting for transfers between devices  49.7 us (25%)
  local copies, waits for them, and re-layouts  23.9 us (12%)
  other arithmetic  22.8 us (12%)
  starting transfers between devices  18.6 us (9%)
  matrix products  5.05 us (3%)
    all_to_all x3, blocking collectives, exchange(): return lax.all_to_all(chunks, AXES, 0, 0, tiled=True)  76.1 us
    all_to_all x3, waiting for transfers between devices, exchange(): return lax.all_to_all(chunks, AXES, 0, 0, tiled=True)  47.5 us
    all_to_all x3, starting transfers between devices, exchange(): return lax.all_to_all(chunks, AXES, 0, 0, tiled=True)  17.1 us
    all_to_all x7, other arithmetic, exchange(): return lax.all_to_all(chunks, AXES, 0, 0, tiled=True)  12.2 us
    unnamed x31, local copies, waits for them, and re-layouts  6.32 us
    reshape x4, local copies, waits for them, and re-layouts, scatter_plane(): plane.reshape(part, rows, cols, wide).transpose(1, 2, 0, 3)  4.09 us
  transfers between devices with their start and end apart: 5, of which 5 were waited for; matrix products, arithmetic and copies ran while one was open for 1% of the time, Pallas kernels for 0%

profile of v1, /device:TPU:1, one launch (start us, length us, event | category | flops | bytes accessed | tf_op | source)
XLA Modules:
  0.0 197.4 jit_solution(976178539168727406)
XLA Ops:
  0.7 1.1 convert_reduce_fusion.2
  1.8 1.2 multiply_reduce_fusion.3
  3.0 0.7 convert_element_type.102
  4.1 1.1 fusion.22
  5.3 1.0 fusion.42
  6.9 0.5 broadcast.150
  7.4 0.8 reduce.9
  8.2 0.4 reshape.223
  8.6 34.0 %all_to_all.54 = bf16[256,2,288]{2,1,0:T(2,128)(2,1)S(1)} all-to-all(bf16[256,2,288]{2,1,0:T(2,128)(2,1)S(1)} %reshape.223), channel_id=1, replica_groups=mesh['row'=32,'col'=8] {'row','col'}, dimensions={0} | all-to-all | bytes 589824 | tf_op jit(solution)/shard_map/all_to_all | solution.py:26
  42.5 0.6 reshape.224
  43.1 2.1 %reduce.5 = bf16[256,576]{1,0:T(8,128)(2,1)S(1)} reduce(bf16[256,1,576]{2,1,0:T(2,128)(2,1)S(1)} %reshape.224, bf16[]{:T(256)} %constant.52), dimensions={1}, to_apply=%all_to_all.35.reduce_sub_computation | reduce | bytes 589826 | tf_op jit(solution)/shard_map/all_to_all | solution.py:26
  45.2 1.0 reshape.198
  46.2 1.1 copy.44
  47.3 1.8 reshape.199
  49.1 0.7 collective-permute-start
  49.8 1.2 collective-permute-done
  51.3 0.3 convolution_convert_fusion.2
  51.6 0.3 reshape.202
  51.9 0.3 copy.67
  52.2 0.6 all_to_all.45
  52.8 1.9 reduce.10
  54.8 20.9 %all_to_all.55 = bf16[256,2,144]{2,1,0:T(2,128)(2,1)S(1)} all-to-all(bf16[256,2,144]{2,1,0:T(2,128)(2,1)S(1)} %reshape.225), channel_id=1, replica_groups=mesh['row'=32,'col'=8] {'row','col'}, dimensions={0} | all-to-all | bytes 294912 | tf_op jit(solution)/shard_map/all_to_all | solution.py:26
  75.7 0.3 reshape.226
  76.6 0.3 reshape.213
  77.0 1.5 fusion.46
  78.6 0.4 multiply_convert_fusion.1
  79.4 0.7 reduce.11
  80.2 21.2 %all_to_all.56 = bf16[256,2,144]{2,1,0:T(2,128)(2,1)S(1)} all-to-all(bf16[256,2,144]{2,1,0:T(2,128)(2,1)S(1)} %reshape.227), channel_id=1, replica_groups=mesh['row'=32,'col'=8] {'row','col'}, dimensions={0} | all-to-all | bytes 294912 | tf_op jit(solution)/shard_map/all_to_all | solution.py:26
  101.4 0.3 reshape.228
  101.7 1.2 reduce.6
  102.9 0.4 reshape.205
  103.4 0.3 reshape.206
  103.7 0.8 collective-permute-start.1
  104.5 1.0 collective-permute-done.1
  105.5 0.9 copy.55
  106.4 1.0 reshape.207
  107.5 0.2 copy.57
  107.8 0.3 convolution_convert_fusion
  108.2 1.5 reshape.209
  109.7 1.9 copy.66
  111.6 1.9 all_to_all.46
  113.5 3.7 %reduce.12 = bf16[256,576]{1,0:T(8,128)(2,1)S(1)} reduce(bf16[256,1,576]{2,1,0:T(2,128)(2,1)} %all_to_all.46, bf16[]{:T(256)} %broadcast.150), dimensions={1}, to_apply=%all_to_all.46.reduce_sub_computation | reduce | bytes 589826 | tf_op jit(solution)/shard_map/all_to_all | solution.py:26
  117.2 1.1 reshape.229
  118.3 5.6 %all-to-all-start.3 = ((bf16[256,2,288]{2,1,0:T(2,128)(2,1)}), bf16[256,2,288]{2,1,0:T(2,128)(2,1)S(1)}, u32[]{:S(2)}, u32[]{:S(2)}) async-start(bf16[256,2,288]{2,1,0:T(2,128)(2,1)} %reshape.229), calls=%async_computation.3 | async-start | bytes 786432 | tf_op jit(solution)/shard_map/all_to_all | solution.py:26
  124.0 1.1 multiply_convert_fusion.2
  125.1 17.5 %all-to-all-done.3 = bf16[256,2,288]{2,1,0:T(2,128)(2,1)S(1)} async-done(((bf16[256,2,288]{2,1,0:T(2,128)(2,1)}), bf16[256,2,288]{2,1,0:T(2,128)(2,1)S(1)}, u32[]{:S(2)}, u32[]{:S(2)}) %all-to-all-start.3) | async-done | bytes 294944 | tf_op jit(solution)/shard_map/all_to_all | solution.py:26
  142.6 0.6 reshape.230
  144.5 0.4 copy-done.4
  145.1 0.3 convolution_convert_fusion.1
  145.7 1.9 reduce.13
  147.6 0.8 reshape.231
  148.4 5.7 %all-to-all-start.4 = ((bf16[256,2,160]{2,1,0:T(2,128)(2,1)}), bf16[256,2,160]{2,1,0:T(2,128)(2,1)S(1)}, u32[]{:S(2)}, u32[]{:S(2)}) async-start(bf16[256,2,160]{2,1,0:T(2,128)(2,1)} %reshape.231), calls=%async_computation.4 | async-start | bytes 524288 | tf_op jit(solution)/shard_map/all_to_all | solution.py:26
  154.1 0.5 fusion.45
  154.7 15.2 %all-to-all-done.4 = bf16[256,2,160]{2,1,0:T(2,128)(2,1)S(1)} async-done(((bf16[256,2,160]{2,1,0:T(2,128)(2,1)}), bf16[256,2,160]{2,1,0:T(2,128)(2,1)S(1)}, u32[]{:S(2)}, u32[]{:S(2)}) %all-to-all-start.4) | async-done | bytes 163872 | tf_op jit(solution)/shard_map/all_to_all | solution.py:26
  169.9 0.3 reshape.232
  170.2 0.5 convert_reduce_fusion.1
  170.9 1.9 reduce.14
  172.8 0.8 reshape.233
  173.6 5.8 %all-to-all-start.5 = ((bf16[256,2,160]{2,1,0:T(2,128)(2,1)}), bf16[256,2,160]{2,1,0:T(2,128)(2,1)S(1)}, u32[]{:S(2)}, u32[]{:S(2)}) async-start(bf16[256,2,160]{2,1,0:T(2,128)(2,1)} %reshape.233), calls=%async_computation.5 | async-start | bytes 524288 | tf_op jit(solution)/shard_map/all_to_all | solution.py:26
  179.4 1.0 multiply_convert_fusion
  180.4 14.7 %all-to-all-done.5 = bf16[256,2,160]{2,1,0:T(2,128)(2,1)S(1)} async-done(((bf16[256,2,160]{2,1,0:T(2,128)(2,1)}), bf16[256,2,160]{2,1,0:T(2,128)(2,1)S(1)}, u32[]{:S(2)}, u32[]{:S(2)}) %all-to-all-start.5) | async-done | bytes 163872 | tf_op jit(solution)/shard_map/all_to_all | solution.py:26
  195.2 0.3 reshape.234
  195.4 1.1 convert_reduce_fusion
  196.5 0.8 reshape.217
  (68 shorter events, 4.8 us)
Async XLA Ops:
  0.6 4.6 %copy-start = (bf16[128,640]{1,0:T(8,128)(2,1)S(1)}, bf16[128,640]{1,0:T(8,128)(2,1)}, u32[]{:S(2)}) copy-start(bf16[128,640]{1,0:T(8,128)(2,1)} %param.10) | copy-start | bytes 491524
  49.1 1.9 collective-permute-start
  76.1 1.0 copy-start.7
  76.1 1.0 copy-start.8
  77.0 2.1 %copy-start.2 = (f32[576,128]{1,0:T(8,128)}, f32[576,128]{1,0:T(8,128)S(1)}, u32[]{:S(2)}) copy-start(f32[576,128]{1,0:T(8,128)S(1)} %copy.50) | copy-start | bytes 884740
  103.7 1.8 collective-permute-start.1
  113.5 10.4 %copy-start.3 = (f32[576,128]{1,0:T(8,128)S(1)}, f32[576,128]{1,0:T(8,128)}, u32[]{:S(2)}) copy-start(f32[576,128]{1,0:T(8,128)} %copy-done.2) | copy-start | bytes 884740
  118.3 24.3 %all-to-all-start.3 = ((bf16[256,2,288]{2,1,0:T(2,128)(2,1)}), bf16[256,2,288]{2,1,0:T(2,128)(2,1)S(1)}, u32[]{:S(2)}, u32[]{:S(2)}) async-start(bf16[256,2,288]{2,1,0:T(2,128)(2,1)} %reshape.229), calls=%async_computation.3 | async-start | bytes 786432 | tf_op jit(solution)/shard_map/all_to_all | solution.py:26
  143.6 0.9 copy-start.5
  143.9 1.0 copy-start.4
  143.9 1.2 copy-start.6
  148.4 21.5 %all-to-all-start.4 = ((bf16[256,2,160]{2,1,0:T(2,128)(2,1)}), bf16[256,2,160]{2,1,0:T(2,128)(2,1)S(1)}, u32[]{:S(2)}, u32[]{:S(2)}) async-start(bf16[256,2,160]{2,1,0:T(2,128)(2,1)} %reshape.231), calls=%async_computation.4 | async-start | bytes 524288 | tf_op jit(solution)/shard_map/all_to_all | solution.py:26
  154.7 24.7 %copy-start.1 = (bf16[12,48,128]{2,1,0:T(8,128)(2,1)S(1)}, bf16[12,48,128]{2,1,0:T(8,128)(2,1)}, u32[]{:S(2)}) copy-start(bf16[12,48,128]{2,1,0:T(8,128)(2,1)} %param.7) | copy-start | bytes 442372
  173.6 21.5 %all-to-all-start.5 = ((bf16[256,2,160]{2,1,0:T(2,128)(2,1)}), bf16[256,2,160]{2,1,0:T(2,128)(2,1)S(1)}, u32[]{:S(2)}, u32[]{:S(2)}) async-start(bf16[256,2,160]{2,1,0:T(2,128)(2,1)} %reshape.233), calls=%async_computation.5 | async-start | bytes 524288 | tf_op jit(solution)/shard_map/all_to_all | solution.py:26

commit v2 on v1

v2 whole, which is shorter than its diff:
```python
import functools

import jax
import jax.numpy as jnp
from jax import lax
from jax.experimental import pallas as pl
from jax.experimental.pallas import tpu as pltpu
from jax.sharding import PartitionSpec as P

EPSILON = 1e-05
BF16 = jnp.bfloat16
F32 = jnp.float32
AXES = ("row", "col")
LANES = 128
SLOT = 64
VMEM_LIMIT = 48 * 1024 * 1024

NT = (((1,), (1,)), ((), ()))
NN = (((1,), (0,)), ((), ()))
TN = (((0,), (0,)), ((), ()))


def matmul(lhs, rhs, dims=NN):
    return lax.dot_general(lhs, rhs, dims, preferred_element_type=F32)


def column(row_ref):
    return jnp.broadcast_to(row_ref[...], (LANES, LANES)).T


def swap_halves(values):
    return pltpu.roll(values, SLOT, 1)


def low_half(shape):
    return lax.broadcasted_iota(jnp.int32, shape, 1) < SLOT


def spread(pairs_ref, spread_ref):
    na, nb, channels = pairs_ref.shape
    for a in range(na):
        spread_ref[a * SLOT : a * SLOT + nb, :] = pairs_ref[a].astype(F32)
        spread_ref[a * SLOT + nb : (a + 1) * SLOT, :] = jnp.zeros((SLOT - nb, channels), F32)


def store_pairs(out_ref, t, values):
    nb = out_ref.shape[1]
    turned = values.T
    out_ref[2 * t] = turned[0:nb].astype(out_ref.dtype)
    out_ref[2 * t + 1] = turned[SLOT : SLOT + nb].astype(out_ref.dtype)


def masks(valid_ref, na, nb):
    lane = lax.broadcasted_iota(jnp.int32, (1, LANES), 1)
    place = lane % SLOT
    first_row = lax.axis_index("row") * na
    first_col = lax.axis_index("col") * nb
    cols = jnp.zeros((1, LANES), jnp.int32)
    for b in range(nb):
        cols = jnp.where(place == b, valid_ref[first_col + b], cols)
    found = []
    for t in range(na // 2):
        rows = jnp.where(lane < SLOT, valid_ref[first_row + 2 * t], valid_ref[first_row + 2 * t + 1])
        found.append((rows * cols).astype(F32))
    return found


def tile_norm(values):
    center = jnp.mean(values, axis=0, keepdims=True)
    shifted = values - center
    inv_std = lax.rsqrt(jnp.mean(shifted * shifted, axis=0, keepdims=True) + EPSILON)
    return shifted * inv_std, inv_std


def tile_norm_grad(upstream, scaled, inv_std):
    first = jnp.mean(upstream, axis=0, keepdims=True)
    second = jnp.mean(upstream * scaled, axis=0, keepdims=True)
    return inv_std * (upstream - first - scaled * second)


def norm_tiles(spread_ref, gain_ref, normed_ref):
    gain = column(gain_ref)
    tiles = spread_ref.shape[0] // LANES
    for t in range(tiles):
        at = slice(t * LANES, (t + 1) * LANES)
        scaled, _ = tile_norm(spread_ref[at, :].T)
        normed_ref[:, at] = (scaled * gain).astype(BF16)


def put_channels(chunk_ref, t, depth, side, values):
    for m in range(values.shape[0] // 8):
        start = depth * (16 * m + 8 * side) + t
        chunk_ref[pl.ds(start, 8, stride=depth), :] = values[8 * m : 8 * m + 8, :]


def get_channels(chunk_ref, t, depth, side, hidden):
    return jnp.concatenate(
        [
            chunk_ref[pl.ds(depth * (16 * m + 8 * side) + t, 8, stride=depth), :]
            for m in range(hidden // 8)
        ],
        axis=0,
    )


def chunks_to_plane(chunk_ref, plane_ref, depth, tiles, first_a, na):
    low = low_half((8, LANES))
    for pair in range(4):
        for t in range(tiles):
            for lo in range(4):
                start = depth * (8 * lo + 2 * pair) + t
                even = chunk_ref[pl.ds(start, 8, stride=32 * depth), :]
                odd = chunk_ref[pl.ds(start + depth, 8, stride=32 * depth), :]
                row = na * lo + first_a + 2 * t
                plane_ref[pair, pl.ds(row, 8, stride=SLOT), :] = jnp.where(low, even, swap_halves(odd))
                plane_ref[pair, pl.ds(row + 1, 8, stride=SLOT), :] = jnp.where(
                    low, swap_halves(even), odd
                )


def plane_to_chunks(plane_ref, chunk_ref, depth, tiles, first_a, na):
    low = low_half((8, LANES))
    for pair in range(4):
        for t in range(tiles):
            for lo in range(4):
                row = na * lo + first_a + 2 * t
                upper = plane_ref[pair, pl.ds(row, 8, stride=SLOT), :]
                lower = plane_ref[pair, pl.ds(row + 1, 8, stride=SLOT), :]
                start = depth * (8 * lo + 2 * pair) + t
                chunk_ref[pl.ds(start, 8, stride=32 * depth), :] = jnp.where(
                    low, upper, swap_halves(lower)
                )
                chunk_ref[pl.ds(start + depth, 8, stride=32 * depth), :] = jnp.where(
                    low, swap_halves(upper), lower
                )


def clear_gaps(plane_ref, used):
    rows = plane_ref.shape[1]
    for pair in range(plane_ref.shape[0]):
        for group in range(rows // SLOT):
            plane_ref[pair, group * SLOT + used : (group + 1) * SLOT, :] = jnp.zeros(
                (SLOT - used, LANES), F32
            )


def whole_plane(plane_ref):
    return jnp.concatenate([plane_ref[pair].astype(BF16) for pair in range(4)], axis=1)


def my_core():
    return lax.axis_index("row") % 2


def sides_kernel(valid_ref, acts_ref, gain_ref, weight_ref, out_ref, spread_ref, normed_ref, chunk_ref):
    na, nb, _ = acts_ref.shape
    tiles = na // 2
    hidden = weight_ref.shape[0]
    spread(acts_ref, spread_ref)
    norm_tiles(spread_ref, gain_ref, normed_ref)
    mask = masks(valid_ref, na, nb)
    projected = matmul(weight_ref[:, 0 : 4 * hidden], normed_ref[...], TN)
    for t in range(tiles):
        at = slice(t * LANES, (t + 1) * LANES)
        for side in range(2):
            base = 2 * side * hidden
            gate = jax.nn.sigmoid(projected[base : base + hidden, at])
            value = projected[base + hidden : base + 2 * hidden, at]
            put_channels(chunk_ref, t, tiles, side, gate * value * mask[t])
    out_ref[...] = chunk_ref[...].astype(BF16)


def tri_kernel(na, nb, mine_ref, theirs_ref, tri_ref, keep_ref, chunk_ref, plane_ref, tri_chunk_ref):
    tiles = na // 2
    half = tiles // 2
    core = my_core()
    chunk_ref[0] = mine_ref[...].astype(F32)
    chunk_ref[1] = theirs_ref[...].astype(F32)
    for side in range(2):
        clear_gaps(plane_ref.at[side], nb)
        chunks_to_plane(chunk_ref.at[side], plane_ref.at[side], tiles, tiles, 0, na)
    keep_ref[...] = whole_plane(plane_ref.at[1])
    left = whole_plane(plane_ref.at[core])
    right = whole_plane(plane_ref.at[1 - core])
    tri = matmul(left, right, NT)
    for pair in range(4):
        plane_ref[0, pair] = tri[:, pair * LANES : (pair + 1) * LANES]
    plane_to_chunks(plane_ref.at[0], tri_chunk_ref, 4, half, core * 2 * half, na)
    tri_ref[...] = tri_chunk_ref[...].astype(BF16)


def middle_kernel(
    valid_ref,
    tri_ref,
    acts_ref,
    cotangent_ref,
    gain_ref,
    weight_ref,
    out_gain_ref,
    out_weight_ref,
    update_ref,
    back_ref,
    gate_ref,
    spread_ref,
    normed_ref,
    tri_chunk_ref,
    tri_plane_ref,
    normed_out_ref,
    back_out_ref,
):
    na, nb, _ = acts_ref.shape
    tiles = na // 2
    half = tiles // 2
    hidden = out_weight_ref.shape[0]
    spread(acts_ref, spread_ref)
    norm_tiles(spread_ref, gain_ref, normed_ref)
    mask = masks(valid_ref, na, nb)
    gate_sig = jax.nn.sigmoid(matmul(weight_ref[:, 4 * hidden :], normed_ref[...], TN))
    spread(cotangent_ref, spread_ref)
    tri_chunk_ref[...] = tri_ref[...].astype(F32)
    out_gain = column(out_gain_ref)
    inv_out = []
    for t in range(tiles):
        at = slice(t * LANES, (t + 1) * LANES)
        scaled, inv = tile_norm(get_channels(tri_chunk_ref, t % half, 4, t // half, hidden))
        inv_out.append(inv)
        tri_plane_ref[:, at] = scaled
        normed_out_ref[:, at] = (scaled * out_gain).astype(BF16)
        gate_mask = gate_sig[:, at] * mask[t]
        back_out_ref[:, at] = (spread_ref[at, :].T * gate_mask).astype(BF16)
    out_proj = matmul(out_weight_ref[...], normed_out_ref[...], TN)
    back_norm = matmul(out_weight_ref[...], back_out_ref[...])
    for t in range(tiles):
        at = slice(t * LANES, (t + 1) * LANES)
        back_tri = tile_norm_grad(back_norm[:, at] * out_gain, tri_plane_ref[:, at], inv_out[t])
        put_channels(tri_chunk_ref, t % half, 4, t // half, back_tri)
    back_ref[...] = tri_chunk_ref[...].astype(BF16)
    for t in range(tiles):
        at = slice(t * LANES, (t + 1) * LANES)
        gate = gate_sig[:, at]
        gate_mask = gate * mask[t]
        store_pairs(update_ref, t, gate_mask * out_proj[:, at])
        cotangent = spread_ref[at, :].T
        gate_ref[:, at] = (cotangent * mask[t] * out_proj[:, at] * gate * (1.0 - gate)).astype(BF16)


def back_kernel(
    na, nb, mine_ref, theirs_ref, keep_ref, out_ref, back_chunk_ref, plane_ref, chunk_ref, whole_ref
):
    tiles = na // 2
    half = tiles // 2
    core = my_core()
    back_chunk_ref[core] = mine_ref[...].astype(F32)
    back_chunk_ref[1 - core] = theirs_ref[...].astype(F32)
    clear_gaps(plane_ref, nb)
    for side in range(2):
        chunks_to_plane(back_chunk_ref.at[side], plane_ref, 4, half, side * 2 * half, na)
    whole_ref[...] = whole_plane(plane_ref)

    def keep_tiles(product):
        for pair in range(4):
            plane_ref[pair] = product[:, pair * LANES : (pair + 1) * LANES]

    @pl.when(core == 0)
    def _():
        keep_tiles(matmul(whole_ref[...], keep_ref[...]))

    @pl.when(core == 1)
    def _():
        keep_tiles(matmul(whole_ref[...], keep_ref[...], TN))

    plane_to_chunks(plane_ref, chunk_ref, tiles, tiles, 0, na)
    out_ref[...] = chunk_ref[...].astype(BF16)


def weight_kernel(
    valid_ref,
    back_ref,
    acts_ref,
    gain_ref,
    weight_ref,
    gate_ref,
    grad_weight_ref,
    back_proj_ref,
    spread_ref,
    normed_ref,
    chunk_ref,
):
    na, nb, _ = acts_ref.shape
    tiles = na // 2
    hidden = weight_ref.shape[0]
    spread(acts_ref, spread_ref)
    norm_tiles(spread_ref, gain_ref, normed_ref)
    mask = masks(valid_ref, na, nb)
    projected = matmul(weight_ref[:, 0 : 4 * hidden], normed_ref[...], TN)
    chunk_ref[...] = back_ref[...].astype(F32)
    back_proj_ref[4 * hidden :, :] = gate_ref[...]
    for t in range(tiles):
        at = slice(t * LANES, (t + 1) * LANES)
        for side in range(2):
            base = 2 * side * hidden
            upstream = get_channels(chunk_ref, t, tiles, side, hidden) * mask[t]
            gate = jax.nn.sigmoid(projected[base : base + hidden, at])
            value = projected[base + hidden : base + 2 * hidden, at]
            back_proj_ref[base : base + hidden, at] = (upstream * value * gate * (1.0 - gate)).astype(
                BF16
            )
            back_proj_ref[base + hidden : base + 2 * hidden, at] = (upstream * gate).astype(BF16)
    grad_weight_ref[...] = matmul(normed_ref[...], back_proj_ref[...], NT).astype(BF16)


def pair_kernel(acts_ref, gain_ref, weight_ref, back_proj_ref, grad_pair_ref, spread_ref):
    na, nb, _ = acts_ref.shape
    spread(acts_ref, spread_ref)
    gain = column(gain_ref)
    back_normed = matmul(weight_ref[...], back_proj_ref[...])
    for t in range(na // 2):
        at = slice(t * LANES, (t + 1) * LANES)
        scaled, inv = tile_norm(spread_ref[at, :].T)
        store_pairs(grad_pair_ref, t, tile_norm_grad(back_normed[:, at] * gain, scaled, inv))


def local_call(body, outs, scratch, flops, smem_first=False, inputs=1):
    specs = [pl.BlockSpec(memory_space=pltpu.VMEM)] * inputs
    if smem_first:
        specs[0] = pl.BlockSpec(memory_space=pltpu.SMEM)
    return pl.pallas_call(
        body,
        out_shape=outs,
        in_specs=specs,
        out_specs=jax.tree.map(lambda _: pl.BlockSpec(memory_space=pltpu.VMEM), outs),
        scratch_shapes=scratch,
        compiler_params=pltpu.CompilerParams(vmem_limit_bytes=VMEM_LIMIT),
        cost_estimate=pl.CostEstimate(flops=flops, bytes_accessed=2_000_000, transcendentals=0),
    )


def exchange(chunks, depth):
    devices = chunks.shape[0] // depth
    split = chunks.reshape(devices, depth // 2, 2, chunks.shape[1])
    return lax.all_to_all(split, AXES, 0, 0, tiled=True).reshape(chunks.shape)


def make_per_device(num_r, num_c):
    devices = num_r * num_c

    def other_core(values):
        return lax.ppermute(values, "row", [(i, i ^ 1) for i in range(num_r)])

    def per_device(pair_acts, token_valid, norm_gain, proj_weight, out_gain, out_weight, out_cotangent):
        na, nb, channels = pair_acts.shape
        hidden = out_weight.shape[0]
        width_all = proj_weight.shape[1]
        full_len = token_valid.shape[0]
        tiles = na // 2
        lanes = tiles * LANES
        plane = (num_r // 4) * SLOT
        full = jax.ShapeDtypeStruct((devices * tiles, LANES), BF16)
        part = jax.ShapeDtypeStruct((devices * 4, LANES), BF16)
        pairs = jax.ShapeDtypeStruct(pair_acts.shape, BF16)
        gain = norm_gain.reshape(1, channels)
        spread_scratch = pltpu.VMEM((lanes, channels), F32)
        normed_scratch = pltpu.VMEM((channels, lanes), BF16)
        full_scratch = pltpu.VMEM(full.shape, F32)

        sides = local_call(
            sides_kernel,
            full,
            [spread_scratch, normed_scratch, full_scratch],
            100_000_000,
            smem_first=True,
            inputs=4,
        )(token_valid, pair_acts, gain, proj_weight)
        mine = exchange(sides, tiles)
        theirs = other_core(mine)
        tri, keep = local_call(
            functools.partial(tri_kernel, na, nb),
            (part, jax.ShapeDtypeStruct((plane, plane), BF16)),
            [
                pltpu.VMEM((2,) + full.shape, F32),
                pltpu.VMEM((2, 4, plane, LANES), F32),
                pltpu.VMEM(part.shape, F32),
            ],
            300_000_000,
            inputs=2,
        )(mine, theirs)
        tri = exchange(tri, 4)
        update, back, gate = local_call(
            middle_kernel,
            (pairs, part, jax.ShapeDtypeStruct((channels, lanes), BF16)),
            [
                spread_scratch,
                normed_scratch,
                pltpu.VMEM(part.shape, F32),
                pltpu.VMEM((hidden, lanes), F32),
                pltpu.VMEM((hidden, lanes), BF16),
                pltpu.VMEM((channels, lanes), BF16),
            ],
            100_000_000,
            smem_first=True,
            inputs=8,
        )(
            token_valid,
            tri,
            pair_acts,
            out_cotangent,
            gain,
            proj_weight,
            out_gain.reshape(1, hidden),
            out_weight,
        )
        back = exchange(back, 4)
        back_sides = local_call(
            functools.partial(back_kernel, na, nb),
            full,
            [
                pltpu.VMEM((2,) + part.shape, F32),
                pltpu.VMEM((4, plane, LANES), F32),
                full_scratch,
                pltpu.VMEM((plane, plane), BF16),
            ],
            300_000_000,
            inputs=3,
        )(back, other_core(back), keep)
        back_sides = exchange(back_sides, tiles)
        weight_term, back_proj = local_call(
            weight_kernel,
            (
                jax.ShapeDtypeStruct((channels, width_all), BF16),
                jax.ShapeDtypeStruct((width_all, lanes), BF16),
            ),
            [spread_scratch, normed_scratch, full_scratch],
            200_000_000,
            smem_first=True,
            inputs=6,
        )(token_valid, back_sides, pair_acts, gain, proj_weight, gate)
        grad_pair = local_call(pair_kernel, pairs, [spread_scratch], 100_000_000, inputs=4)(
            pair_acts, gain, proj_weight, back_proj
        )
        parts = lax.all_to_all(weight_term.reshape(devices, -1), AXES, 0, 0, tiled=True)
        total = jnp.sum(parts.astype(F32), axis=0) / full_len
        copies = jnp.broadcast_to(total.astype(BF16), (devices,) + total.shape)
        grad_weight = lax.all_to_all(copies, AXES, 0, 0, tiled=True)
        return update, grad_pair, grad_weight.reshape(channels, width_all).astype(F32)

    return per_device


def solution(mesh):
    placed = (P("row", "col", None), P(), P(), P(), P(), P(), P("row", "col", None))
    return jax.shard_map(
        make_per_device(mesh.shape["row"], mesh.shape["col"]),
        mesh=mesh,
        in_specs=placed,
        out_specs=(P("row", "col", None), P("row", "col", None), P()),
        check_vma=False,
    )
```

time: 198 us -> 171 us (0.86)
  blocking collectives: 76.1 us -> 121 us
  waiting for transfers between devices: 49.7 us -> 17.1 us
  other arithmetic: 22.8 us -> 5.47 us
  local copies, waits for them, and re-layouts: 23.9 us -> 7.79 us
  starting transfers between devices: 18.6 us -> 7.1 us
  Pallas kernels: 0 us -> 11.3 us
  matrix products: 5.05 us -> 0 us
    all_to_all x3 -> x5, blocking collectives: 76.1 us -> 121 us  [the longest x4 100 us: exchange(): return lax.all_to_all(split, AXES, 0, 0, tiled=True).reshape(chunks.shape)]
    all_to_all x3 -> x1, waiting for transfers between devices: 47.5 us -> 14.6 us  [per_device(): grad_weight = lax.all_to_all(copies, AXES, 0, 0, tiled=True)]
    all_to_all x3 -> x1, starting transfers between devices: 17.1 us -> 5.74 us  [per_device(): grad_weight = lax.all_to_all(copies, AXES, 0, 0, tiled=True)]
    pallas_call x0 -> x6, Pallas kernels: none -> 11.3 us  [the longest x1 2.86 us: per_device(): local_call(functools.partial(tri_kernel, na, nb), (part, jax.ShapeDtypeSt...]
    all_to_all x7 -> x1, other arithmetic: 12.2 us -> 1.93 us  [per_device(): lax.all_to_all(weight_term.reshape(devices, -1), AXES, 0, 0, tiled=True)]
    reshape x12 -> x0, local copies, waits for them, and re-layouts: 9.08 us -> none  [the longest x4 4.09 us: scatter_plane(): plane.reshape(part, rows, cols, wide).transpose(1, 2, 0, 3)]
    dot_general x7 -> x0, matrix products: 5.05 us -> none  [the longest x1 1.5 us: per_device(): jnp.dot(back_out, out_weight.T, preferred_element_type=F32) * out_gain]
    all_to_all x5 -> x2, local copies, waits for them, and re-layouts: 3.24 us -> 0.72 us  [per_device(): lax.all_to_all(weight_term.reshape(devices, -1), AXES, 0, 0, tiled=True)]
  transfers between devices with their start and end apart: 5 -> 3, of which waited for: 5 -> 3; matrix products, arithmetic and copies ran while one was open for 1% -> 0% of each run, Pallas kernels for 0% -> 1%
where the time goes in v2:
time: 171 us
  blocking collectives  121 us (71%)
  waiting for transfers between devices  17.1 us (10%)
  Pallas kernels  11.3 us (7%)
  local copies, waits for them, and re-layouts  7.79 us (5%)
  starting transfers between devices  7.1 us (4%)
  other arithmetic  5.47 us (3%)
    all_to_all x4, blocking collectives, exchange(): return lax.all_to_all(split, AXES, 0, 0, tiled=True).reshape(chunks.shape)  100 us
    all_to_all x1, blocking collectives, per_device(): lax.all_to_all(weight_term.reshape(devices, -1), AXES, 0, 0, tiled=True)  21.2 us
    all_to_all x1, waiting for transfers between devices, per_device(): grad_weight = lax.all_to_all(copies, AXES, 0, 0, tiled=True)  14.6 us
    unnamed x24, local copies, waits for them, and re-layouts  6.01 us
    all_to_all x1, starting transfers between devices, per_device(): grad_weight = lax.all_to_all(copies, AXES, 0, 0, tiled=True)  5.74 us
  transfers between devices with their start and end apart: 3, of which 3 were waited for; matrix products, arithmetic and copies ran while one was open for 0% of the time, Pallas kernels for 1%

profile of v2, /device:TPU:1, one launch (start us, length us, event | category | flops | bytes accessed | tf_op | source)
XLA Modules:
  0.0 170.8 jit_solution(14231312013361161767)
XLA Ops:
  0.6 0.0 copy-start.8
  0.6 0.6 copy-done.8
  1.3 0.0 copy-start
  1.3 0.9 copy-done
  2.2 0.0 copy-start.2
  2.2 0.9 copy-done.2
  3.1 0.0 copy-start.6
  3.1 0.7 copy-done.6
  3.8 1.2 shard_map.94
  5.0 33.9 %all_to_all.36 = bf16[256,3,2,128]{3,2,1,0:T(2,128)(2,1)S(1)} all-to-all(bf16[256,3,2,128]{3,2,1,0:T(2,128)(2,1)S(1)} %bitcast.11), channel_id=1, replica_groups=mesh['row'=32,'col'=8] {'row','col'}, dimensions={0} | all-to-all | bytes 786432 | tf_op jit(solution)/shard_map/all_to_all | solution.py:341
  38.9 0.7 collective-permute-start
  39.6 1.3 collective-permute-done.theirs_ref
  40.9 2.9 %shard_map.95 = (bf16[1024,128]{1,0:T(8,128)(2,1)S(1)}, bf16[512,512]{1,0:T(8,128)(2,1)S(1)}) custom-call(bf16[1536,128]{1,0:T(8,128)(2,1)S(1)} %bitcast.17, bf16[1536,128]{1,0:T(8,128)(2,1)S(1)} %collective-permute-done.theirs_ref), custom_call_target="tpu_custom_call" | custom-call | flops 300000000 | bytes 2000000 | tf_op jit(solution)/shard_map/pallas_call | solution.py:376
  43.8 0.0 copy-start.1
  43.8 0.0 copy-start.3
  43.8 0.0 copy-start.4
  43.8 0.0 copy-start.5
  43.8 21.0 %all_to_all.37 = bf16[256,2,2,128]{3,2,1,0:T(2,128)(2,1)S(1)} all-to-all(bf16[256,2,2,128]{3,2,1,0:T(2,128)(2,1)S(1)} %bitcast.18), channel_id=1, replica_groups=mesh['row'=32,'col'=8] {'row','col'}, dimensions={0} | all-to-all | bytes 524288 | tf_op jit(solution)/shard_map/all_to_all | solution.py:341
  64.8 0.0 copy-start.9
  64.9 0.0 copy-done.1
  64.9 0.0 copy-done.3
  64.9 0.0 copy-done.4
  64.9 0.0 copy-done.5
  64.9 0.6 copy-done.9
  65.5 2.1 %shard_map.96 = (bf16[12,48,128]{2,1,0:T(8,128)(2,1)}, bf16[1024,128]{1,0:T(8,128)(2,1)S(1)}, bf16[128,768]{1,0:T(8,128)(2,1)S(1)}) custom-call(s32[384]{0:T(512)S(1)} %copy-done.6, bf16[1024,128]{1,0:T(8,128)(2,1)S(1)} %bitcast.13, bf16[12,48,128]{2,1,0:T(8,128)(2,1)S(1)} %copy-done.3, bf16[12,48,128]{2,1,0:T(8,128)(2,1)S(1)} %copy-done.4, ...), custom_call_target="tpu_custom_call" | custom-call | flops 100000000 | bytes 2000000 | tf_op jit(solution)/shard_map/pallas_call | solution.py:388
  67.6 21.2 %all_to_all.38 = bf16[256,2,2,128]{3,2,1,0:T(2,128)(2,1)S(1)} all-to-all(bf16[256,2,2,128]{3,2,1,0:T(2,128)(2,1)S(1)} %bitcast.19), channel_id=1, replica_groups=mesh['row'=32,'col'=8] {'row','col'}, dimensions={0} | all-to-all | bytes 524288 | tf_op jit(solution)/shard_map/all_to_all | solution.py:341
  88.9 0.7 collective-permute-start.1
  89.6 1.2 collective-permute-done.1.theirs_ref
  90.7 2.5 %shard_map.97 = bf16[1536,128]{1,0:T(8,128)(2,1)S(1)} custom-call(bf16[1024,128]{1,0:T(8,128)(2,1)S(1)} %bitcast.15, bf16[1024,128]{1,0:T(8,128)(2,1)S(1)} %collective-permute-done.1.theirs_ref, bf16[512,512]{1,0:T(8,128)(2,1)S(1)} %get-tuple-element.13.keep_ref), custom_call_target="tpu_custom_call" | custom-call | flops 300000000 | bytes 2000000 | tf_op jit(solution)/shard_map/pallas_call | solution.py:413
  93.2 23.8 %all_to_all.39 = bf16[256,3,2,128]{3,2,1,0:T(2,128)(2,1)S(1)} all-to-all(bf16[256,3,2,128]{3,2,1,0:T(2,128)(2,1)S(1)} %bitcast.12), channel_id=1, replica_groups=mesh['row'=32,'col'=8] {'row','col'}, dimensions={0} | all-to-all | bytes 786432 | tf_op jit(solution)/shard_map/all_to_all | solution.py:341
  117.1 0.0 copy-start.7
  117.1 0.7 copy-done.7
  117.7 1.5 shard_map.98
  119.3 0.2 all_to_all.29
  119.5 0.5 broadcast.5
  120.0 1.9 %reduce.3 = bf16[256,320]{1,0:T(8,128)(2,1)S(1)} reduce(bf16[256,1,320]{2,1,0:T(2,128)(2,1)S(1)} %all_to_all.29, bf16[]{:T(256)} %broadcast.5), dimensions={1}, to_apply=%all_to_all.29.reduce_sub_computation | reduce | bytes 327682 | tf_op jit(solution)/shard_map/all_to_all | solution.py:440
  121.9 0.1 reshape.61
  122.1 21.2 %all_to_all.40 = bf16[256,2,160]{2,1,0:T(2,128)(2,1)S(1)} all-to-all(bf16[256,2,160]{2,1,0:T(2,128)(2,1)S(1)} %reshape.61), channel_id=1, replica_groups=mesh['row'=32,'col'=8] {'row','col'}, dimensions={0} | all-to-all | bytes 327680 | tf_op jit(solution)/shard_map/all_to_all | solution.py:440
  143.2 0.3 reshape.62
  143.5 0.5 convert_reduce_fusion.1
  144.0 0.2 broadcast_in_dim.3
  144.2 1.9 %reduce.4 = bf16[256,320]{1,0:T(8,128)(2,1)S(1)} reduce(bf16[256,1,320]{2,1,0:T(2,128)(2,1)S(1)} %broadcast_in_dim.3, bf16[]{:T(256)} %broadcast.5), dimensions={1}, to_apply=%broadcast_in_dim.3.reduce_sub_computation | reduce | bytes 327682 | tf_op jit(solution)/shard_map/broadcast_in_dim | solution.py:442
  146.2 0.8 reshape.63
  147.0 5.7 %all-to-all-start.5 = ((bf16[256,2,160]{2,1,0:T(2,128)(2,1)}), bf16[256,2,160]{2,1,0:T(2,128)(2,1)S(1)}, u32[]{:S(2)}, u32[]{:S(2)}) async-start(bf16[256,2,160]{2,1,0:T(2,128)(2,1)} %reshape.63), calls=%async_computation.5 | async-start | bytes 524288 | tf_op jit(solution)/shard_map/all_to_all | solution.py:443
  152.8 1.2 shard_map.99
  153.9 14.6 %all-to-all-done.5 = bf16[256,2,160]{2,1,0:T(2,128)(2,1)S(1)} async-done(((bf16[256,2,160]{2,1,0:T(2,128)(2,1)}), bf16[256,2,160]{2,1,0:T(2,128)(2,1)S(1)}, u32[]{:S(2)}, u32[]{:S(2)}) %all-to-all-start.5) | async-done | bytes 163872 | tf_op jit(solution)/shard_map/all_to_all | solution.py:443
  168.6 0.3 reshape.64
  168.8 1.1 convert_reduce_fusion
  169.9 0.8 reshape.59
  (1 shorter events, 0.0 us)
Async XLA Ops:
  0.6 0.7 copy-start.8
  1.3 0.9 copy-start
  2.2 0.9 copy-start.2
  3.1 0.7 copy-start.6
  38.9 2.0 %collective-permute-start = (bf16[1536,128]{1,0:T(8,128)(2,1)S(1)}, bf16[1536,128]{1,0:T(8,128)(2,1)S(1)}, u32[]{:S(2)}, u32[]{:S(2)}) collective-permute-start(bf16[1536,128]{1,0:T(8,128)(2,1)S(1)} %bitcast.16), channel_id=1, source_target_pairs={{0,8},{8,0},{16,24},{24,16},{32,40},{40,32},{48,56},{56,48},{64,72... | collective-permute-start | bytes 1179656 | tf_op jit(solution)/shard_map/ppermute | solution.py:348
  43.8 21.1 %copy-start.1 = (bf16[128,640]{1,0:T(8,128)(2,1)S(1)}, bf16[128,640]{1,0:T(8,128)(2,1)}, u32[]{:S(2)}) copy-start(bf16[128,640]{1,0:T(8,128)(2,1)} %weight_ref.7) | copy-start | bytes 491524
  43.8 21.1 %copy-start.3 = (bf16[12,48,128]{2,1,0:T(8,128)(2,1)S(1)}, bf16[12,48,128]{2,1,0:T(8,128)(2,1)}, u32[]{:S(2)}) copy-start(bf16[12,48,128]{2,1,0:T(8,128)(2,1)} %acts_ref.7) | copy-start | bytes 442372
  43.8 21.1 %copy-start.4 = (bf16[12,48,128]{2,1,0:T(8,128)(2,1)S(1)}, bf16[12,48,128]{2,1,0:T(8,128)(2,1)}, u32[]{:S(2)}) copy-start(bf16[12,48,128]{2,1,0:T(8,128)(2,1)} %cotangent_ref.1) | copy-start | bytes 442372
  43.8 21.1 %copy-start.5 = (bf16[128,128]{1,0:T(8,128)(2,1)S(1)}, bf16[128,128]{1,0:T(8,128)(2,1)}, u32[]{:S(2)}) copy-start(bf16[128,128]{1,0:T(8,128)(2,1)} %out_weight_ref.1) | copy-start | bytes 98308
  64.8 0.7 copy-start.9
  88.9 1.9 %collective-permute-start.1 = (bf16[1024,128]{1,0:T(8,128)(2,1)S(1)}, bf16[1024,128]{1,0:T(8,128)(2,1)S(1)}, u32[]{:S(2)}, u32[]{:S(2)}) collective-permute-start(bf16[1024,128]{1,0:T(8,128)(2,1)S(1)} %bitcast.14), channel_id=1, source_target_pairs={{0,8},{8,0},{16,24},{24,16},{32,40},{40,32},{48,56},{56,48},{64,72... | collective-permute-start | bytes 786440 | tf_op jit(solution)/shard_map/ppermute | solution.py:348
  117.1 0.7 copy-start.7
  147.0 21.5 %all-to-all-start.5 = ((bf16[256,2,160]{2,1,0:T(2,128)(2,1)}), bf16[256,2,160]{2,1,0:T(2,128)(2,1)S(1)}, u32[]{:S(2)}, u32[]{:S(2)}) async-start(bf16[256,2,160]{2,1,0:T(2,128)(2,1)} %reshape.63), calls=%async_computation.5 | async-start | bytes 524288 | tf_op jit(solution)/shard_map/all_to_all | solution.py:443

commit v3 on v2

v3 whole, which is shorter than its diff:
```python
import functools

import jax
import jax.numpy as jnp
from jax import lax
from jax.experimental import pallas as pl
from jax.experimental.pallas import tpu as pltpu
from jax.sharding import Mesh
from jax.sharding import PartitionSpec as P

EPSILON = 1e-05
BF16 = jnp.bfloat16
F32 = jnp.float32
ALL_AXES = ("chip", "core", "col")
CHANNEL_AXES = ("chip", "col")
LANES = 128
SLOT = 64
PIECE = 16
SIDE_ROWS = 10
TRI_ROWS = 6
VMEM_LIMIT = 48 * 1024 * 1024

NT = (((1,), (1,)), ((), ()))
NN = (((1,), (0,)), ((), ()))
TN = (((0,), (0,)), ((), ()))


def matmul(lhs, rhs, dims=NN):
    return lax.dot_general(lhs, rhs, dims, preferred_element_type=F32)


def column(row_ref):
    return jnp.broadcast_to(row_ref[...], (LANES, LANES)).T


def swap_halves(values):
    return pltpu.roll(values, SLOT, 1)


def low_half(shape):
    return lax.broadcasted_iota(jnp.int32, shape, 1) < SLOT


def spread(pairs_ref, spread_ref):
    na, nb, channels = pairs_ref.shape
    for a in range(na):
        spread_ref[a * SLOT : a * SLOT + nb, :] = pairs_ref[a].astype(F32)
        spread_ref[a * SLOT + nb : (a + 1) * SLOT, :] = jnp.zeros((SLOT - nb, channels), F32)


def store_pairs(out_ref, t, values):
    nb = out_ref.shape[1]
    turned = values.T
    out_ref[2 * t] = turned[0:nb].astype(out_ref.dtype)
    out_ref[2 * t + 1] = turned[SLOT : SLOT + nb].astype(out_ref.dtype)


def masks(valid_ref, na, nb):
    lane = lax.broadcasted_iota(jnp.int32, (1, LANES), 1)
    place = lane % SLOT
    first_row = (2 * lax.axis_index("chip") + lax.axis_index("core")) * na
    first_col = lax.axis_index("col") * nb
    cols = jnp.zeros((1, LANES), jnp.int32)
    for b in range(nb):
        cols = jnp.where(place == b, valid_ref[first_col + b], cols)
    found = []
    for t in range(na // 2):
        rows = jnp.where(lane < SLOT, valid_ref[first_row + 2 * t], valid_ref[first_row + 2 * t + 1])
        found.append((rows * cols).astype(F32))
    return found


def tile_norm(values):
    center = jnp.mean(values, axis=0, keepdims=True)
    shifted = values - center
    inv_std = lax.rsqrt(jnp.mean(shifted * shifted, axis=0, keepdims=True) + EPSILON)
    return shifted * inv_std, inv_std


def tile_norm_grad(upstream, scaled, inv_std):
    first = jnp.mean(upstream, axis=0, keepdims=True)
    second = jnp.mean(upstream * scaled, axis=0, keepdims=True)
    return inv_std * (upstream - first - scaled * second)


def norm_tiles(spread_ref, gain_ref, normed_ref):
    gain = column(gain_ref)
    tiles = spread_ref.shape[0] // LANES
    for t in range(tiles):
        at = slice(t * LANES, (t + 1) * LANES)
        scaled, _ = tile_norm(spread_ref[at, :].T)
        normed_ref[:, at] = (scaled * gain).astype(BF16)


def gap(shape):
    return lax.broadcasted_iota(jnp.int32, shape, 1) % SLOT >= SLOT - PIECE


def pack_tiles(tiles):
    free = gap(tiles[0].shape)
    rows = []
    for t in range(9):
        moved = pltpu.roll(tiles[9 + t // 3], SLOT - PIECE - PIECE * (t % 3), 1)
        rows.append(jnp.where(free, moved, tiles[t]))
    return rows


def unpack_tiles(rows):
    free = gap(rows[0].shape)
    place = lax.broadcasted_iota(jnp.int32, rows[0].shape, 1) % SLOT // PIECE
    tiles = [jnp.where(free, 0.0, row) for row in rows]
    for m in range(3):
        tile = jnp.zeros_like(rows[0])
        for p in range(3):
            moved = pltpu.roll(rows[3 * m + p], LANES - (SLOT - PIECE) + PIECE * p, 1)
            tile = jnp.where(place == p, moved, tile)
        tiles.append(tile)
    return tiles


def device_rows(chunk_ref, depth, row):
    return chunk_ref[pl.ds(row, chunk_ref.shape[0] // depth, stride=depth), :]


def put_device_rows(chunk_ref, depth, row, values):
    chunk_ref[pl.ds(row, chunk_ref.shape[0] // depth, stride=depth), :] = values


def group_rows(depth, lo, col, row):
    return pl.ds(depth * (8 * lo + col) + row, 8, stride=16 * depth)


def put_plane(plane_ref, pair, start, step, even, odd):
    low = low_half(even.shape)
    plane_ref[pair, pl.ds(start, 8, stride=step), :] = jnp.where(low, even, swap_halves(odd))
    plane_ref[pair, pl.ds(start + 1, 8, stride=step), :] = jnp.where(low, swap_halves(even), odd)


def get_plane(plane_ref, pair, start, step):
    upper = plane_ref[pair, pl.ds(start, 8, stride=step), :]
    lower = plane_ref[pair, pl.ds(start + 1, 8, stride=step), :]
    low = low_half(upper.shape)
    return jnp.where(low, upper, swap_halves(lower)), jnp.where(low, swap_halves(upper), lower)


def clear_rows(plane_ref, group, used):
    for pair in range(plane_ref.shape[0]):
        for start in range(0, plane_ref.shape[1], group):
            plane_ref[pair, start + used : start + group, :] = jnp.zeros((group - used, LANES), F32)


def whole_plane(plane_ref, rows=slice(None)):
    return jnp.concatenate([plane_ref[pair, rows, :].astype(BF16) for pair in range(4)], axis=1)


def keep_tiles(plane_ref, product):
    for pair in range(4):
        plane_ref[pair] = product[:, pair * LANES : (pair + 1) * LANES]


def sides_kernel(valid_ref, acts_ref, gain_ref, weight_ref, out_ref, spread_ref, normed_ref, chunk_ref):
    na, nb, _ = acts_ref.shape
    tiles = na // 2
    hidden = weight_ref.shape[0]
    spread(acts_ref, spread_ref)
    norm_tiles(spread_ref, gain_ref, normed_ref)
    mask = masks(valid_ref, na, nb)
    projected = matmul(weight_ref[:, 0 : 4 * hidden], normed_ref[...], TN)
    found = []
    for side in range(2):
        base = 2 * side * hidden
        for t in range(tiles):
            at = slice(t * LANES, (t + 1) * LANES)
            gate = jax.nn.sigmoid(projected[base : base + hidden, at])
            value = projected[base + hidden : base + 2 * hidden, at]
            found.append(gate * value * mask[t])
    for t, row in enumerate(pack_tiles(found)):
        put_device_rows(chunk_ref, SIDE_ROWS, t, row)
    put_device_rows(chunk_ref, SIDE_ROWS, 9, jnp.zeros((hidden, LANES), F32))
    out_ref[...] = chunk_ref[...].astype(BF16)


def tri_kernel(
    na, nb, mine_ref, theirs_ref, tri_ref, left_ref, right_ref, chunk_ref, left_plane_ref, right_plane_ref, tri_chunk_ref
):
    tiles = na // 2
    core = lax.axis_index("core")
    chunk_ref[core] = mine_ref[...].astype(F32)
    chunk_ref[1 - core] = theirs_ref[...].astype(F32)
    clear_rows(left_plane_ref, 32, 2 * na)
    clear_rows(right_plane_ref, SLOT, 4 * na)
    for side in range(2):
        for pair in range(4):
            for lo in range(2):
                both = []
                for col in (2 * pair, 2 * pair + 1):
                    both.append(
                        unpack_tiles(
                            [chunk_ref[side, group_rows(SIDE_ROWS, lo, col, t), :] for t in range(9)]
                        )
                    )
                even, odd = both
                for t in range(tiles):
                    put_plane(left_plane_ref, pair, 256 * side + na * lo + 2 * t, 32, even[t], odd[t])
                    start = na * (2 * lo + side) + 2 * t
                    put_plane(right_plane_ref, pair, start, SLOT, even[tiles + t], odd[tiles + t])
    left_ref[...] = whole_plane(left_plane_ref)
    right_ref[...] = whole_plane(right_plane_ref)
    half = pl.ds(pl.multiple_of(core * 256, 256), 256)
    tri = matmul(whole_plane(left_plane_ref, half), right_ref[...], NT)
    keep_tiles(left_plane_ref.at[:, 0:256], tri)
    for pair in range(4):
        for lo in range(2):
            for t in range(tiles):
                even, odd = get_plane(left_plane_ref, pair, na * lo + 2 * t, 32)
                tri_chunk_ref[group_rows(TRI_ROWS, lo, 2 * pair, t), :] = even
                tri_chunk_ref[group_rows(TRI_ROWS, lo, 2 * pair + 1, t), :] = odd
    tri_ref[...] = tri_chunk_ref[...].astype(BF16)


def middle_kernel(
    valid_ref,
    tri_ref,
    acts_ref,
    cotangent_ref,
    gain_ref,
    weight_ref,
    out_gain_ref,
    out_weight_ref,
    update_ref,
    back_ref,
    gate_ref,
    spread_ref,
    normed_ref,
    tri_chunk_ref,
    tri_plane_ref,
    normed_out_ref,
    back_out_ref,
):
    na, nb, _ = acts_ref.shape
    tiles = na // 2
    hidden = out_weight_ref.shape[0]
    spread(acts_ref, spread_ref)
    norm_tiles(spread_ref, gain_ref, normed_ref)
    mask = masks(valid_ref, na, nb)
    gate_sig = jax.nn.sigmoid(matmul(weight_ref[:, 4 * hidden :], normed_ref[...], TN))
    spread(cotangent_ref, spread_ref)
    tri_chunk_ref[...] = tri_ref[...].astype(F32)
    out_gain = column(out_gain_ref)
    inv_out = []
    for t in range(tiles):
        at = slice(t * LANES, (t + 1) * LANES)
        scaled, inv = tile_norm(device_rows(tri_chunk_ref, TRI_ROWS, t))
        inv_out.append(inv)
        tri_plane_ref[:, at] = scaled
        normed_out_ref[:, at] = (scaled * out_gain).astype(BF16)
        gate_mask = gate_sig[:, at] * mask[t]
        back_out_ref[:, at] = (spread_ref[at, :].T * gate_mask).astype(BF16)
    out_proj = matmul(out_weight_ref[...], normed_out_ref[...], TN)
    back_norm = matmul(out_weight_ref[...], back_out_ref[...])
    for t in range(tiles):
        at = slice(t * LANES, (t + 1) * LANES)
        gate = gate_sig[:, at]
        store_pairs(update_ref, t, gate * mask[t] * out_proj[:, at])
        cotangent = spread_ref[at, :].T
        gate_ref[:, at] = (cotangent * mask[t] * out_proj[:, at] * gate * (1.0 - gate)).astype(BF16)
    term = matmul(normed_ref[...], gate_ref[...], NT)
    free = gap(term.shape)
    for t in range(tiles):
        at = slice(t * LANES, (t + 1) * LANES)
        row = tile_norm_grad(back_norm[:, at] * out_gain, tri_plane_ref[:, at], inv_out[t])
        if t < 4:
            moved = pltpu.roll(term, SLOT - PIECE - PIECE * t, 1) if t < 3 else term
            row = jnp.where(free, moved, row)
        put_device_rows(tri_chunk_ref, TRI_ROWS, t, row)
    back_ref[...] = tri_chunk_ref[...].astype(BF16)


def back_kernel(
    na,
    nb,
    mine_ref,
    theirs_ref,
    left_ref,
    right_ref,
    out_ref,
    back_chunk_ref,
    left_plane_ref,
    right_plane_ref,
    chunk_ref,
    whole_ref,
):
    tiles = na // 2
    core = lax.axis_index("core")
    back_chunk_ref[core] = mine_ref[...].astype(F32)
    back_chunk_ref[1 - core] = theirs_ref[...].astype(F32)
    clear_rows(right_plane_ref, 32, 2 * na)
    free = gap((8, LANES))
    for side in range(2):
        for pair in range(4):
            for lo in range(2):
                for t in range(tiles):
                    even, odd = [
                        jnp.where(free, 0.0, back_chunk_ref[side, group_rows(TRI_ROWS, lo, col, t), :])
                        for col in (2 * pair, 2 * pair + 1)
                    ]
                    start = 256 * side + na * lo + 2 * t
                    put_plane(right_plane_ref, pair, start, 32, even, odd)
    whole_ref[...] = whole_plane(right_plane_ref)
    half = pl.ds(pl.multiple_of(core * 256, 256), 256)
    keep_tiles(left_plane_ref, matmul(whole_ref[half, :], right_ref[...]))
    keep_tiles(right_plane_ref, matmul(whole_ref[...], left_ref[...], TN))

    place = lax.broadcasted_iota(jnp.int32, (8, LANES), 1) % SLOT // PIECE
    total = jnp.zeros((8, LANES), F32)
    for t in range(4):
        rows = jnp.zeros((8, LANES), F32)
        for side in range(2):
            for m in range(back_chunk_ref.shape[1] // (8 * TRI_ROWS)):
                rows += back_chunk_ref[side, pl.ds(8 * TRI_ROWS * m + t, 8, stride=TRI_ROWS), :]
        rows = jnp.sum(rows, axis=0, keepdims=True)
        rows = jnp.broadcast_to(rows, (8, LANES))
        if t < 3:
            rows = pltpu.roll(rows, LANES - (SLOT - PIECE) + PIECE * t, 1)
        total = jnp.where(place == t, rows, total)
    total = total * (1.0 / (4 * 8 * na))
    for m in range(chunk_ref.shape[0] // (8 * SIDE_ROWS)):
        chunk_ref[pl.ds(8 * SIDE_ROWS * m + 9, 8, stride=SIDE_ROWS), :] = total

    for pair in range(4):
        for lo in range(2):
            found = [get_plane(left_plane_ref, pair, na * lo + 2 * t, 32) for t in range(tiles)]
            for t in range(tiles):
                start = na * (2 * lo + core) + 2 * t
                found.append(get_plane(right_plane_ref, pair, start, SLOT))
            for side in range(2):
                for t, row in enumerate(pack_tiles([both[side] for both in found])):
                    chunk_ref[group_rows(SIDE_ROWS, lo, 2 * pair + side, t), :] = row
    out_ref[...] = chunk_ref[...].astype(BF16)


def weight_kernel(
    valid_ref,
    back_ref,
    acts_ref,
    gain_ref,
    weight_ref,
    gate_ref,
    term_ref,
    back_proj_ref,
    gate_total_ref,
    spread_ref,
    normed_ref,
    chunk_ref,
    term_chunk_ref,
):
    na, nb, _ = acts_ref.shape
    tiles = na // 2
    hidden = weight_ref.shape[0]
    spread(acts_ref, spread_ref)
    norm_tiles(spread_ref, gain_ref, normed_ref)
    mask = masks(valid_ref, na, nb)
    projected = matmul(weight_ref[:, 0 : 4 * hidden], normed_ref[...], TN)
    chunk_ref[...] = back_ref[...].astype(F32)
    gate_total_ref[...] = device_rows(chunk_ref, SIDE_ROWS, 9)
    back_proj_ref[4 * hidden :, :] = gate_ref[...]
    upstreams = unpack_tiles([device_rows(chunk_ref, SIDE_ROWS, t) for t in range(9)])
    for t in range(tiles):
        at = slice(t * LANES, (t + 1) * LANES)
        for side in range(2):
            base = 2 * side * hidden
            upstream = upstreams[tiles * side + t] * mask[t]
            gate = jax.nn.sigmoid(projected[base : base + hidden, at])
            value = projected[base + hidden : base + 2 * hidden, at]
            back_proj_ref[base : base + hidden, at] = (upstream * value * gate * (1.0 - gate)).astype(
                BF16
            )
            back_proj_ref[base + hidden : base + 2 * hidden, at] = (upstream * gate).astype(BF16)
    term = matmul(normed_ref[...], back_proj_ref[0 : 4 * hidden, :], NT)
    for t in range(4):
        for m in range(hidden // 8):
            term_chunk_ref[weight_rows(m, t), :] = term[8 * m : 8 * m + 8, t * LANES : (t + 1) * LANES]
    term_ref[...] = term_chunk_ref[...].astype(BF16)


def weight_rows(chip, t):
    return pl.ds(2 * (16 * chip + 8 * (t // 2)) + t % 2, 8, stride=2)


def sum_kernel(full_len, parts_ref, out_ref):
    total = jnp.zeros((16, LANES), F32)
    for m in range(parts_ref.shape[0] // 16):
        total += parts_ref[16 * m : 16 * m + 16, :].astype(F32)
    total = total[0:8] + total[8:16]
    total = total + pltpu.roll(total, 4, 0)
    total = total + pltpu.roll(total, 2, 0)
    total = total / full_len
    total = jnp.concatenate([total, total], axis=0).astype(BF16)
    for m in range(parts_ref.shape[0] // 16):
        out_ref[16 * m : 16 * m + 16, :] = total


def grad_weight_kernel(sums_ref, gate_total_ref, out_ref, chunk_ref):
    chunk_ref[...] = sums_ref[...].astype(F32)
    for t in range(4):
        for m in range(out_ref.shape[0] // 8):
            out_ref[8 * m : 8 * m + 8, t * LANES : (t + 1) * LANES] = chunk_ref[weight_rows(m, t), :]
    out_ref[:, 4 * LANES :] = gate_total_ref[...]


def pair_kernel(acts_ref, gain_ref, weight_ref, back_proj_ref, grad_pair_ref, spread_ref):
    na, nb, _ = acts_ref.shape
    spread(acts_ref, spread_ref)
    gain = column(gain_ref)
    back_normed = matmul(weight_ref[...], back_proj_ref[...])
    for t in range(na // 2):
        at = slice(t * LANES, (t + 1) * LANES)
        scaled, inv = tile_norm(spread_ref[at, :].T)
        store_pairs(grad_pair_ref, t, tile_norm_grad(back_normed[:, at] * gain, scaled, inv))


def local_call(body, outs, scratch, flops, smem_first=False, inputs=1):
    specs = [pl.BlockSpec(memory_space=pltpu.VMEM)] * inputs
    if smem_first:
        specs[0] = pl.BlockSpec(memory_space=pltpu.SMEM)
    return pl.pallas_call(
        body,
        out_shape=outs,
        in_specs=specs,
        out_specs=jax.tree.map(lambda _: pl.BlockSpec(memory_space=pltpu.VMEM), outs),
        scratch_shapes=scratch,
        compiler_params=pltpu.CompilerParams(vmem_limit_bytes=VMEM_LIMIT),
        cost_estimate=pl.CostEstimate(flops=flops, bytes_accessed=2_000_000, transcendentals=0),
    )


def exchange(chunks, depth, axes):
    devices = chunks.shape[0] // depth
    split = chunks.reshape(devices, depth // 2, 2, chunks.shape[1])
    return lax.all_to_all(split, axes, 0, 0, tiled=True).reshape(chunks.shape)


def other_core(values):
    return lax.ppermute(values, "core", [(0, 1), (1, 0)])


def per_device(pair_acts, token_valid, norm_gain, proj_weight, out_gain, out_weight, out_cotangent):
    na, nb, channels = pair_acts.shape
    hidden = out_weight.shape[0]
    width_all = proj_weight.shape[1]
    full_len = token_valid.shape[0]
    lanes = na // 2 * LANES
    plane = 512
    sides_chunk = (hidden * SIDE_ROWS, LANES)
    tri_chunk = (hidden * TRI_ROWS, LANES)
    term_chunk = (4 * hidden, LANES)
    pairs = jax.ShapeDtypeStruct(pair_acts.shape, BF16)
    whole = jax.ShapeDtypeStruct((plane, plane), BF16)
    gain = norm_gain.reshape(1, channels)
    spread_scratch = pltpu.VMEM((lanes, channels), F32)
    normed_scratch = pltpu.VMEM((channels, lanes), BF16)
    half_plane = pltpu.VMEM((4, plane // 2, LANES), F32)
    full_plane = pltpu.VMEM((4, plane, LANES), F32)

    sides = local_call(
        sides_kernel,
        jax.ShapeDtypeStruct(sides_chunk, BF16),
        [spread_scratch, normed_scratch, pltpu.VMEM(sides_chunk, F32)],
        100_000_000,
        smem_first=True,
        inputs=4,
    )(token_valid, pair_acts, gain, proj_weight)
    mine = exchange(sides, SIDE_ROWS, CHANNEL_AXES)
    tri, left, right = local_call(
        functools.partial(tri_kernel, na, nb),
        (jax.ShapeDtypeStruct(tri_chunk, BF16), whole, whole),
        [pltpu.VMEM((2,) + sides_chunk, F32), full_plane, full_plane, pltpu.VMEM(tri_chunk, F32)],
        300_000_000,
        inputs=2,
    )(mine, other_core(mine))
    tri = exchange(tri, TRI_ROWS, CHANNEL_AXES)
    update, back, gate = local_call(
        middle_kernel,
        (pairs, jax.ShapeDtypeStruct(tri_chunk, BF16), jax.ShapeDtypeStruct((channels, lanes), BF16)),
        [
            spread_scratch,
            normed_scratch,
            pltpu.VMEM(tri_chunk, F32),
            pltpu.VMEM((hidden, lanes), F32),
            pltpu.VMEM((hidden, lanes), BF16),
            pltpu.VMEM((channels, lanes), BF16),
        ],
        100_000_000,
        smem_first=True,
        inputs=8,
    )(
        token_valid,
        tri,
        pair_acts,
        out_cotangent,
        gain,
        proj_weight,
        out_gain.reshape(1, hidden),
        out_weight,
    )
    back = exchange(back, TRI_ROWS, CHANNEL_AXES)
    back_sides = local_call(
        functools.partial(back_kernel, na, nb),
        jax.ShapeDtypeStruct(sides_chunk, BF16),
        [
            pltpu.VMEM((2,) + tri_chunk, F32),
            half_plane,
            full_plane,
            pltpu.VMEM(sides_chunk, F32),
            pltpu.VMEM((plane, plane), BF16),
        ],
        300_000_000,
        inputs=4,
    )(back, other_core(back), left, right)
    back_sides = exchange(back_sides, SIDE_ROWS, CHANNEL_AXES)
    term, back_proj, gate_total = local_call(
        weight_kernel,
        (
            jax.ShapeDtypeStruct(term_chunk, BF16),
            jax.ShapeDtypeStruct((width_all, lanes), BF16),
            jax.ShapeDtypeStruct((channels, channels), F32),
        ),
        [
            spread_scratch,
            normed_scratch,
            pltpu.VMEM(sides_chunk, F32),
            pltpu.VMEM(term_chunk, F32),
        ],
        200_000_000,
        smem_first=True,
        inputs=6,
    )(token_valid, back_sides, pair_acts, gain, proj_weight, gate)
    grad_pair = local_call(pair_kernel, pairs, [spread_scratch], 100_000_000, inputs=4)(
        pair_acts, gain, proj_weight, back_proj
    )
    parts = exchange(term, 2, ALL_AXES)
    sums = local_call(
        functools.partial(sum_kernel, full_len), jax.ShapeDtypeStruct(term_chunk, BF16), [], 100_000
    )(parts)
    sums = exchange(sums, 2, ALL_AXES)
    grad_weight = local_call(
        grad_weight_kernel,
        jax.ShapeDtypeStruct((channels, width_all), F32),
        [pltpu.VMEM(term_chunk, F32)],
        100_000,
        inputs=2,
    )(sums, gate_total)
    return update, grad_pair, grad_weight


def solution(mesh):
    rows, cols = mesh.devices.shape
    split = Mesh(mesh.devices.reshape(rows // 2, 2, cols), ("chip", "core", "col"))
    pairs = P(("chip", "core"), "col", None)
    return jax.shard_map(
        per_device,
        mesh=split,
        in_specs=(pairs, P(), P(), P(), P(), P(), pairs),
        out_specs=(pairs, pairs, P()),
        check_vma=False,
    )
```

time: 171 us -> 150 us (0.88)
  blocking collectives: 121 us -> 105 us
  other arithmetic: 5.47 us -> 0 us
  starting transfers between devices: 7.1 us -> 12.4 us
  local copies, waits for them, and re-layouts: 7.79 us -> 4.49 us
  waiting for transfers between devices: 17.1 us -> 13.9 us
    all_to_all x5, blocking collectives: 121 us -> 105 us  [exchange(): return lax.all_to_all(split, axes, 0, 0, tiled=True).reshape(chunks.shape)]
    ppermute x2, starting transfers between devices: 1.36 us -> 6.29 us  [other_core(): return lax.ppermute(values, 'core', [(0, 1), (1, 0)])]
    all_to_all x1, waiting for transfers between devices: 14.6 us -> 11.6 us  [exchange(): return lax.all_to_all(split, axes, 0, 0, tiled=True).reshape(chunks.shape)]
    broadcast_in_dim x1 -> x0, other arithmetic: 1.94 us -> none  [per_device(): copies = jnp.broadcast_to(total.astype(BF16), (devices,) + total.shape)]
    all_to_all x1 -> x0, other arithmetic: 1.93 us -> none  [per_device(): lax.all_to_all(weight_term.reshape(devices, -1), AXES, 0, 0, tiled=True)]
    pallas_call x5 -> x7, Pallas kernels: 10.2 us -> 11.7 us  [the longest x1 2.77 us: per_device(): local_call(functools.partial(tri_kernel, na, nb), (jax.ShapeDtypeStruct(t...]
    unnamed x24 -> x20, local copies, waits for them, and re-layouts: 6.01 us -> 4.49 us
where the time goes in v3:
time: 150 us
  blocking collectives  105 us (70%)
  waiting for transfers between devices  13.9 us (9%)
  Pallas kernels  12.8 us (9%)
  starting transfers between devices  12.4 us (8%)
  local copies, waits for them, and re-layouts  4.49 us (3%)
    all_to_all x5, blocking collectives, exchange(): return lax.all_to_all(split, axes, 0, 0, tiled=True).reshape(chunks.shape)  105 us
    all_to_all x1, waiting for transfers between devices, exchange(): return lax.all_to_all(split, axes, 0, 0, tiled=True).reshape(chunks.shape)  11.6 us
    ppermute x2, starting transfers between devices, other_core(): return lax.ppermute(values, 'core', [(0, 1), (1, 0)])  6.29 us
    all_to_all x1, starting transfers between devices, exchange(): return lax.all_to_all(split, axes, 0, 0, tiled=True).reshape(chunks.shape)  6.07 us
    unnamed x20, local copies, waits for them, and re-layouts  4.49 us
  transfers between devices with their start and end apart: 3, of which 3 were waited for; matrix products, arithmetic and copies ran while one was open for 0% of the time, Pallas kernels for 1%

profile of v3, /device:TPU:1, one launch (start us, length us, event | category | flops | bytes accessed | tf_op | source)
XLA Modules:
  0.0 149.7 jit_solution(15384596282200271141)
XLA Ops:
  0.6 0.0 copy-start.8
  0.6 0.6 copy-done.8
  1.3 0.0 copy-start
  1.3 0.9 copy-done
  2.2 0.0 copy-start.2
  2.2 0.9 copy-done.2
  3.1 0.0 copy-start.6
  3.1 0.7 copy-done.6
  3.8 1.3 shard_map.94
  5.1 29.8 %all_to_all.30 = bf16[128,5,2,128]{3,2,1,0:T(2,128)(2,1)S(1)} all-to-all(bf16[128,5,2,128]{3,2,1,0:T(2,128)(2,1)S(1)} %bitcast.20), channel_id=1, replica_groups=mesh['chip'=16,'core'=2,'col'=8] {'chip','col'}, dimensions={0} | all-to-all | bytes 655360 | tf_op jit(solution)/shard_map/all_to_all | solution.py:440
  34.9 3.1 %collective-permute-start = (bf16[1280,128]{1,0:T(8,128)(2,1)S(1)}, bf16[1280,128]{1,0:T(8,128)(2,1)S(1)}, u32[]{:S(2)}, u32[]{:S(2)}) collective-permute-start(bf16[1280,128]{1,0:T(8,128)(2,1)S(1)} %bitcast.26), channel_id=1, source_target_pairs={{0,8},{8,0},{1,9},{9,1},{2,10},{10,2},{3,11},{11,3},{4,12},{12,4},... | collective-permute-start | bytes 983048 | tf_op jit(solution)/shard_map/ppermute | solution.py:444
  38.1 1.3 collective-permute-done.theirs_ref
  39.3 0.0 copy-start.4
  39.3 2.8 %shard_map.95 = (bf16[768,128]{1,0:T(8,128)(2,1)S(1)}, bf16[512,512]{1,0:T(8,128)(2,1)S(1)}, bf16[512,512]{1,0:T(8,128)(2,1)S(1)}) custom-call(bf16[1280,128]{1,0:T(8,128)(2,1)S(1)} %bitcast.27, bf16[1280,128]{1,0:T(8,128)(2,1)S(1)} %collective-permute-done.theirs_ref), custom_call_target="tpu_custom_call" | custom-call | flops 300000000 | bytes 2000000 | tf_op jit(solution)/shard_map/pallas_call | solution.py:474
  42.1 0.0 copy-start.1
  42.1 0.0 copy-start.3
  42.1 0.0 copy-start.5
  42.1 17.6 %all_to_all.31 = bf16[128,3,2,128]{3,2,1,0:T(2,128)(2,1)S(1)} all-to-all(bf16[128,3,2,128]{3,2,1,0:T(2,128)(2,1)S(1)} %bitcast.28), channel_id=1, replica_groups=mesh['chip'=16,'core'=2,'col'=8] {'chip','col'}, dimensions={0} | all-to-all | bytes 393216 | tf_op jit(solution)/shard_map/all_to_all | solution.py:440
  59.7 0.0 copy-start.9
  59.7 0.0 copy-done.4
  59.7 0.0 copy-done.1
  59.7 0.0 copy-done.3
  59.7 0.0 copy-done.5
  59.7 0.6 copy-done.9
  60.4 2.1 %shard_map.96 = (bf16[12,48,128]{2,1,0:T(8,128)(2,1)}, bf16[768,128]{1,0:T(8,128)(2,1)S(1)}, bf16[128,768]{1,0:T(8,128)(2,1)S(1)}) custom-call(s32[384]{0:T(512)S(1)} %copy-done.6, bf16[768,128]{1,0:T(8,128)(2,1)S(1)} %bitcast.23, bf16[12,48,128]{2,1,0:T(8,128)(2,1)S(1)} %copy-done.3, bf16[12,48,128]{2,1,0:T(8,128)(2,1)S(1)} %copy-done.4, ...), custom_call_target="tpu_custom_call" | custom-call | flops 100000000 | bytes 2000000 | tf_op jit(solution)/shard_map/pallas_call | solution.py:482
  62.4 18.2 %all_to_all.32 = bf16[128,3,2,128]{3,2,1,0:T(2,128)(2,1)S(1)} all-to-all(bf16[128,3,2,128]{3,2,1,0:T(2,128)(2,1)S(1)} %bitcast.29), channel_id=1, replica_groups=mesh['chip'=16,'core'=2,'col'=8] {'chip','col'}, dimensions={0} | all-to-all | bytes 393216 | tf_op jit(solution)/shard_map/all_to_all | solution.py:440
  80.6 3.1 %collective-permute-start.1 = (bf16[768,128]{1,0:T(8,128)(2,1)S(1)}, bf16[768,128]{1,0:T(8,128)(2,1)S(1)}, u32[]{:S(2)}, u32[]{:S(2)}) collective-permute-start(bf16[768,128]{1,0:T(8,128)(2,1)S(1)} %bitcast.21), channel_id=1, source_target_pairs={{0,8},{8,0},{1,9},{9,1},{2,10},{10,2},{3,11},{11,3},{4,12},{12,4},... | collective-permute-start | bytes 589832 | tf_op jit(solution)/shard_map/ppermute | solution.py:444
  83.8 1.1 collective-permute-done.1.theirs_ref
  84.9 2.4 %shard_map.97 = bf16[1280,128]{1,0:T(8,128)(2,1)S(1)} custom-call(bf16[768,128]{1,0:T(8,128)(2,1)S(1)} %bitcast.22, bf16[768,128]{1,0:T(8,128)(2,1)S(1)} %collective-permute-done.1.theirs_ref, bf16[512,512]{1,0:T(8,128)(2,1)S(1)} %get-tuple-element.15.left_ref, bf16[512,512]{1,0:T(8,128)(2,1)S(1)} %get-tuple-element.16.right_ref), custom_call_target="tpu_custom_call" | custom-call | flops 300000000 | bytes 2000000 | tf_op jit(solution)/shard_map/pallas_call | solution.py:507
  87.2 19.8 %all_to_all.33 = bf16[128,5,2,128]{3,2,1,0:T(2,128)(2,1)S(1)} all-to-all(bf16[128,5,2,128]{3,2,1,0:T(2,128)(2,1)S(1)} %bitcast.18), channel_id=1, replica_groups=mesh['chip'=16,'core'=2,'col'=8] {'chip','col'}, dimensions={0} | all-to-all | bytes 655360 | tf_op jit(solution)/shard_map/all_to_all | solution.py:440
  107.0 0.0 copy-start.7
  107.0 0.7 copy-done.7
  107.7 1.6 %shard_map.98 = (bf16[512,128]{1,0:T(8,128)(2,1)S(1)}, bf16[640,768]{1,0:T(8,128)(2,1)S(1)}, f32[128,128]{1,0:T(8,128)S(1)}) custom-call(s32[384]{0:T(512)S(1)} %copy-done.7, bf16[1280,128]{1,0:T(8,128)(2,1)S(1)} %bitcast.19, bf16[12,48,128]{2,1,0:T(8,128)(2,1)S(1)} %copy-done.3, f32[1,128]{1,0:T(1,128)S(1)} %bitcast.33, bf16[128,640]{1,0:T(8,128)(2,1)S(1)} %copy-done.1, ...), custom_call_target="tpu_custom_call" | custom-call | flops 200000000 | bytes 2000000 | tf_op jit(solution)/shard_map/pallas_call | solution.py:521
  109.3 20.1 %all_to_all.34 = bf16[256,1,2,128]{3,2,1,0:T(2,128)(2,1)S(1)} all-to-all(bf16[256,1,2,128]{3,2,1,0:T(2,128)(2,1)S(1)} %bitcast.30), channel_id=1, replica_groups=mesh['chip'=16,'core'=2,'col'=8] {'chip','core','col'}, dimensions={0} | all-to-all | bytes 262144 | tf_op jit(solution)/shard_map/all_to_all | solution.py:440
  129.4 0.7 shard_map.100
  130.1 6.1 %all-to-all-start.5 = ((bf16[256,1,2,128]{3,2,1,0:T(2,128)(2,1)}), bf16[256,1,2,128]{3,2,1,0:T(2,128)(2,1)S(1)}, u32[]{:S(2)}, u32[]{:S(2)}) async-start(bf16[256,1,2,128]{3,2,1,0:T(2,128)(2,1)} %bitcast.14), calls=%async_computation.5 | async-start | bytes 262144 | tf_op jit(solution)/shard_map/all_to_all | solution.py:440
  136.2 1.2 shard_map.99
  137.3 11.6 %all-to-all-done.5 = bf16[256,1,2,128]{3,2,1,0:T(2,128)(2,1)S(1)} async-done(((bf16[256,1,2,128]{3,2,1,0:T(2,128)(2,1)}), bf16[256,1,2,128]{3,2,1,0:T(2,128)(2,1)S(1)}, u32[]{:S(2)}, u32[]{:S(2)}) %all-to-all-start.5) | async-done | bytes 131104 | tf_op jit(solution)/shard_map/all_to_all | solution.py:440
  148.9 0.8 shard_map.101
Async XLA Ops:
  0.6 0.7 copy-start.8
  1.3 0.9 copy-start
  2.2 0.9 copy-start.2
  3.1 0.7 copy-start.6
  34.9 4.4 %collective-permute-start = (bf16[1280,128]{1,0:T(8,128)(2,1)S(1)}, bf16[1280,128]{1,0:T(8,128)(2,1)S(1)}, u32[]{:S(2)}, u32[]{:S(2)}) collective-permute-start(bf16[1280,128]{1,0:T(8,128)(2,1)S(1)} %bitcast.26), channel_id=1, source_target_pairs={{0,8},{8,0},{1,9},{9,1},{2,10},{10,2},{3,11},{11,3},{4,12},{12,4},... | collective-permute-start | bytes 983048 | tf_op jit(solution)/shard_map/ppermute | solution.py:444
  39.3 20.4 %copy-start.4 = (bf16[12,48,128]{2,1,0:T(8,128)(2,1)S(1)}, bf16[12,48,128]{2,1,0:T(8,128)(2,1)}, u32[]{:S(2)}) copy-start(bf16[12,48,128]{2,1,0:T(8,128)(2,1)} %cotangent_ref.1) | copy-start | bytes 442372
  42.1 17.6 %copy-start.1 = (bf16[128,640]{1,0:T(8,128)(2,1)S(1)}, bf16[128,640]{1,0:T(8,128)(2,1)}, u32[]{:S(2)}) copy-start(bf16[128,640]{1,0:T(8,128)(2,1)} %weight_ref.7) | copy-start | bytes 491524
  42.1 17.6 %copy-start.3 = (bf16[12,48,128]{2,1,0:T(8,128)(2,1)S(1)}, bf16[12,48,128]{2,1,0:T(8,128)(2,1)}, u32[]{:S(2)}) copy-start(bf16[12,48,128]{2,1,0:T(8,128)(2,1)} %acts_ref.7) | copy-start | bytes 442372
  42.1 17.6 %copy-start.5 = (bf16[128,128]{1,0:T(8,128)(2,1)S(1)}, bf16[128,128]{1,0:T(8,128)(2,1)}, u32[]{:S(2)}) copy-start(bf16[128,128]{1,0:T(8,128)(2,1)} %out_weight_ref.1) | copy-start | bytes 98308
  59.7 0.7 copy-start.9
  80.6 4.2 %collective-permute-start.1 = (bf16[768,128]{1,0:T(8,128)(2,1)S(1)}, bf16[768,128]{1,0:T(8,128)(2,1)S(1)}, u32[]{:S(2)}, u32[]{:S(2)}) collective-permute-start(bf16[768,128]{1,0:T(8,128)(2,1)S(1)} %bitcast.21), channel_id=1, source_target_pairs={{0,8},{8,0},{1,9},{9,1},{2,10},{10,2},{3,11},{11,3},{4,12},{12,4},... | collective-permute-start | bytes 589832 | tf_op jit(solution)/shard_map/ppermute | solution.py:444
  107.0 0.7 copy-start.7
  130.1 18.8 %all-to-all-start.5 = ((bf16[256,1,2,128]{3,2,1,0:T(2,128)(2,1)}), bf16[256,1,2,128]{3,2,1,0:T(2,128)(2,1)S(1)}, u32[]{:S(2)}, u32[]{:S(2)}) async-start(bf16[256,1,2,128]{3,2,1,0:T(2,128)(2,1)} %bitcast.14), calls=%async_computation.5 | async-start | bytes 262144 | tf_op jit(solution)/shard_map/all_to_all | solution.py:440

commit v4 on v3

v4 whole, which is shorter than its diff:
```python
import functools

import jax
import jax.numpy as jnp
from jax import lax
from jax.experimental import pallas as pl
from jax.experimental.pallas import tpu as pltpu
from jax.sharding import Mesh
from jax.sharding import PartitionSpec as P

EPSILON = 1e-05
BF16 = jnp.bfloat16
F32 = jnp.float32
ALL_AXES = ("chip", "core", "col")
CHANNEL_AXES = ("col", "chip")
LANES = 128
SLOT = 64
PIECE = 16
SIDE_ROWS = 10
TRI_ROWS = 6
VMEM_LIMIT = 48 * 1024 * 1024

NT = (((1,), (1,)), ((), ()))
NN = (((1,), (0,)), ((), ()))
TN = (((0,), (0,)), ((), ()))


def matmul(lhs, rhs, dims=NN):
    return lax.dot_general(lhs, rhs, dims, preferred_element_type=F32)


def column(row_ref):
    return jnp.broadcast_to(row_ref[...], (LANES, LANES)).T


def swap_halves(values):
    return pltpu.roll(values, SLOT, 1)


def low_half(shape):
    return lax.broadcasted_iota(jnp.int32, shape, 1) < SLOT


def spread(pairs_ref, spread_ref):
    na, nb, channels = pairs_ref.shape
    for a in range(na):
        spread_ref[a * SLOT : a * SLOT + nb, :] = pairs_ref[a].astype(F32)
        spread_ref[a * SLOT + nb : (a + 1) * SLOT, :] = jnp.zeros((SLOT - nb, channels), F32)


def store_pairs(out_ref, t, values):
    nb = out_ref.shape[1]
    turned = values.T
    out_ref[2 * t] = turned[0:nb].astype(out_ref.dtype)
    out_ref[2 * t + 1] = turned[SLOT : SLOT + nb].astype(out_ref.dtype)


def masks(valid_ref, na, nb):
    lane = lax.broadcasted_iota(jnp.int32, (1, LANES), 1)
    place = lane % SLOT
    first_row = (2 * lax.axis_index("chip") + lax.axis_index("core")) * na
    first_col = lax.axis_index("col") * nb
    cols = jnp.zeros((1, LANES), jnp.int32)
    for b in range(nb):
        cols = jnp.where(place == b, valid_ref[first_col + b], cols)
    found = []
    for t in range(na // 2):
        rows = jnp.where(lane < SLOT, valid_ref[first_row + 2 * t], valid_ref[first_row + 2 * t + 1])
        found.append((rows * cols).astype(F32))
    return found


def tile_norm(values):
    center = jnp.mean(values, axis=0, keepdims=True)
    shifted = values - center
    inv_std = lax.rsqrt(jnp.mean(shifted * shifted, axis=0, keepdims=True) + EPSILON)
    return shifted * inv_std, inv_std


def tile_norm_grad(upstream, scaled, inv_std):
    first = jnp.mean(upstream, axis=0, keepdims=True)
    second = jnp.mean(upstream * scaled, axis=0, keepdims=True)
    return inv_std * (upstream - first - scaled * second)


def norm_tiles(spread_ref, gain_ref, normed_ref):
    gain = column(gain_ref)
    tiles = spread_ref.shape[0] // LANES
    for t in range(tiles):
        at = slice(t * LANES, (t + 1) * LANES)
        scaled, _ = tile_norm(spread_ref[at, :].T)
        normed_ref[:, at] = (scaled * gain).astype(BF16)


def gap(shape):
    return lax.broadcasted_iota(jnp.int32, shape, 1) % SLOT >= SLOT - PIECE


def pack_tiles(tiles):
    free = gap(tiles[0].shape)
    rows = []
    for t in range(9):
        moved = pltpu.roll(tiles[9 + t // 3], SLOT - PIECE - PIECE * (t % 3), 1)
        rows.append(jnp.where(free, moved, tiles[t]))
    return rows


def unpack_tiles(rows):
    free = gap(rows[0].shape)
    place = lax.broadcasted_iota(jnp.int32, rows[0].shape, 1) % SLOT // PIECE
    tiles = [jnp.where(free, 0.0, row) for row in rows]
    for m in range(3):
        tile = jnp.zeros_like(rows[0])
        for p in range(3):
            moved = pltpu.roll(rows[3 * m + p], LANES - (SLOT - PIECE) + PIECE * p, 1)
            tile = jnp.where(place == p, moved, tile)
        tiles.append(tile)
    return tiles


def device_rows(chunk_ref, depth, row):
    return chunk_ref[pl.ds(row, chunk_ref.shape[0] // depth, stride=depth), :]


def put_device_rows(chunk_ref, depth, row, values):
    chunk_ref[pl.ds(row, chunk_ref.shape[0] // depth, stride=depth), :] = values


def group_rows(depth, lo, col, row):
    return pl.ds(depth * (16 * col + lo) + row, 8, stride=2 * depth)


def plane_rows(na, lo, t):
    return slice(8 * (na * lo + 2 * t), 8 * (na * lo + 2 * t) + 16)


def plane_tile(even, odd):
    low = low_half(even.shape)
    upper = jnp.where(low, even, swap_halves(odd))
    lower = jnp.where(low, swap_halves(even), odd)
    return jnp.concatenate([upper, lower], axis=0)


def chunk_tiles(rows):
    upper, lower = rows[0:8], rows[8:16]
    low = low_half(upper.shape)
    return jnp.where(low, upper, swap_halves(lower)), jnp.where(low, swap_halves(upper), lower)


def token_order(na, plane):
    row = lax.broadcasted_iota(jnp.int32, (16 * 2 * na, plane), 0)
    token = lax.broadcasted_iota(jnp.int32, (16 * 2 * na, plane), 1)
    place = row // 8
    core = (place >= 2 * na).astype(jnp.int32)
    place = place - 2 * na * core
    lo = (place >= na).astype(jnp.int32)
    a = place - na * lo
    return (token == SLOT * (row % 8) + na * (2 * lo + core) + a).astype(F32).astype(BF16)


def sides_kernel(
    valid_hbm, acts_hbm, gain_hbm, weight_hbm, out_ref, mask_ref,
    valid_ref, acts_ref, gain_ref, weight_ref, spread_ref, normed_ref, chunk_ref, sems,
):
    na, nb, _ = acts_hbm.shape
    tiles = na // 2
    hidden = weight_hbm.shape[0]
    copies = [
        pltpu.make_async_copy(valid_hbm, valid_ref, sems.at[0]),
        pltpu.make_async_copy(acts_hbm, acts_ref, sems.at[1]),
        pltpu.make_async_copy(gain_hbm, gain_ref, sems.at[2]),
        pltpu.make_async_copy(weight_hbm, weight_ref, sems.at[3]),
    ]
    for copy in copies:
        copy.start()
    copies[0].wait()
    mask = masks(valid_ref, na, nb)
    for t in range(tiles):
        mask_ref[:, t * LANES : (t + 1) * LANES] = mask[t]
    copies[1].wait()
    spread(acts_ref, spread_ref)
    copies[2].wait()
    norm_tiles(spread_ref, gain_ref, normed_ref)
    copies[3].wait()
    projected = matmul(weight_ref[:, 0 : 4 * hidden], normed_ref[...], TN)
    found = []
    for side in range(2):
        base = 2 * side * hidden
        for t in range(tiles):
            at = slice(t * LANES, (t + 1) * LANES)
            gate = jax.nn.sigmoid(projected[base : base + hidden, at])
            value = projected[base + hidden : base + 2 * hidden, at]
            found.append(gate * value * mask[t])
    for t, row in enumerate(pack_tiles(found)):
        put_device_rows(chunk_ref, SIDE_ROWS, t, row)
    put_device_rows(chunk_ref, SIDE_ROWS, 9, jnp.zeros((hidden, LANES), F32))
    out_ref[...] = chunk_ref[...].astype(BF16)


def ready_kernel(
    mask_ref, acts_ref, cotangent_ref, gain_ref, weight_ref, out_gain_ref, out_weight_ref,
    normed_ref, back_norm_ref, gate_mask_ref, gate_coef_ref, coef_ref, order_ref,
    spread_ref, back_out_ref,
):
    na = acts_ref.shape[0]
    tiles = na // 2
    hidden = out_weight_ref.shape[0]
    spread(acts_ref, spread_ref)
    norm_tiles(spread_ref, gain_ref, normed_ref)
    spread(cotangent_ref, spread_ref)
    projected = matmul(weight_ref[...], normed_ref[...], TN)
    for t in range(tiles):
        at = slice(t * LANES, (t + 1) * LANES)
        mask = mask_ref[:, at]
        gate = jax.nn.sigmoid(projected[4 * hidden :, at])
        gate_mask = gate * mask
        cotangent = spread_ref[at, :].T
        gate_mask_ref[:, at] = gate_mask
        gate_coef_ref[:, at] = cotangent * gate_mask * (1.0 - gate)
        back_out_ref[:, at] = (cotangent * gate_mask).astype(BF16)
        for base in (0, 2 * hidden):
            gate = jax.nn.sigmoid(projected[base : base + hidden, at])
            value = projected[base + hidden : base + 2 * hidden, at]
            coef_ref[base : base + hidden, at] = value * gate * (1.0 - gate) * mask
            coef_ref[base + hidden : base + 2 * hidden, at] = gate * mask
    out_gain = column(out_gain_ref)
    back_norm = matmul(out_weight_ref[...], back_out_ref[...])
    for t in range(tiles):
        at = slice(t * LANES, (t + 1) * LANES)
        back_norm_ref[:, at] = back_norm[:, at] * out_gain
    order_ref[...] = token_order(na, order_ref.shape[1])


def my_rows(ref):
    half = ref.shape[-2] // 2
    return pl.ds(pl.multiple_of(lax.axis_index("core") * half, half), half)


def tri_kernel(
    na, mine_ref, theirs_ref, order_ref, tri_ref, left_ref, right_ref, chunk_ref, tri_chunk_ref
):
    tiles = na // 2
    core = lax.axis_index("core")
    chunk_ref[core] = mine_ref[...].astype(F32)
    chunk_ref[1 - core] = theirs_ref[...].astype(F32)
    half = left_ref.shape[0] // 2
    for side in range(2):
        for pair in range(4):
            at = slice(pair * LANES, (pair + 1) * LANES)
            for lo in range(2):
                even, odd = [
                    unpack_tiles(
                        [chunk_ref[side, group_rows(SIDE_ROWS, lo, col, t), :] for t in range(9)]
                    )
                    for col in (2 * pair, 2 * pair + 1)
                ]
                for t in range(tiles):
                    rows = plane_rows(na, lo, t)
                    rows = slice(side * half + rows.start, side * half + rows.stop)
                    left_ref[rows, at] = plane_tile(even[t], odd[t]).astype(BF16)
                    right_ref[rows, at] = plane_tile(even[tiles + t], odd[tiles + t]).astype(BF16)
    tri = matmul(left_ref[my_rows(left_ref), :], right_ref[...], NT).astype(BF16)
    tri = matmul(tri, order_ref[...])
    for pair in range(4):
        for lo in range(2):
            for t in range(tiles):
                both = chunk_tiles(tri[plane_rows(na, lo, t), pair * LANES : (pair + 1) * LANES])
                for side in range(2):
                    tri_chunk_ref[group_rows(TRI_ROWS, lo, 2 * pair + side, t), :] = both[side]
    tri_ref[...] = tri_chunk_ref[...].astype(BF16)


def middle_kernel(
    tri_ref, normed_ref, back_norm_ref, gate_coef_ref, out_gain_ref, out_weight_ref,
    back_ref, gate_ref, out_proj_ref,
    tri_chunk_ref, scaled_ref, normed_out_ref,
):
    tiles = normed_ref.shape[1] // LANES
    tri_chunk_ref[...] = tri_ref[...].astype(F32)
    out_gain = column(out_gain_ref)
    inv_out = []
    for t in range(tiles):
        at = slice(t * LANES, (t + 1) * LANES)
        scaled, inv = tile_norm(device_rows(tri_chunk_ref, TRI_ROWS, t))
        inv_out.append(inv)
        scaled_ref[:, at] = scaled
        normed_out_ref[:, at] = (scaled * out_gain).astype(BF16)
    out_proj = matmul(out_weight_ref[...], normed_out_ref[...], TN)
    out_proj_ref[...] = out_proj
    gate_ref[...] = (out_proj * gate_coef_ref[...]).astype(BF16)
    term = matmul(normed_ref[...], gate_ref[...], NT)
    free = gap(term.shape)
    for t in range(tiles):
        at = slice(t * LANES, (t + 1) * LANES)
        row = tile_norm_grad(back_norm_ref[:, at], scaled_ref[:, at], inv_out[t])
        if t < 4:
            moved = pltpu.roll(term, SLOT - PIECE - PIECE * t, 1) if t < 3 else term
            row = jnp.where(free, moved, row)
        put_device_rows(tri_chunk_ref, TRI_ROWS, t, row)
    back_ref[...] = tri_chunk_ref[...].astype(BF16)


def update_kernel(gate_mask_ref, out_proj_ref, update_ref):
    for t in range(update_ref.shape[0] // 2):
        at = slice(t * LANES, (t + 1) * LANES)
        store_pairs(update_ref, t, gate_mask_ref[:, at] * out_proj_ref[:, at])


def back_kernel(
    na, mine_ref, theirs_ref, left_ref, right_ref, order_ref, out_ref,
    back_chunk_ref, chunk_ref, back_ref, turned_ref, side_ref,
):
    tiles = na // 2
    core = lax.axis_index("core")
    back_chunk_ref[core] = mine_ref[...].astype(F32)
    back_chunk_ref[1 - core] = theirs_ref[...].astype(F32)
    half = back_ref.shape[0] // 2
    free = gap((8, LANES))
    for side in range(2):
        for pair in range(4):
            for lo in range(2):
                for t in range(tiles):
                    even, odd = [
                        jnp.where(free, 0.0, back_chunk_ref[side, group_rows(TRI_ROWS, lo, col, t), :])
                        for col in (2 * pair, 2 * pair + 1)
                    ]
                    rows = plane_rows(na, lo, t)
                    rows = slice(side * half + rows.start, side * half + rows.stop)
                    back_ref[rows, pair * LANES : (pair + 1) * LANES] = plane_tile(even, odd).astype(BF16)
    turned_ref[...] = matmul(back_ref[...], order_ref[...], NT).astype(BF16)
    back_left = matmul(turned_ref[my_rows(turned_ref), :], right_ref[...])
    side_ref[...] = matmul(turned_ref[...], left_ref[...], TN)
    back_right = side_ref[my_rows(side_ref), :]

    place = lax.broadcasted_iota(jnp.int32, (8, LANES), 1) % SLOT // PIECE
    total = jnp.zeros((8, LANES), F32)
    for t in range(4):
        rows = jnp.zeros((8, LANES), F32)
        for side in range(2):
            for m in range(back_chunk_ref.shape[1] // (8 * TRI_ROWS)):
                rows += back_chunk_ref[side, pl.ds(8 * TRI_ROWS * m + t, 8, stride=TRI_ROWS), :]
        rows = jnp.sum(rows, axis=0, keepdims=True)
        rows = jnp.broadcast_to(rows, (8, LANES))
        if t < 3:
            rows = pltpu.roll(rows, LANES - (SLOT - PIECE) + PIECE * t, 1)
        total = jnp.where(place == t, rows, total)
    total = total / (4 * 8 * na)
    for m in range(chunk_ref.shape[0] // (8 * SIDE_ROWS)):
        chunk_ref[pl.ds(8 * SIDE_ROWS * m + 9, 8, stride=SIDE_ROWS), :] = total

    for pair in range(4):
        at = slice(pair * LANES, (pair + 1) * LANES)
        for lo in range(2):
            found = [
                chunk_tiles(product[plane_rows(na, lo, t), at])
                for product in (back_left, back_right)
                for t in range(tiles)
            ]
            for side in range(2):
                for t, row in enumerate(pack_tiles([both[side] for both in found])):
                    chunk_ref[group_rows(SIDE_ROWS, lo, 2 * pair + side, t), :] = row
    out_ref[...] = chunk_ref[...].astype(BF16)


def weight_kernel(
    back_ref, normed_ref, coef_ref, gate_ref, term_ref, back_proj_ref, gate_total_ref,
    chunk_ref, term_chunk_ref,
):
    tiles = normed_ref.shape[1] // LANES
    hidden = normed_ref.shape[0]
    chunk_ref[...] = back_ref[...].astype(F32)
    gate_total_ref[...] = device_rows(chunk_ref, SIDE_ROWS, 9)
    back_proj_ref[4 * hidden :, :] = gate_ref[...]
    upstreams = unpack_tiles([device_rows(chunk_ref, SIDE_ROWS, t) for t in range(9)])
    for side in range(2):
        for t in range(tiles):
            at = slice(t * LANES, (t + 1) * LANES)
            for base in (2 * side * hidden, (2 * side + 1) * hidden):
                rows = slice(base, base + hidden)
                back_proj_ref[rows, at] = (upstreams[tiles * side + t] * coef_ref[rows, at]).astype(BF16)
    term = matmul(normed_ref[...], back_proj_ref[0 : 4 * hidden, :], NT)
    for t in range(4):
        for m in range(hidden // 8):
            term_chunk_ref[weight_rows(m, t), :] = term[8 * m : 8 * m + 8, t * LANES : (t + 1) * LANES]
    term_ref[...] = term_chunk_ref[...].astype(BF16)


def weight_rows(chip, t):
    return pl.ds(2 * (16 * chip + 8 * (t // 2)) + t % 2, 8, stride=2)


def sum_kernel(full_len, parts_ref, out_ref):
    total = jnp.zeros((16, LANES), F32)
    for m in range(parts_ref.shape[0] // 16):
        total += parts_ref[16 * m : 16 * m + 16, :].astype(F32)
    total = total[0:8] + total[8:16]
    total = total + pltpu.roll(total, 4, 0)
    total = total + pltpu.roll(total, 2, 0)
    total = total / full_len
    total = jnp.concatenate([total, total], axis=0).astype(BF16)
    for m in range(parts_ref.shape[0] // 16):
        out_ref[16 * m : 16 * m + 16, :] = total


def grad_weight_kernel(sums_ref, gate_total_ref, out_ref, chunk_ref):
    chunk_ref[...] = sums_ref[...].astype(F32)
    for t in range(4):
        for m in range(out_ref.shape[0] // 8):
            out_ref[8 * m : 8 * m + 8, t * LANES : (t + 1) * LANES] = chunk_ref[weight_rows(m, t), :]
    out_ref[:, 4 * LANES :] = gate_total_ref[...]


def pair_kernel(acts_ref, gain_ref, weight_ref, back_proj_ref, grad_pair_ref, spread_ref):
    na, nb, _ = acts_ref.shape
    spread(acts_ref, spread_ref)
    gain = column(gain_ref)
    back_normed = matmul(weight_ref[...], back_proj_ref[...])
    for t in range(na // 2):
        at = slice(t * LANES, (t + 1) * LANES)
        scaled, inv = tile_norm(spread_ref[at, :].T)
        store_pairs(grad_pair_ref, t, tile_norm_grad(back_normed[:, at] * gain, scaled, inv))


def local_call(body, outs, scratch, flops, inputs, space=pltpu.VMEM, limit=VMEM_LIMIT):
    return pl.pallas_call(
        body,
        out_shape=outs,
        in_specs=[pl.BlockSpec(memory_space=space)] * inputs,
        out_specs=jax.tree.map(lambda _: pl.BlockSpec(memory_space=pltpu.VMEM), outs),
        scratch_shapes=scratch,
        compiler_params=pltpu.CompilerParams(vmem_limit_bytes=limit),
        cost_estimate=pl.CostEstimate(flops=flops, bytes_accessed=2_000_000, transcendentals=0),
    )


def exchange(chunks, depth, axes):
    devices = chunks.shape[0] // depth
    split = chunks.reshape(devices, depth // 2, 2, chunks.shape[1])
    return lax.all_to_all(split, axes, 0, 0, tiled=True).reshape(chunks.shape)


def other_core(values):
    return lax.ppermute(values, "core", [(0, 1), (1, 0)])


def array(shape, dtype=BF16):
    return jax.ShapeDtypeStruct(shape, dtype)


def per_device(pair_acts, token_valid, norm_gain, proj_weight, out_gain, out_weight, out_cotangent):
    na, _, channels = pair_acts.shape
    hidden = out_weight.shape[0]
    width_all = proj_weight.shape[1]
    full_len = token_valid.shape[0]
    lanes = na // 2 * LANES
    plane = (full_len, 8 * SLOT)
    sides_chunk = (hidden * SIDE_ROWS, LANES)
    tri_chunk = (hidden * TRI_ROWS, LANES)
    term_chunk = (4 * hidden, LANES)
    gain = norm_gain.reshape(1, channels)
    out_gain = out_gain.reshape(1, hidden)
    spread_scratch = pltpu.VMEM((lanes, channels), F32)

    sides, mask = local_call(
        sides_kernel,
        (array(sides_chunk), array((1, lanes), F32)),
        [
            pltpu.SMEM(token_valid.shape, jnp.int32),
            pltpu.VMEM(pair_acts.shape, BF16),
            pltpu.VMEM(gain.shape, F32),
            pltpu.VMEM(proj_weight.shape, BF16),
            spread_scratch,
            pltpu.VMEM((channels, lanes), BF16),
            pltpu.VMEM(sides_chunk, F32),
            pltpu.SemaphoreType.DMA((4,)),
        ],
        100_000_000,
        4,
        pltpu.HBM,
        64 * 1024 * 1024 - 65536,
    )(token_valid, pair_acts, gain, proj_weight)
    mine = exchange(sides, SIDE_ROWS, CHANNEL_AXES)
    normed, back_norm, gate_mask, gate_coef, coef, order = local_call(
        ready_kernel,
        (
            array((channels, lanes)),
            array((hidden, lanes), F32),
            array((channels, lanes), F32),
            array((channels, lanes), F32),
            array((4 * hidden, lanes), F32),
            array(plane),
        ),
        [spread_scratch, pltpu.VMEM((channels, lanes), BF16)],
        1_000_000_000,
        7,
    )(mask, pair_acts, out_cotangent, gain, proj_weight, out_gain, out_weight)
    mine, normed, order = lax.optimization_barrier((mine, normed, order))
    tri, left, right = local_call(
        functools.partial(tri_kernel, na),
        (array(tri_chunk), array(plane), array(plane)),
        [pltpu.VMEM((2,) + sides_chunk, F32), pltpu.VMEM(tri_chunk, F32)],
        300_000_000,
        3,
    )(mine, other_core(mine), order)
    tri = exchange(tri, TRI_ROWS, CHANNEL_AXES)
    back, gate, out_proj = local_call(
        middle_kernel,
        (array(tri_chunk), array((channels, lanes)), array((channels, lanes), F32)),
        [
            pltpu.VMEM(tri_chunk, F32),
            pltpu.VMEM((hidden, lanes), F32),
            pltpu.VMEM((hidden, lanes), BF16),
        ],
        100_000_000,
        6,
    )(tri, normed, back_norm, gate_coef, out_gain, out_weight)
    back = exchange(back, TRI_ROWS, CHANNEL_AXES)
    update = local_call(update_kernel, array(pair_acts.shape), [], 1_000_000_000, 2)(
        gate_mask, out_proj
    )
    back_sides = local_call(
        functools.partial(back_kernel, na),
        array(sides_chunk),
        [
            pltpu.VMEM((2,) + tri_chunk, F32),
            pltpu.VMEM(sides_chunk, F32),
            pltpu.VMEM(plane, BF16),
            pltpu.VMEM((full_len, full_len), BF16),
            pltpu.VMEM(plane, F32),
        ],
        300_000_000,
        5,
    )(back, other_core(back), left, right, order)
    back_sides = exchange(back_sides, SIDE_ROWS, CHANNEL_AXES)
    term, back_proj, gate_total = local_call(
        weight_kernel,
        (array(term_chunk), array((width_all, lanes)), array((channels, channels), F32)),
        [pltpu.VMEM(sides_chunk, F32), pltpu.VMEM(term_chunk, F32)],
        200_000_000,
        4,
    )(back_sides, normed, coef, gate)
    grad_pair = local_call(
        pair_kernel, array(pair_acts.shape), [spread_scratch], 1_000_000_000, 4
    )(pair_acts, gain, proj_weight, back_proj)
    parts = exchange(term, 2, ALL_AXES)
    sums = local_call(functools.partial(sum_kernel, full_len), array(term_chunk), [], 100_000, 1)(parts)
    sums = exchange(sums, 2, ALL_AXES)
    grad_weight = local_call(
        grad_weight_kernel,
        array((channels, width_all), F32),
        [pltpu.VMEM(term_chunk, F32)],
        100_000,
        2,
    )(sums, gate_total)
    return update, grad_pair, grad_weight


def solution(mesh):
    rows, cols = mesh.devices.shape
    split = Mesh(mesh.devices.reshape(rows // 2, 2, cols), ("chip", "core", "col"))
    pairs = P(("chip", "core"), "col", None)
    return jax.shard_map(
        per_device,
        mesh=split,
        in_specs=(pairs, P(), P(), P(), P(), P(), pairs),
        out_specs=(pairs, pairs, P()),
        check_vma=False,
    )
```

time: 150 us -> 141 us (0.940)
  blocking collectives: 105 us -> 75.4 us
  starting transfers between devices: 12.4 us -> 28.1 us
  waiting for transfers between devices: 13.9 us -> 18.1 us
  local copies, waits for them, and re-layouts: 4.49 us -> 7.4 us
  Pallas kernels: 12.8 us -> 10.8 us
    all_to_all x5 -> x4, blocking collectives: 105 us -> 75.4 us  [exchange(): return lax.all_to_all(split, axes, 0, 0, tiled=True).reshape(chunks.shape)]
    all_to_all x1 -> x2, starting transfers between devices: 6.07 us -> 22.4 us  [exchange(): return lax.all_to_all(split, axes, 0, 0, tiled=True).reshape(chunks.shape)]
    all_to_all x1 -> x2, waiting for transfers between devices: 11.6 us -> 15.8 us  [exchange(): return lax.all_to_all(split, axes, 0, 0, tiled=True).reshape(chunks.shape)]
    unnamed x20 -> x32, local copies, waits for them, and re-layouts: 4.49 us -> 7.4 us
    pallas_call x8 -> x10, Pallas kernels: 12.8 us -> 10.8 us  [the longest x1 2.55 us: per_device(): local_call(sides_kernel, (array(sides_chunk), array((1, lanes), F32)), [p...]
  transfers between devices with their start and end apart: 3 -> 4, of which waited for: 3 -> 4; matrix products, arithmetic and copies ran while one was open for 0% -> 0% of each run, Pallas kernels for 1% -> 2%
where the time goes in v4:
time: 141 us
  blocking collectives  75.4 us (53%)
  starting transfers between devices  28.1 us (20%)
  waiting for transfers between devices  18.1 us (13%)
  Pallas kernels  10.8 us (8%)
  local copies, waits for them, and re-layouts  7.4 us (5%)
    all_to_all x4, blocking collectives, exchange(): return lax.all_to_all(split, axes, 0, 0, tiled=True).reshape(chunks.shape)  75.4 us
    all_to_all x2, starting transfers between devices, exchange(): return lax.all_to_all(split, axes, 0, 0, tiled=True).reshape(chunks.shape)  22.4 us
    all_to_all x2, waiting for transfers between devices, exchange(): return lax.all_to_all(split, axes, 0, 0, tiled=True).reshape(chunks.shape)  15.8 us
    unnamed x32, local copies, waits for them, and re-layouts  7.4 us
    ppermute x2, starting transfers between devices, other_core(): return lax.ppermute(values, 'core', [(0, 1), (1, 0)])  5.73 us
  transfers between devices with their start and end apart: 4, of which 4 were waited for; matrix products, arithmetic and copies ran while one was open for 0% of the time, Pallas kernels for 2%

profile of v4, /device:TPU:1, one launch (start us, length us, event | category | flops | bytes accessed | tf_op | source)
XLA Modules:
  0.0 140.7 jit_solution(8577085476858760850)
XLA Ops:
  0.6 2.6 %shard_map.94 = (bf16[1280,128]{1,0:T(8,128)(2,1)}, f32[1,768]{1,0:T(1,128)}) custom-call(s32[384]{0:T(512)} %valid_hbm.1, bf16[12,48,128]{2,1,0:T(8,128)(2,1)} %acts_ref.3, f32[1,128]{1,0:T(1,128)} %bitcast.32, bf16[128,640]{1,0:T(8,128)(2,1)} %weight_ref.3), custom_call_target="tpu_custom_call" | custom-call | flops 100000000 | bytes 2000000 | tf_op jit(solution)/shard_map/pallas_call | solution.py:464
  3.2 16.3 %all-to-all-start = ((bf16[128,5,2,128]{3,2,1,0:T(2,128)(2,1)}), bf16[128,5,2,128]{3,2,1,0:T(2,128)(2,1)S(1)}, u32[]{:S(2)}, u32[]{:S(2)}) async-start(bf16[128,5,2,128]{3,2,1,0:T(2,128)(2,1)} %bitcast.35), calls=%async_computation | async-start | bytes 655360 | tf_op jit(solution)/shard_map/all_to_all | solution.py:439
  19.5 0.0 copy-start
  19.6 0.7 copy-done
  20.3 0.0 copy-start.2
  20.3 0.7 copy-done.2
  21.0 0.0 copy-start.6
  21.0 0.9 copy-done.6
  21.9 0.0 copy-start.8
  21.9 0.9 copy-done.8
  22.8 0.0 copy-start.9
  22.8 0.9 copy-done.9
  23.7 0.0 copy-start.11
  23.7 0.7 copy-done.11
  24.4 0.0 copy-start.13
  24.4 0.7 copy-done.13
  25.0 0.0 copy-start.1
  25.0 0.0 copy-start.3
  25.0 1.1 shard_map.95
  26.1 0.0 copy-start.14
  26.2 0.7 copy-done.14
  26.9 6.2 %all-to-all-done = bf16[128,5,2,128]{3,2,1,0:T(2,128)(2,1)S(1)} async-done(((bf16[128,5,2,128]{3,2,1,0:T(2,128)(2,1)}), bf16[128,5,2,128]{3,2,1,0:T(2,128)(2,1)S(1)}, u32[]{:S(2)}, u32[]{:S(2)}) %all-to-all-start) | async-done | bytes 327712 | tf_op jit(solution)/shard_map/all_to_all | solution.py:439
  33.1 2.6 %collective-permute-start = (bf16[1280,128]{1,0:T(8,128)(2,1)S(1)}, bf16[1280,128]{1,0:T(8,128)(2,1)S(1)}, u32[]{:S(2)}, u32[]{:S(2)}) collective-permute-start(bf16[1280,128]{1,0:T(8,128)(2,1)S(1)} %bitcast.25), channel_id=1, source_target_pairs={{0,8},{8,0},{1,9},{9,1},{2,10},{10,2},{3,11},{11,3},{4,12},{12,4},... | collective-permute-start | bytes 983048 | tf_op jit(solution)/shard_map/ppermute | solution.py:443
  35.7 1.3 collective-permute-done.theirs_ref
  37.0 1.3 shard_map.96
  38.3 17.9 %all_to_all.30 = bf16[128,3,2,128]{3,2,1,0:T(2,128)(2,1)S(1)} all-to-all(bf16[128,3,2,128]{3,2,1,0:T(2,128)(2,1)S(1)} %bitcast.28), channel_id=1, replica_groups=mesh['chip'=16,'core'=2,'col'=8] {'col','chip'}, dimensions={0} | all-to-all | bytes 393216 | tf_op jit(solution)/shard_map/all_to_all | solution.py:439
  56.1 0.0 copy-done.1
  56.1 0.0 copy-done.3
  56.1 0.7 shard_map.97
  56.8 0.0 copy-start.4
  56.8 17.8 %all_to_all.31 = bf16[128,3,2,128]{3,2,1,0:T(2,128)(2,1)S(1)} all-to-all(bf16[128,3,2,128]{3,2,1,0:T(2,128)(2,1)S(1)} %bitcast.27), channel_id=1, replica_groups=mesh['chip'=16,'core'=2,'col'=8] {'col','chip'}, dimensions={0} | all-to-all | bytes 393216 | tf_op jit(solution)/shard_map/all_to_all | solution.py:439
  74.6 3.1 %collective-permute-start.1 = (bf16[768,128]{1,0:T(8,128)(2,1)S(1)}, bf16[768,128]{1,0:T(8,128)(2,1)S(1)}, u32[]{:S(2)}, u32[]{:S(2)}) collective-permute-start(bf16[768,128]{1,0:T(8,128)(2,1)S(1)} %bitcast.20), channel_id=1, source_target_pairs={{0,8},{8,0},{1,9},{9,1},{2,10},{10,2},{3,11},{11,3},{4,12},{12,4},... | collective-permute-start | bytes 589832 | tf_op jit(solution)/shard_map/ppermute | solution.py:443
  77.7 1.1 collective-permute-done.1.theirs_ref
  78.8 1.3 shard_map.99
  80.0 19.8 %all_to_all.32 = bf16[128,5,2,128]{3,2,1,0:T(2,128)(2,1)S(1)} all-to-all(bf16[128,5,2,128]{3,2,1,0:T(2,128)(2,1)S(1)} %bitcast.19), channel_id=1, replica_groups=mesh['chip'=16,'core'=2,'col'=8] {'col','chip'}, dimensions={0} | all-to-all | bytes 655360 | tf_op jit(solution)/shard_map/all_to_all | solution.py:439
  99.8 0.0 copy-start.15
  99.8 0.5 shard_map.100
  100.4 0.0 copy-done.4
  100.4 20.0 %all_to_all.33 = bf16[256,1,2,128]{3,2,1,0:T(2,128)(2,1)S(1)} all-to-all(bf16[256,1,2,128]{3,2,1,0:T(2,128)(2,1)S(1)} %bitcast.29), channel_id=1, replica_groups=mesh['chip'=16,'core'=2,'col'=8] {'chip','core','col'}, dimensions={0} | all-to-all | bytes 262144 | tf_op jit(solution)/shard_map/all_to_all | solution.py:439
  120.4 0.7 shard_map.102
  121.1 6.1 %all-to-all-start.5 = ((bf16[256,1,2,128]{3,2,1,0:T(2,128)(2,1)}), bf16[256,1,2,128]{3,2,1,0:T(2,128)(2,1)S(1)}, u32[]{:S(2)}, u32[]{:S(2)}) async-start(bf16[256,1,2,128]{3,2,1,0:T(2,128)(2,1)} %bitcast.14), calls=%async_computation.5 | async-start | bytes 262144 | tf_op jit(solution)/shard_map/all_to_all | solution.py:439
  127.2 0.0 copy-done.15
  127.2 0.0 copy-start.5
  127.2 1.0 copy-done.5
  128.2 0.0 copy-start.7
  128.2 0.0 copy-start.10
  128.2 0.0 copy-start.12
  128.2 0.8 shard_map.98
  129.0 0.1 copy-done.7
  129.1 0.1 copy-done.10
  129.2 0.0 copy-done.12
  129.2 1.1 shard_map.101
  130.3 9.6 %all-to-all-done.5 = bf16[256,1,2,128]{3,2,1,0:T(2,128)(2,1)S(1)} async-done(((bf16[256,1,2,128]{3,2,1,0:T(2,128)(2,1)}), bf16[256,1,2,128]{3,2,1,0:T(2,128)(2,1)S(1)}, u32[]{:S(2)}, u32[]{:S(2)}) %all-to-all-start.5) | async-done | bytes 131104 | tf_op jit(solution)/shard_map/all_to_all | solution.py:439
  139.9 0.8 shard_map.103
Async XLA Ops:
  3.2 29.9 %all-to-all-start = ((bf16[128,5,2,128]{3,2,1,0:T(2,128)(2,1)}), bf16[128,5,2,128]{3,2,1,0:T(2,128)(2,1)S(1)}, u32[]{:S(2)}, u32[]{:S(2)}) async-start(bf16[128,5,2,128]{3,2,1,0:T(2,128)(2,1)} %bitcast.35), calls=%async_computation | async-start | bytes 655360 | tf_op jit(solution)/shard_map/all_to_all | solution.py:439
  19.5 0.8 copy-start
  20.3 0.7 copy-start.2
  21.0 0.9 copy-start.6
  21.9 0.9 copy-start.8
  22.8 0.9 copy-start.9
  23.7 0.7 copy-start.11
  24.4 0.7 copy-start.13
  25.0 31.1 %copy-start.1 = (bf16[128,128]{1,0:T(8,128)(2,1)S(1)}, bf16[128,128]{1,0:T(8,128)(2,1)}, u32[]{:S(2)}) copy-start(bf16[128,128]{1,0:T(8,128)(2,1)} %out_weight_ref.3) | copy-start | bytes 98308
  25.0 31.1 %copy-start.3 = (f32[128]{0:T(128)S(1)}, f32[128]{0:T(128)}, u32[]{:S(2)}) copy-start(f32[128]{0:T(128)} %param.11) | copy-start | bytes 1540
  26.1 0.7 copy-start.14
  33.1 3.9 %collective-permute-start = (bf16[1280,128]{1,0:T(8,128)(2,1)S(1)}, bf16[1280,128]{1,0:T(8,128)(2,1)S(1)}, u32[]{:S(2)}, u32[]{:S(2)}) collective-permute-start(bf16[1280,128]{1,0:T(8,128)(2,1)S(1)} %bitcast.25), channel_id=1, source_target_pairs={{0,8},{8,0},{1,9},{9,1},{2,10},{10,2},{3,11},{11,3},{4,12},{12,4},... | collective-permute-start | bytes 983048 | tf_op jit(solution)/shard_map/ppermute | solution.py:443
  56.8 43.6 %copy-start.4 = (f32[128,768]{1,0:T(8,128)}, f32[128,768]{1,0:T(8,128)S(1)}, u32[]{:S(2)}) copy-start(f32[128,768]{1,0:T(8,128)S(1)} %get-tuple-element.34.out_proj_ref) | copy-start | bytes 1179652
  74.6 4.2 %collective-permute-start.1 = (bf16[768,128]{1,0:T(8,128)(2,1)S(1)}, bf16[768,128]{1,0:T(8,128)(2,1)S(1)}, u32[]{:S(2)}, u32[]{:S(2)}) collective-permute-start(bf16[768,128]{1,0:T(8,128)(2,1)S(1)} %bitcast.20), channel_id=1, source_target_pairs={{0,8},{8,0},{1,9},{9,1},{2,10},{10,2},{3,11},{11,3},{4,12},{12,4},... | collective-permute-start | bytes 589832 | tf_op jit(solution)/shard_map/ppermute | solution.py:443
  99.8 27.3 %copy-start.15 = (f32[128,768]{1,0:T(8,128)S(1)}, f32[128,768]{1,0:T(8,128)}, u32[]{:S(2)}) copy-start(f32[128,768]{1,0:T(8,128)} %copy-done.14) | copy-start | bytes 1179652
  121.1 18.8 %all-to-all-start.5 = ((bf16[256,1,2,128]{3,2,1,0:T(2,128)(2,1)}), bf16[256,1,2,128]{3,2,1,0:T(2,128)(2,1)S(1)}, u32[]{:S(2)}, u32[]{:S(2)}) async-start(bf16[256,1,2,128]{3,2,1,0:T(2,128)(2,1)} %bitcast.14), calls=%async_computation.5 | async-start | bytes 262144 | tf_op jit(solution)/shard_map/all_to_all | solution.py:439
  127.2 1.0 copy-start.5
  128.2 0.9 copy-start.7
  128.2 1.0 copy-start.10
  128.2 1.0 copy-start.12

commit v5 on v4

--- a/solution.py
+++ b/solution.py
@@ -19,6 +19,8 @@
 SIDE_ROWS = 10
 TRI_ROWS = 6
 VMEM_LIMIT = 48 * 1024 * 1024
+WHOLE_VMEM = 64 * 1024 * 1024 - 65536
+READY_VMEM = 62 * 1024 * 1024
 
 NT = (((1,), (1,)), ((), ()))
 NN = (((1,), (0,)), ((), ()))
@@ -198,13 +200,27 @@
 
 
 def ready_kernel(
-    mask_ref, acts_ref, cotangent_ref, gain_ref, weight_ref, out_gain_ref, out_weight_ref,
-    normed_ref, back_norm_ref, gate_mask_ref, gate_coef_ref, coef_ref, order_ref,
-    spread_ref, back_out_ref,
+    acts_hbm, gain_hbm, weight_hbm, cotangent_hbm, mask_hbm, out_weight_hbm, out_gain_hbm,
+    normed_ref, back_norm_ref, gate_mask_ref, gate_coef_ref, coef_ref,
+    acts_ref, gain_ref, weight_ref, cotangent_ref, mask_ref, out_weight_ref, out_gain_ref,
+    spread_ref, back_out_ref, sems,
 ):
     na = acts_ref.shape[0]
     tiles = na // 2
     hidden = out_weight_ref.shape[0]
+    copies = [
+        pltpu.make_async_copy(acts_hbm, acts_ref, sems.at[0]),
+        pltpu.make_async_copy(gain_hbm, gain_ref, sems.at[1]),
+        pltpu.make_async_copy(weight_hbm, weight_ref, sems.at[2]),
+        pltpu.make_async_copy(cotangent_hbm, cotangent_ref, sems.at[3]),
+        pltpu.make_async_copy(mask_hbm, mask_ref, sems.at[4]),
+        pltpu.make_async_copy(out_weight_hbm, out_weight_ref, sems.at[5]),
+        pltpu.make_async_copy(out_gain_hbm, out_gain_ref, sems.at[6]),
+    ]
+    for copy in copies:
+        copy.start()
+    for copy in copies:
+        copy.wait()
     spread(acts_ref, spread_ref)
     norm_tiles(spread_ref, gain_ref, normed_ref)
     spread(cotangent_ref, spread_ref)
@@ -228,6 +244,11 @@
     for t in range(tiles):
         at = slice(t * LANES, (t + 1) * LANES)
         back_norm_ref[:, at] = back_norm[:, at] * out_gain
+    back_norm_ref[:, tiles * LANES : (tiles + 1) * LANES] = out_gain
+    back_norm_ref[:, (tiles + 1) * LANES :] = out_weight_ref[...].astype(F32)
+
+
+def order_kernel(na, order_ref):
     order_ref[...] = token_order(na, order_ref.shape[1])
 
 
@@ -271,13 +292,14 @@
 
 
 def middle_kernel(
-    tri_ref, normed_ref, back_norm_ref, gate_coef_ref, out_gain_ref, out_weight_ref,
+    tri_ref, normed_ref, back_norm_ref, gate_coef_ref,
     back_ref, gate_ref, out_proj_ref,
     tri_chunk_ref, scaled_ref, normed_out_ref,
 ):
     tiles = normed_ref.shape[1] // LANES
     tri_chunk_ref[...] = tri_ref[...].astype(F32)
-    out_gain = column(out_gain_ref)
+    out_gain = back_norm_ref[:, tiles * LANES : (tiles + 1) * LANES]
+    out_weight = back_norm_ref[:, (tiles + 1) * LANES :].astype(BF16)
     inv_out = []
     for t in range(tiles):
         at = slice(t * LANES, (t + 1) * LANES)
@@ -285,7 +307,7 @@
         inv_out.append(inv)
         scaled_ref[:, at] = scaled
         normed_out_ref[:, at] = (scaled * out_gain).astype(BF16)
-    out_proj = matmul(out_weight_ref[...], normed_out_ref[...], TN)
+    out_proj = matmul(out_weight, normed_out_ref[...], TN)
     out_proj_ref[...] = out_proj
     gate_ref[...] = (out_proj * gate_coef_ref[...]).astype(BF16)
     term = matmul(normed_ref[...], gate_ref[...], NT)
@@ -398,15 +420,18 @@
     total = total + pltpu.roll(total, 2, 0)
     total = total / full_len
     total = jnp.concatenate([total, total], axis=0).astype(BF16)
-    for m in range(parts_ref.shape[0] // 16):
+    for m in range(out_ref.shape[0] // 16):
         out_ref[16 * m : 16 * m + 16, :] = total
 
 
-def grad_weight_kernel(sums_ref, gate_total_ref, out_ref, chunk_ref):
-    chunk_ref[...] = sums_ref[...].astype(F32)
+def grad_weight_kernel(mine_ref, theirs_ref, gate_total_ref, out_ref, chunk_ref):
+    core = lax.axis_index("core")
+    chunk_ref[core] = mine_ref[...].astype(F32)
+    chunk_ref[1 - core] = theirs_ref[...].astype(F32)
     for t in range(4):
-        for m in range(out_ref.shape[0] // 8):
-            out_ref[8 * m : 8 * m + 8, t * LANES : (t + 1) * LANES] = chunk_ref[weight_rows(m, t), :]
+        out_ref[:, t * LANES : (t + 1) * LANES] = chunk_ref[
+            t // 2, pl.ds(t % 2, out_ref.shape[0], stride=2), :
+        ]
     out_ref[:, 4 * LANES :] = gate_total_ref[...]
 
 
@@ -477,23 +502,36 @@
         100_000_000,
         4,
         pltpu.HBM,
-        64 * 1024 * 1024 - 65536,
+        WHOLE_VMEM,
     )(token_valid, pair_acts, gain, proj_weight)
     mine = exchange(sides, SIDE_ROWS, CHANNEL_AXES)
-    normed, back_norm, gate_mask, gate_coef, coef, order = local_call(
+    order = local_call(functools.partial(order_kernel, na), array(plane), [], 1_000_000_000, 0)()
+    normed, back_norm, gate_mask, gate_coef, coef = local_call(
         ready_kernel,
         (
             array((channels, lanes)),
-            array((hidden, lanes), F32),
+            array((hidden, lanes + 2 * LANES), F32),
             array((channels, lanes), F32),
             array((channels, lanes), F32),
             array((4 * hidden, lanes), F32),
-            array(plane),
         ),
-        [spread_scratch, pltpu.VMEM((channels, lanes), BF16)],
+        [
+            pltpu.VMEM(pair_acts.shape, BF16),
+            pltpu.VMEM(gain.shape, F32),
+            pltpu.VMEM(proj_weight.shape, BF16),
+            pltpu.VMEM(out_cotangent.shape, BF16),
+            pltpu.VMEM(mask.shape, F32),
+            pltpu.VMEM(out_weight.shape, BF16),
+            pltpu.VMEM(out_gain.shape, F32),
+            spread_scratch,
+            pltpu.VMEM((channels, lanes), BF16),
+            pltpu.SemaphoreType.DMA((7,)),
+        ],
         1_000_000_000,
         7,
-    )(mask, pair_acts, out_cotangent, gain, proj_weight, out_gain, out_weight)
+        pltpu.HBM,
+        READY_VMEM,
+    )(pair_acts, gain, proj_weight, out_cotangent, mask, out_weight, out_gain)
     mine, normed, order = lax.optimization_barrier((mine, normed, order))
     tri, left, right = local_call(
         functools.partial(tri_kernel, na),
@@ -512,8 +550,8 @@
             pltpu.VMEM((hidden, lanes), BF16),
         ],
         100_000_000,
-        6,
-    )(tri, normed, back_norm, gate_coef, out_gain, out_weight)
+        4,
+    )(tri, normed, back_norm, gate_coef)
     back = exchange(back, TRI_ROWS, CHANNEL_AXES)
     update = local_call(update_kernel, array(pair_acts.shape), [], 1_000_000_000, 2)(
         gate_mask, out_proj
@@ -543,15 +581,17 @@
         pair_kernel, array(pair_acts.shape), [spread_scratch], 1_000_000_000, 4
     )(pair_acts, gain, proj_weight, back_proj)
     parts = exchange(term, 2, ALL_AXES)
-    sums = local_call(functools.partial(sum_kernel, full_len), array(term_chunk), [], 100_000, 1)(parts)
-    sums = exchange(sums, 2, ALL_AXES)
+    sums = local_call(
+        functools.partial(sum_kernel, full_len), array((2 * hidden, LANES)), [], 100_000, 1
+    )(parts)
+    sums = exchange(sums, 2, ("chip", "col"))
     grad_weight = local_call(
         grad_weight_kernel,
         array((channels, width_all), F32),
-        [pltpu.VMEM(term_chunk, F32)],
+        [pltpu.VMEM((2, 2 * hidden, LANES), F32)],
         100_000,
-        2,
-    )(sums, gate_total)
+        3,
+    )(sums, other_core(sums), gate_total)
     return update, grad_pair, grad_weight
 
 

time: 141 us -> 142 us (level)
  local copies, waits for them, and re-layouts: 7.4 us -> 0.04 us
  waiting for transfers between devices: 18.1 us -> 21.9 us
  Pallas kernels: 10.8 us -> 13.3 us
  starting transfers between devices: 28.1 us -> 30.4 us
    unnamed x32 -> x16, local copies, waits for them, and re-layouts: 7.4 us -> 0.04 us
    all_to_all x2, waiting for transfers between devices: 15.8 us -> 19.5 us  [exchange(): return lax.all_to_all(split, axes, 0, 0, tiled=True).reshape(chunks.shape)]
    pallas_call x2 -> x3, Pallas kernels: 1.8 us -> 4.3 us  [the longest x1 3.52 us: per_device(): local_call(ready_kernel, (array((channels, lanes)), array((hidden, lanes...]
    ppermute x2 -> x3, starting transfers between devices: 5.73 us -> 7.95 us  [other_core(): return lax.ppermute(values, 'core', [(0, 1), (1, 0)])]
  transfers between devices with their start and end apart: 4 -> 5, of which waited for: 4 -> 4; matrix products, arithmetic and copies ran while one was open for 0% -> 0% of each run, Pallas kernels for 2% -> 4%
where the time goes in v5:
time: 142 us
  blocking collectives  75.6 us (53%)
  starting transfers between devices  30.4 us (21%)
  waiting for transfers between devices  21.9 us (15%)
  Pallas kernels  13.3 us (9%)
    all_to_all x4, blocking collectives, exchange(): return lax.all_to_all(split, axes, 0, 0, tiled=True).reshape(chunks.shape)  75.6 us
    all_to_all x2, starting transfers between devices, exchange(): return lax.all_to_all(split, axes, 0, 0, tiled=True).reshape(chunks.shape)  22.5 us
    all_to_all x2, waiting for transfers between devices, exchange(): return lax.all_to_all(split, axes, 0, 0, tiled=True).reshape(chunks.shape)  19.5 us
    ppermute x3, starting transfers between devices, other_core(): return lax.ppermute(values, 'core', [(0, 1), (1, 0)])  7.95 us
    pallas_call x1, Pallas kernels, per_device(): local_call(ready_kernel, (array((channels, lanes)), array((hidden, lanes...  3.52 us
  transfers between devices with their start and end apart: 5, of which 4 were waited for; matrix products, arithmetic and copies ran while one was open for 0% of the time, Pallas kernels for 4%

profile of v5, /device:TPU:1, one launch (start us, length us, event | category | flops | bytes accessed | tf_op | source)
XLA Modules:
  0.0 142.0 jit_solution(18305749854749955110)
XLA Ops:
  0.6 2.6 %shard_map.94 = (bf16[1280,128]{1,0:T(8,128)(2,1)}, f32[1,768]{1,0:T(1,128)}) custom-call(s32[384]{0:T(512)} %valid_hbm.1, bf16[12,48,128]{2,1,0:T(8,128)(2,1)} %acts_ref.1, f32[1,128]{1,0:T(1,128)} %bitcast.31, bf16[128,640]{1,0:T(8,128)(2,1)} %weight_ref.1), custom_call_target="tpu_custom_call" | custom-call | flops 100000000 | bytes 2000000 | tf_op jit(solution)/shard_map/pallas_call | solution.py:489
  3.2 16.3 %all-to-all-start = ((bf16[128,5,2,128]{3,2,1,0:T(2,128)(2,1)}), bf16[128,5,2,128]{3,2,1,0:T(2,128)(2,1)S(1)}, u32[]{:S(2)}, u32[]{:S(2)}) async-start(bf16[128,5,2,128]{3,2,1,0:T(2,128)(2,1)} %bitcast.34), calls=%async_computation | async-start | bytes 655360 | tf_op jit(solution)/shard_map/all_to_all | solution.py:464
  19.5 0.1 shard_map.96.order_ref
  19.7 3.5 %shard_map.95 = (bf16[128,768]{1,0:T(8,128)(2,1)}, f32[128,1024]{1,0:T(8,128)}, f32[128,768]{1,0:T(8,128)}, f32[128,768]{1,0:T(8,128)}, f32[512,768]{1,0:T(8,128)}) custom-call(bf16[12,48,128]{2,1,0:T(8,128)(2,1)} %acts_ref.1, f32[1,128]{1,0:T(1,128)} %bitcast.32, bf16[128,640]{1,0:T(8,128)(2,1)} %weight_ref.1, bf16[12,48,128]{2,1,0:T(8,128)(2,1)} %cotangent_hbm.1, ...), custom_call_target="tpu_custom_call" | custom-call | flops 1000000000 | bytes 2000000 | tf_op jit(solution)/shard_map/pallas_call | solution.py:509
  23.2 0.0 copy-start.1
  23.2 0.0 copy-start.2
  23.2 0.0 copy-start.3
  23.2 9.9 %all-to-all-done = bf16[128,5,2,128]{3,2,1,0:T(2,128)(2,1)S(1)} async-done(((bf16[128,5,2,128]{3,2,1,0:T(2,128)(2,1)}), bf16[128,5,2,128]{3,2,1,0:T(2,128)(2,1)S(1)}, u32[]{:S(2)}, u32[]{:S(2)}) %all-to-all-start) | async-done | bytes 327712 | tf_op jit(solution)/shard_map/all_to_all | solution.py:464
  33.1 2.6 %collective-permute-start = (bf16[1280,128]{1,0:T(8,128)(2,1)S(1)}, bf16[1280,128]{1,0:T(8,128)(2,1)S(1)}, u32[]{:S(2)}, u32[]{:S(2)}) collective-permute-start(bf16[1280,128]{1,0:T(8,128)(2,1)S(1)} %bitcast.24), channel_id=1, source_target_pairs={{0,8},{8,0},{1,9},{9,1},{2,10},{10,2},{3,11},{11,3},{4,12},{12,4},... | collective-permute-start | bytes 983048 | tf_op jit(solution)/shard_map/ppermute | solution.py:468
  35.7 1.3 collective-permute-done.theirs_ref
  37.0 1.3 shard_map.97
  38.3 17.9 %all_to_all.30 = bf16[128,3,2,128]{3,2,1,0:T(2,128)(2,1)S(1)} all-to-all(bf16[128,3,2,128]{3,2,1,0:T(2,128)(2,1)S(1)} %bitcast.29), channel_id=1, replica_groups=mesh['chip'=16,'core'=2,'col'=8] {'col','chip'}, dimensions={0} | all-to-all | bytes 393216 | tf_op jit(solution)/shard_map/all_to_all | solution.py:464
  56.1 0.0 copy-done.1
  56.1 0.0 copy-done.2
  56.1 0.0 copy-done.3
  56.1 0.6 shard_map.98
  56.8 0.0 copy-start
  56.8 17.9 %all_to_all.31 = bf16[128,3,2,128]{3,2,1,0:T(2,128)(2,1)S(1)} all-to-all(bf16[128,3,2,128]{3,2,1,0:T(2,128)(2,1)S(1)} %bitcast.28), channel_id=1, replica_groups=mesh['chip'=16,'core'=2,'col'=8] {'col','chip'}, dimensions={0} | all-to-all | bytes 393216 | tf_op jit(solution)/shard_map/all_to_all | solution.py:464
  74.7 3.1 %collective-permute-start.1 = (bf16[768,128]{1,0:T(8,128)(2,1)S(1)}, bf16[768,128]{1,0:T(8,128)(2,1)S(1)}, u32[]{:S(2)}, u32[]{:S(2)}) collective-permute-start(bf16[768,128]{1,0:T(8,128)(2,1)S(1)} %bitcast.20), channel_id=1, source_target_pairs={{0,8},{8,0},{1,9},{9,1},{2,10},{10,2},{3,11},{11,3},{4,12},{12,4},... | collective-permute-start | bytes 589832 | tf_op jit(solution)/shard_map/ppermute | solution.py:468
  77.8 1.1 collective-permute-done.1.theirs_ref
  78.9 1.3 shard_map.100
  80.1 19.8 %all_to_all.32 = bf16[128,5,2,128]{3,2,1,0:T(2,128)(2,1)S(1)} all-to-all(bf16[128,5,2,128]{3,2,1,0:T(2,128)(2,1)S(1)} %bitcast.19), channel_id=1, replica_groups=mesh['chip'=16,'core'=2,'col'=8] {'col','chip'}, dimensions={0} | all-to-all | bytes 655360 | tf_op jit(solution)/shard_map/all_to_all | solution.py:464
  100.0 0.0 copy-start.7
  100.0 0.0 copy-done
  100.0 0.5 shard_map.101
  100.5 20.0 %all_to_all.33 = bf16[256,1,2,128]{3,2,1,0:T(2,128)(2,1)S(1)} all-to-all(bf16[256,1,2,128]{3,2,1,0:T(2,128)(2,1)S(1)} %bitcast.30), channel_id=1, replica_groups=mesh['chip'=16,'core'=2,'col'=8] {'chip','core','col'}, dimensions={0} | all-to-all | bytes 262144 | tf_op jit(solution)/shard_map/all_to_all | solution.py:464
  120.5 0.7 shard_map.103
  121.2 6.2 %all-to-all-start.5 = ((bf16[128,1,2,128]{3,2,1,0:T(2,128)(2,1)}), bf16[128,1,2,128]{3,2,1,0:T(2,128)(2,1)S(1)}, u32[]{:S(2)}, u32[]{:S(2)}) async-start(bf16[128,1,2,128]{3,2,1,0:T(2,128)(2,1)} %bitcast.14), calls=%async_computation.5 | async-start | bytes 131072 | tf_op jit(solution)/shard_map/all_to_all | solution.py:464
  127.3 0.0 copy-done.7
  127.3 0.0 copy-start.4
  127.3 0.0 copy-start.5
  127.3 0.0 copy-start.6
  127.4 0.8 shard_map.99
  128.2 9.6 %all-to-all-done.5 = bf16[128,1,2,128]{3,2,1,0:T(2,128)(2,1)S(1)} async-done(((bf16[128,1,2,128]{3,2,1,0:T(2,128)(2,1)}), bf16[128,1,2,128]{3,2,1,0:T(2,128)(2,1)S(1)}, u32[]{:S(2)}, u32[]{:S(2)}) %all-to-all-start.5) | async-done | bytes 65568 | tf_op jit(solution)/shard_map/all_to_all | solution.py:464
  137.8 2.2 %collective-permute-start.2 = (bf16[256,128]{1,0:T(8,128)(2,1)S(1)}, bf16[256,128]{1,0:T(8,128)(2,1)S(1)}, u32[]{:S(2)}, u32[]{:S(2)}) collective-permute-start(bf16[256,128]{1,0:T(8,128)(2,1)S(1)} %bitcast.26), channel_id=1, source_target_pairs={{0,8},{8,0},{1,9},{9,1},{2,10},{10,2},{3,11},{11,3},{4,12},{12,4},... | collective-permute-start | bytes 196616 | tf_op jit(solution)/shard_map/ppermute | solution.py:468
  140.0 0.0 copy-done.4
  140.0 0.0 copy-done.5
  140.0 0.0 copy-done.6
  140.0 1.2 shard_map.102
  141.2 0.0 collective-permute-done.2.theirs_ref
  141.2 0.8 shard_map.104
Async XLA Ops:
  3.2 29.9 %all-to-all-start = ((bf16[128,5,2,128]{3,2,1,0:T(2,128)(2,1)}), bf16[128,5,2,128]{3,2,1,0:T(2,128)(2,1)S(1)}, u32[]{:S(2)}, u32[]{:S(2)}) async-start(bf16[128,5,2,128]{3,2,1,0:T(2,128)(2,1)} %bitcast.34), calls=%async_computation | async-start | bytes 655360 | tf_op jit(solution)/shard_map/all_to_all | solution.py:464
  23.2 32.9 %copy-start.1 = (bf16[128,768]{1,0:T(8,128)(2,1)S(1)}, bf16[128,768]{1,0:T(8,128)(2,1)}, u32[]{:S(2)}) copy-start(bf16[128,768]{1,0:T(8,128)(2,1)} %get-tuple-element.29.normed_ref) | copy-start | bytes 589828
  23.2 32.9 %copy-start.2 = (f32[128,1024]{1,0:T(8,128)S(1)}, f32[128,1024]{1,0:T(8,128)}, u32[]{:S(2)}) copy-start(f32[128,1024]{1,0:T(8,128)} %get-tuple-element.30.back_norm_ref) | copy-start | bytes 1572868
  23.2 32.9 %copy-start.3 = (f32[128,768]{1,0:T(8,128)S(1)}, f32[128,768]{1,0:T(8,128)}, u32[]{:S(2)}) copy-start(f32[128,768]{1,0:T(8,128)} %get-tuple-element.31.gate_coef_ref) | copy-start | bytes 1179652
  33.1 3.9 %collective-permute-start = (bf16[1280,128]{1,0:T(8,128)(2,1)S(1)}, bf16[1280,128]{1,0:T(8,128)(2,1)S(1)}, u32[]{:S(2)}, u32[]{:S(2)}) collective-permute-start(bf16[1280,128]{1,0:T(8,128)(2,1)S(1)} %bitcast.24), channel_id=1, source_target_pairs={{0,8},{8,0},{1,9},{9,1},{2,10},{10,2},{3,11},{11,3},{4,12},{12,4},... | collective-permute-start | bytes 983048 | tf_op jit(solution)/shard_map/ppermute | solution.py:468
  56.8 43.2 %copy-start = (f32[512,768]{1,0:T(8,128)S(1)}, f32[512,768]{1,0:T(8,128)}, u32[]{:S(2)}) copy-start(f32[512,768]{1,0:T(8,128)} %get-tuple-element.36.coef_ref) | copy-start | bytes 4718596
  74.7 4.2 %collective-permute-start.1 = (bf16[768,128]{1,0:T(8,128)(2,1)S(1)}, bf16[768,128]{1,0:T(8,128)(2,1)S(1)}, u32[]{:S(2)}, u32[]{:S(2)}) collective-permute-start(bf16[768,128]{1,0:T(8,128)(2,1)S(1)} %bitcast.20), channel_id=1, source_target_pairs={{0,8},{8,0},{1,9},{9,1},{2,10},{10,2},{3,11},{11,3},{4,12},{12,4},... | collective-permute-start | bytes 589832 | tf_op jit(solution)/shard_map/ppermute | solution.py:468
  100.0 27.4 %copy-start.7 = (f32[128,768]{1,0:T(8,128)S(1)}, f32[128,768]{1,0:T(8,128)}, u32[]{:S(2)}) copy-start(f32[128,768]{1,0:T(8,128)} %get-tuple-element.23.gate_mask_ref) | copy-start | bytes 1179652
  121.2 16.7 %all-to-all-start.5 = ((bf16[128,1,2,128]{3,2,1,0:T(2,128)(2,1)}), bf16[128,1,2,128]{3,2,1,0:T(2,128)(2,1)S(1)}, u32[]{:S(2)}, u32[]{:S(2)}) async-start(bf16[128,1,2,128]{3,2,1,0:T(2,128)(2,1)} %bitcast.14), calls=%async_computation.5 | async-start | bytes 131072 | tf_op jit(solution)/shard_map/all_to_all | solution.py:464
  127.3 12.7 %copy-start.4 = (bf16[128,640]{1,0:T(8,128)(2,1)S(1)}, bf16[128,640]{1,0:T(8,128)(2,1)}, u32[]{:S(2)}) copy-start(bf16[128,640]{1,0:T(8,128)(2,1)} %weight_ref.1) | copy-start | bytes 491524
  127.3 12.7 %copy-start.5 = (bf16[12,48,128]{2,1,0:T(8,128)(2,1)S(1)}, bf16[12,48,128]{2,1,0:T(8,128)(2,1)}, u32[]{:S(2)}) copy-start(bf16[12,48,128]{2,1,0:T(8,128)(2,1)} %acts_ref.1) | copy-start | bytes 442372
  127.3 12.7 %copy-start.6 = (f32[128]{0:T(128)S(1)}, f32[128]{0:T(128)}, u32[]{:S(2)}) copy-start(f32[128]{0:T(128)} %param.9) | copy-start | bytes 1540
  137.8 3.4 %collective-permute-start.2 = (bf16[256,128]{1,0:T(8,128)(2,1)S(1)}, bf16[256,128]{1,0:T(8,128)(2,1)S(1)}, u32[]{:S(2)}, u32[]{:S(2)}) collective-permute-start(bf16[256,128]{1,0:T(8,128)(2,1)S(1)} %bitcast.26), channel_id=1, source_target_pairs={{0,8},{8,0},{1,9},{9,1},{2,10},{10,2},{3,11},{11,3},{4,12},{12,4},... | collective-permute-start | bytes 196616 | tf_op jit(solution)/shard_map/ppermute | solution.py:468

commit v6 on v5

--- a/solution.py
+++ b/solution.py
@@ -153,8 +153,10 @@
     row = lax.broadcasted_iota(jnp.int32, (16 * 2 * na, plane), 0)
     token = lax.broadcasted_iota(jnp.int32, (16 * 2 * na, plane), 1)
     place = row // 8
-    core = (place >= 2 * na).astype(jnp.int32)
-    place = place - 2 * na * core
+    theirs = (place >= 2 * na).astype(jnp.int32)
+    place = place - 2 * na * theirs
+    core = lax.axis_index("core")
+    core = core + theirs * (1 - 2 * core)
     lo = (place >= na).astype(jnp.int32)
     a = place - na * lo
     return (token == SLOT * (row % 8) + na * (2 * lo + core) + a).astype(F32).astype(BF16)
@@ -252,35 +254,38 @@
     order_ref[...] = token_order(na, order_ref.shape[1])
 
 
-def my_rows(ref):
-    half = ref.shape[-2] // 2
-    return pl.ds(pl.multiple_of(lax.axis_index("core") * half, half), half)
+def side_planes(na, chunk_ref, left_ref, right_ref, first):
+    tiles = na // 2
+    for pair in range(4):
+        at = slice(pair * LANES, (pair + 1) * LANES)
+        for lo in range(2):
+            even, odd = [
+                unpack_tiles([chunk_ref[group_rows(SIDE_ROWS, lo, col, t), :] for t in range(9)])
+                for col in (2 * pair, 2 * pair + 1)
+            ]
+            for t in range(tiles):
+                rows = plane_rows(na, lo, t)
+                rows = slice(first + rows.start, first + rows.stop)
+                left_ref[rows, at] = plane_tile(even[t], odd[t]).astype(BF16)
+                right_ref[rows, at] = plane_tile(even[tiles + t], odd[tiles + t]).astype(BF16)
+
+
+def own_sides_kernel(na, mine_ref, left_ref, right_ref, chunk_ref):
+    chunk_ref[...] = mine_ref[...].astype(F32)
+    side_planes(na, chunk_ref, left_ref, right_ref, 0)
 
 
 def tri_kernel(
-    na, mine_ref, theirs_ref, order_ref, tri_ref, left_ref, right_ref, chunk_ref, tri_chunk_ref
+    na, theirs_ref, left_mine_ref, right_mine_ref, order_ref, tri_ref, left_ref, right_ref,
+    chunk_ref, tri_chunk_ref,
 ):
     tiles = na // 2
-    core = lax.axis_index("core")
-    chunk_ref[core] = mine_ref[...].astype(F32)
-    chunk_ref[1 - core] = theirs_ref[...].astype(F32)
-    half = left_ref.shape[0] // 2
-    for side in range(2):
-        for pair in range(4):
-            at = slice(pair * LANES, (pair + 1) * LANES)
-            for lo in range(2):
-                even, odd = [
-                    unpack_tiles(
-                        [chunk_ref[side, group_rows(SIDE_ROWS, lo, col, t), :] for t in range(9)]
-                    )
-                    for col in (2 * pair, 2 * pair + 1)
-                ]
-                for t in range(tiles):
-                    rows = plane_rows(na, lo, t)
-                    rows = slice(side * half + rows.start, side * half + rows.stop)
-                    left_ref[rows, at] = plane_tile(even[t], odd[t]).astype(BF16)
-                    right_ref[rows, at] = plane_tile(even[tiles + t], odd[tiles + t]).astype(BF16)
-    tri = matmul(left_ref[my_rows(left_ref), :], right_ref[...], NT).astype(BF16)
+    half = left_mine_ref.shape[0]
+    chunk_ref[...] = theirs_ref[...].astype(F32)
+    left_ref[0:half, :] = left_mine_ref[...]
+    right_ref[0:half, :] = right_mine_ref[...]
+    side_planes(na, chunk_ref, left_ref, right_ref, half)
+    tri = matmul(left_mine_ref[...], right_ref[...], NT).astype(BF16)
     tri = matmul(tri, order_ref[...])
     for pair in range(4):
         for lo in range(2):
@@ -328,56 +333,63 @@
         store_pairs(update_ref, t, gate_mask_ref[:, at] * out_proj_ref[:, at])
 
 
-def back_kernel(
-    na, mine_ref, theirs_ref, left_ref, right_ref, order_ref, out_ref,
-    back_chunk_ref, chunk_ref, back_ref, turned_ref, side_ref,
-):
-    tiles = na // 2
-    core = lax.axis_index("core")
-    back_chunk_ref[core] = mine_ref[...].astype(F32)
-    back_chunk_ref[1 - core] = theirs_ref[...].astype(F32)
-    half = back_ref.shape[0] // 2
+def back_plane(na, chunk_ref, plane_ref):
     free = gap((8, LANES))
-    for side in range(2):
-        for pair in range(4):
-            for lo in range(2):
-                for t in range(tiles):
-                    even, odd = [
-                        jnp.where(free, 0.0, back_chunk_ref[side, group_rows(TRI_ROWS, lo, col, t), :])
-                        for col in (2 * pair, 2 * pair + 1)
-                    ]
-                    rows = plane_rows(na, lo, t)
-                    rows = slice(side * half + rows.start, side * half + rows.stop)
-                    back_ref[rows, pair * LANES : (pair + 1) * LANES] = plane_tile(even, odd).astype(BF16)
-    turned_ref[...] = matmul(back_ref[...], order_ref[...], NT).astype(BF16)
-    back_left = matmul(turned_ref[my_rows(turned_ref), :], right_ref[...])
-    side_ref[...] = matmul(turned_ref[...], left_ref[...], TN)
-    back_right = side_ref[my_rows(side_ref), :]
-
+    for pair in range(4):
+        for lo in range(2):
+            for t in range(na // 2):
+                even, odd = [
+                    jnp.where(free, 0.0, chunk_ref[group_rows(TRI_ROWS, lo, col, t), :])
+                    for col in (2 * pair, 2 * pair + 1)
+                ]
+                plane_ref[plane_rows(na, lo, t), pair * LANES : (pair + 1) * LANES] = plane_tile(
+                    even, odd
+                ).astype(BF16)
+
+
+def gap_total(chunk_ref):
     place = lax.broadcasted_iota(jnp.int32, (8, LANES), 1) % SLOT // PIECE
     total = jnp.zeros((8, LANES), F32)
     for t in range(4):
         rows = jnp.zeros((8, LANES), F32)
-        for side in range(2):
-            for m in range(back_chunk_ref.shape[1] // (8 * TRI_ROWS)):
-                rows += back_chunk_ref[side, pl.ds(8 * TRI_ROWS * m + t, 8, stride=TRI_ROWS), :]
-        rows = jnp.sum(rows, axis=0, keepdims=True)
-        rows = jnp.broadcast_to(rows, (8, LANES))
+        for m in range(chunk_ref.shape[0] // (8 * TRI_ROWS)):
+            rows += chunk_ref[pl.ds(8 * TRI_ROWS * m + t, 8, stride=TRI_ROWS), :]
+        rows = jnp.broadcast_to(jnp.sum(rows, axis=0, keepdims=True), (8, LANES))
         if t < 3:
             rows = pltpu.roll(rows, LANES - (SLOT - PIECE) + PIECE * t, 1)
         total = jnp.where(place == t, rows, total)
-    total = total / (4 * 8 * na)
+    return total
+
+
+def own_back_kernel(
+    na, mine_ref, right_ref, order_ref, turned_ref, back_left_ref, total_ref, chunk_ref, plane_ref
+):
+    chunk_ref[...] = mine_ref[...].astype(F32)
+    back_plane(na, chunk_ref, plane_ref)
+    turned_ref[...] = matmul(plane_ref[...], order_ref[...], NT).astype(BF16)
+    back_left_ref[...] = matmul(turned_ref[...], right_ref[...])
+    total_ref[...] = gap_total(chunk_ref)
+
+
+def back_kernel(
+    na, theirs_ref, turned_mine_ref, back_left_ref, total_ref, left_ref, order_ref, out_ref,
+    back_chunk_ref, chunk_ref, plane_ref, turned_ref,
+):
+    tiles = na // 2
+    half = turned_mine_ref.shape[0]
+    back_chunk_ref[...] = theirs_ref[...].astype(F32)
+    back_plane(na, back_chunk_ref, plane_ref)
+    turned_ref[0:half, :] = turned_mine_ref[...]
+    turned_ref[half:, :] = matmul(plane_ref[...], order_ref[...], NT).astype(BF16)
+    back_right = matmul(turned_ref[:, 0:half], left_ref[...], TN)
+    total = (total_ref[...] + gap_total(back_chunk_ref)) / (4 * 8 * na)
     for m in range(chunk_ref.shape[0] // (8 * SIDE_ROWS)):
         chunk_ref[pl.ds(8 * SIDE_ROWS * m + 9, 8, stride=SIDE_ROWS), :] = total
-
     for pair in range(4):
         at = slice(pair * LANES, (pair + 1) * LANES)
         for lo in range(2):
-            found = [
-                chunk_tiles(product[plane_rows(na, lo, t), at])
-                for product in (back_left, back_right)
-                for t in range(tiles)
-            ]
+            found = [chunk_tiles(back_left_ref[plane_rows(na, lo, t), at]) for t in range(tiles)]
+            found += [chunk_tiles(back_right[plane_rows(na, lo, t), at]) for t in range(tiles)]
             for side in range(2):
                 for t, row in enumerate(pack_tiles([both[side] for both in found])):
                     chunk_ref[group_rows(SIDE_ROWS, lo, 2 * pair + side, t), :] = row
@@ -424,14 +436,11 @@
         out_ref[16 * m : 16 * m + 16, :] = total
 
 
-def grad_weight_kernel(mine_ref, theirs_ref, gate_total_ref, out_ref, chunk_ref):
-    core = lax.axis_index("core")
-    chunk_ref[core] = mine_ref[...].astype(F32)
-    chunk_ref[1 - core] = theirs_ref[...].astype(F32)
+def grad_weight_kernel(sums_ref, gate_total_ref, out_ref, chunk_ref):
+    chunk_ref[...] = sums_ref[...].astype(F32)
     for t in range(4):
-        out_ref[:, t * LANES : (t + 1) * LANES] = chunk_ref[
-            t // 2, pl.ds(t % 2, out_ref.shape[0], stride=2), :
-        ]
+        for m in range(out_ref.shape[0] // 8):
+            out_ref[8 * m : 8 * m + 8, t * LANES : (t + 1) * LANES] = chunk_ref[weight_rows(m, t), :]
     out_ref[:, 4 * LANES :] = gate_total_ref[...]
 
 
@@ -533,13 +542,22 @@
         READY_VMEM,
     )(pair_acts, gain, proj_weight, out_cotangent, mask, out_weight, out_gain)
     mine, normed, order = lax.optimization_barrier((mine, normed, order))
+    half_plane = (full_len // 2, plane[1])
+    theirs = other_core(mine)
+    left_mine, right_mine = local_call(
+        functools.partial(own_sides_kernel, na),
+        (array(half_plane), array(half_plane)),
+        [pltpu.VMEM(sides_chunk, F32)],
+        1_000_000_000,
+        1,
+    )(mine)
     tri, left, right = local_call(
         functools.partial(tri_kernel, na),
         (array(tri_chunk), array(plane), array(plane)),
-        [pltpu.VMEM((2,) + sides_chunk, F32), pltpu.VMEM(tri_chunk, F32)],
+        [pltpu.VMEM(sides_chunk, F32), pltpu.VMEM(tri_chunk, F32)],
         300_000_000,
-        3,
-    )(mine, other_core(mine), order)
+        4,
+    )(theirs, left_mine, right_mine, order)
     tri = exchange(tri, TRI_ROWS, CHANNEL_AXES)
     back, gate, out_proj = local_call(
         middle_kernel,
@@ -556,19 +574,26 @@
     update = local_call(update_kernel, array(pair_acts.shape), [], 1_000_000_000, 2)(
         gate_mask, out_proj
     )
+    theirs = other_core(back)
+    turned, back_left, total = local_call(
+        functools.partial(own_back_kernel, na),
+        (array((full_len // 2, full_len)), array(half_plane, F32), array((8, LANES), F32)),
+        [pltpu.VMEM(tri_chunk, F32), pltpu.VMEM(half_plane, BF16)],
+        1_000_000_000,
+        3,
+    )(back, right, order)
     back_sides = local_call(
         functools.partial(back_kernel, na),
         array(sides_chunk),
         [
-            pltpu.VMEM((2,) + tri_chunk, F32),
+            pltpu.VMEM(tri_chunk, F32),
             pltpu.VMEM(sides_chunk, F32),
-            pltpu.VMEM(plane, BF16),
+            pltpu.VMEM(half_plane, BF16),
             pltpu.VMEM((full_len, full_len), BF16),
-            pltpu.VMEM(plane, F32),
         ],
         300_000_000,
-        5,
-    )(back, other_core(back), left, right, order)
+        6,
+    )(theirs, turned, back_left, total, left, order)
     back_sides = exchange(back_sides, SIDE_ROWS, CHANNEL_AXES)
     term, back_proj, gate_total = local_call(
         weight_kernel,
@@ -581,17 +606,15 @@
         pair_kernel, array(pair_acts.shape), [spread_scratch], 1_000_000_000, 4
     )(pair_acts, gain, proj_weight, back_proj)
     parts = exchange(term, 2, ALL_AXES)
-    sums = local_call(
-        functools.partial(sum_kernel, full_len), array((2 * hidden, LANES)), [], 100_000, 1
-    )(parts)
-    sums = exchange(sums, 2, ("chip", "col"))
+    sums = local_call(functools.partial(sum_kernel, full_len), array(term_chunk), [], 100_000, 1)(parts)
+    sums = exchange(sums, 2, ALL_AXES)
     grad_weight = local_call(
         grad_weight_kernel,
         array((channels, width_all), F32),
-        [pltpu.VMEM((2, 2 * hidden, LANES), F32)],
+        [pltpu.VMEM(term_chunk, F32)],
         100_000,
-        3,
-    )(sums, other_core(sums), gate_total)
+        2,
+    )(sums, gate_total)
     return update, grad_pair, grad_weight
 
 

time: 142 us -> 140 us (0.986)
  starting transfers between devices: 30.4 us -> 28.2 us
    ppermute x3 -> x2, starting transfers between devices: 7.95 us -> 5.73 us  [other_core(): return lax.ppermute(values, 'core', [(0, 1), (1, 0)])]
  transfers between devices with their start and end apart: 5 -> 4, of which waited for: 4 -> 4; matrix products, arithmetic and copies ran while one was open for 0% -> 0% of each run, Pallas kernels for 4% -> 5%
where the time goes in v6:
time: 140 us
  blocking collectives  75.6 us (54%)
  starting transfers between devices  28.2 us (20%)
  waiting for transfers between devices  21.7 us (16%)
  Pallas kernels  13.5 us (10%)
    all_to_all x4, blocking collectives, exchange(): return lax.all_to_all(split, axes, 0, 0, tiled=True).reshape(chunks.shape)  75.6 us
    all_to_all x2, starting transfers between devices, exchange(): return lax.all_to_all(split, axes, 0, 0, tiled=True).reshape(chunks.shape)  22.4 us
    all_to_all x2, waiting for transfers between devices, exchange(): return lax.all_to_all(split, axes, 0, 0, tiled=True).reshape(chunks.shape)  20.5 us
    ppermute x2, starting transfers between devices, other_core(): return lax.ppermute(values, 'core', [(0, 1), (1, 0)])  5.73 us
    pallas_call x1, Pallas kernels, per_device(): local_call(ready_kernel, (array((channels, lanes)), array((hidden, lanes...  3.51 us
  transfers between devices with their start and end apart: 4, of which 4 were waited for; matrix products, arithmetic and copies ran while one was open for 0% of the time, Pallas kernels for 5%

profile of v6, /device:TPU:1, one launch (start us, length us, event | category | flops | bytes accessed | tf_op | source)
XLA Modules:
  0.0 140.0 jit_solution(15959600547815615200)
XLA Ops:
  0.6 2.6 %shard_map.94 = (bf16[1280,128]{1,0:T(8,128)(2,1)}, f32[1,768]{1,0:T(1,128)}) custom-call(s32[384]{0:T(512)} %valid_hbm.1, bf16[12,48,128]{2,1,0:T(8,128)(2,1)} %acts_ref.1, f32[1,128]{1,0:T(1,128)} %bitcast.30, bf16[128,640]{1,0:T(8,128)(2,1)} %weight_ref.1), custom_call_target="tpu_custom_call" | custom-call | flops 100000000 | bytes 2000000 | tf_op jit(solution)/shard_map/pallas_call | solution.py:498
  3.2 16.3 %all-to-all-start = ((bf16[128,5,2,128]{3,2,1,0:T(2,128)(2,1)}), bf16[128,5,2,128]{3,2,1,0:T(2,128)(2,1)S(1)}, u32[]{:S(2)}, u32[]{:S(2)}) async-start(bf16[128,5,2,128]{3,2,1,0:T(2,128)(2,1)} %bitcast.33), calls=%async_computation | async-start | bytes 655360 | tf_op jit(solution)/shard_map/all_to_all | solution.py:473
  19.5 0.1 shard_map.96.order_ref
  19.7 3.5 %shard_map.95 = (bf16[128,768]{1,0:T(8,128)(2,1)}, f32[128,1024]{1,0:T(8,128)}, f32[128,768]{1,0:T(8,128)}, f32[128,768]{1,0:T(8,128)}, f32[512,768]{1,0:T(8,128)}) custom-call(bf16[12,48,128]{2,1,0:T(8,128)(2,1)} %acts_ref.1, f32[1,128]{1,0:T(1,128)} %bitcast.31, bf16[128,640]{1,0:T(8,128)(2,1)} %weight_ref.1, bf16[12,48,128]{2,1,0:T(8,128)(2,1)} %cotangent_hbm.1, ...), custom_call_target="tpu_custom_call" | custom-call | flops 1000000000 | bytes 2000000 | tf_op jit(solution)/shard_map/pallas_call | solution.py:518
  23.2 9.9 %all-to-all-done = bf16[128,5,2,128]{3,2,1,0:T(2,128)(2,1)S(1)} async-done(((bf16[128,5,2,128]{3,2,1,0:T(2,128)(2,1)}), bf16[128,5,2,128]{3,2,1,0:T(2,128)(2,1)S(1)}, u32[]{:S(2)}, u32[]{:S(2)}) %all-to-all-start) | async-done | bytes 327712 | tf_op jit(solution)/shard_map/all_to_all | solution.py:473
  33.1 2.6 %collective-permute-start = (bf16[1280,128]{1,0:T(8,128)(2,1)S(1)}, bf16[1280,128]{1,0:T(8,128)(2,1)S(1)}, u32[]{:S(2)}, u32[]{:S(2)}) collective-permute-start(bf16[1280,128]{1,0:T(8,128)(2,1)S(1)} %bitcast.23), channel_id=1, source_target_pairs={{0,8},{8,0},{1,9},{9,1},{2,10},{10,2},{3,11},{11,3},{4,12},{12,4},... | collective-permute-start | bytes 983048 | tf_op jit(solution)/shard_map/ppermute | solution.py:477
  35.7 0.5 shard_map.97
  36.2 0.0 copy-start.1
  36.2 0.0 copy-start.2
  36.3 0.0 copy-start.3
  36.3 0.7 collective-permute-done.theirs_ref
  37.0 0.8 shard_map.98
  37.8 17.9 %all_to_all.30 = bf16[128,3,2,128]{3,2,1,0:T(2,128)(2,1)S(1)} all-to-all(bf16[128,3,2,128]{3,2,1,0:T(2,128)(2,1)S(1)} %bitcast.27), channel_id=1, replica_groups=mesh['chip'=16,'core'=2,'col'=8] {'col','chip'}, dimensions={0} | all-to-all | bytes 393216 | tf_op jit(solution)/shard_map/all_to_all | solution.py:473
  55.7 0.0 copy-done.1
  55.7 0.0 copy-done.2
  55.7 0.0 copy-done.3
  55.7 0.6 shard_map.99
  56.4 17.8 %all_to_all.31 = bf16[128,3,2,128]{3,2,1,0:T(2,128)(2,1)S(1)} all-to-all(bf16[128,3,2,128]{3,2,1,0:T(2,128)(2,1)S(1)} %bitcast.28), channel_id=1, replica_groups=mesh['chip'=16,'core'=2,'col'=8] {'col','chip'}, dimensions={0} | all-to-all | bytes 393216 | tf_op jit(solution)/shard_map/all_to_all | solution.py:473
  74.1 3.1 %collective-permute-start.1 = (bf16[768,128]{1,0:T(8,128)(2,1)S(1)}, bf16[768,128]{1,0:T(8,128)(2,1)S(1)}, u32[]{:S(2)}, u32[]{:S(2)}) collective-permute-start(bf16[768,128]{1,0:T(8,128)(2,1)S(1)} %bitcast.25), channel_id=1, source_target_pairs={{0,8},{8,0},{1,9},{9,1},{2,10},{10,2},{3,11},{11,3},{4,12},{12,4},... | collective-permute-start | bytes 589832 | tf_op jit(solution)/shard_map/ppermute | solution.py:477
  77.2 0.6 shard_map.101
  77.8 0.0 copy-start
  77.8 0.5 collective-permute-done.1.theirs_ref
  78.3 0.9 shard_map.102
  79.2 20.0 %all_to_all.32 = bf16[128,5,2,128]{3,2,1,0:T(2,128)(2,1)S(1)} all-to-all(bf16[128,5,2,128]{3,2,1,0:T(2,128)(2,1)S(1)} %bitcast.19), channel_id=1, replica_groups=mesh['chip'=16,'core'=2,'col'=8] {'col','chip'}, dimensions={0} | all-to-all | bytes 655360 | tf_op jit(solution)/shard_map/all_to_all | solution.py:473
  99.2 0.0 copy-start.7
  99.2 0.0 copy-done
  99.2 0.5 shard_map.103
  99.7 20.0 %all_to_all.33 = bf16[256,1,2,128]{3,2,1,0:T(2,128)(2,1)S(1)} all-to-all(bf16[256,1,2,128]{3,2,1,0:T(2,128)(2,1)S(1)} %bitcast.29), channel_id=1, replica_groups=mesh['chip'=16,'core'=2,'col'=8] {'chip','core','col'}, dimensions={0} | all-to-all | bytes 262144 | tf_op jit(solution)/shard_map/all_to_all | solution.py:473
  119.7 0.7 shard_map.105
  120.4 6.1 %all-to-all-start.5 = ((bf16[256,1,2,128]{3,2,1,0:T(2,128)(2,1)}), bf16[256,1,2,128]{3,2,1,0:T(2,128)(2,1)S(1)}, u32[]{:S(2)}, u32[]{:S(2)}) async-start(bf16[256,1,2,128]{3,2,1,0:T(2,128)(2,1)} %bitcast.14), calls=%async_computation.5 | async-start | bytes 262144 | tf_op jit(solution)/shard_map/all_to_all | solution.py:473
  126.5 0.0 copy-done.7
  126.5 0.0 copy-start.4
  126.5 0.0 copy-start.5
  126.5 0.0 copy-start.6
  126.5 0.8 shard_map.100
  127.3 0.1 copy-done.4
  127.4 0.1 copy-done.5
  127.5 0.0 copy-done.6
  127.5 1.1 shard_map.104
  128.6 10.6 %all-to-all-done.5 = bf16[256,1,2,128]{3,2,1,0:T(2,128)(2,1)S(1)} async-done(((bf16[256,1,2,128]{3,2,1,0:T(2,128)(2,1)}), bf16[256,1,2,128]{3,2,1,0:T(2,128)(2,1)S(1)}, u32[]{:S(2)}, u32[]{:S(2)}) %all-to-all-start.5) | async-done | bytes 131104 | tf_op jit(solution)/shard_map/all_to_all | solution.py:473
  139.2 0.8 shard_map.106
Async XLA Ops:
  3.2 29.9 %all-to-all-start = ((bf16[128,5,2,128]{3,2,1,0:T(2,128)(2,1)}), bf16[128,5,2,128]{3,2,1,0:T(2,128)(2,1)S(1)}, u32[]{:S(2)}, u32[]{:S(2)}) async-start(bf16[128,5,2,128]{3,2,1,0:T(2,128)(2,1)} %bitcast.33), calls=%async_computation | async-start | bytes 655360 | tf_op jit(solution)/shard_map/all_to_all | solution.py:473
  33.1 3.9 %collective-permute-start = (bf16[1280,128]{1,0:T(8,128)(2,1)S(1)}, bf16[1280,128]{1,0:T(8,128)(2,1)S(1)}, u32[]{:S(2)}, u32[]{:S(2)}) collective-permute-start(bf16[1280,128]{1,0:T(8,128)(2,1)S(1)} %bitcast.23), channel_id=1, source_target_pairs={{0,8},{8,0},{1,9},{9,1},{2,10},{10,2},{3,11},{11,3},{4,12},{12,4},... | collective-permute-start | bytes 983048 | tf_op jit(solution)/shard_map/ppermute | solution.py:477
  36.2 19.5 %copy-start.1 = (bf16[128,768]{1,0:T(8,128)(2,1)S(1)}, bf16[128,768]{1,0:T(8,128)(2,1)}, u32[]{:S(2)}) copy-start(bf16[128,768]{1,0:T(8,128)(2,1)} %get-tuple-element.36.normed_ref) | copy-start | bytes 589828
  36.2 19.5 %copy-start.2 = (f32[128,1024]{1,0:T(8,128)S(1)}, f32[128,1024]{1,0:T(8,128)}, u32[]{:S(2)}) copy-start(f32[128,1024]{1,0:T(8,128)} %get-tuple-element.37.back_norm_ref) | copy-start | bytes 1572868
  36.3 19.5 %copy-start.3 = (f32[128,768]{1,0:T(8,128)S(1)}, f32[128,768]{1,0:T(8,128)}, u32[]{:S(2)}) copy-start(f32[128,768]{1,0:T(8,128)} %get-tuple-element.38.gate_coef_ref) | copy-start | bytes 1179652
  74.1 4.2 %collective-permute-start.1 = (bf16[768,128]{1,0:T(8,128)(2,1)S(1)}, bf16[768,128]{1,0:T(8,128)(2,1)S(1)}, u32[]{:S(2)}, u32[]{:S(2)}) collective-permute-start(bf16[768,128]{1,0:T(8,128)(2,1)S(1)} %bitcast.25), channel_id=1, source_target_pairs={{0,8},{8,0},{1,9},{9,1},{2,10},{10,2},{3,11},{11,3},{4,12},{12,4},... | collective-permute-start | bytes 589832 | tf_op jit(solution)/shard_map/ppermute | solution.py:477
  77.8 21.4 %copy-start = (f32[512,768]{1,0:T(8,128)S(1)}, f32[512,768]{1,0:T(8,128)}, u32[]{:S(2)}) copy-start(f32[512,768]{1,0:T(8,128)} %get-tuple-element.46.coef_ref) | copy-start | bytes 4718596
  99.2 27.3 %copy-start.7 = (f32[128,768]{1,0:T(8,128)S(1)}, f32[128,768]{1,0:T(8,128)}, u32[]{:S(2)}) copy-start(f32[128,768]{1,0:T(8,128)} %get-tuple-element.28.gate_mask_ref) | copy-start | bytes 1179652
  120.4 18.8 %all-to-all-start.5 = ((bf16[256,1,2,128]{3,2,1,0:T(2,128)(2,1)}), bf16[256,1,2,128]{3,2,1,0:T(2,128)(2,1)S(1)}, u32[]{:S(2)}, u32[]{:S(2)}) async-start(bf16[256,1,2,128]{3,2,1,0:T(2,128)(2,1)} %bitcast.14), calls=%async_computation.5 | async-start | bytes 262144 | tf_op jit(solution)/shard_map/all_to_all | solution.py:473
  126.5 0.9 copy-start.4
  126.5 1.0 copy-start.5
  126.5 1.0 copy-start.6

commit v7 on v6

--- a/solution.py
+++ b/solution.py
@@ -11,8 +11,8 @@
 EPSILON = 1e-05
 BF16 = jnp.bfloat16
 F32 = jnp.float32
-ALL_AXES = ("chip", "core", "col")
-CHANNEL_AXES = ("col", "chip")
+ALL_AXES = ("zh", "x", "col", "core")
+CHANNEL_AXES = ("x", "zh", "col")
 LANES = 128
 SLOT = 64
 PIECE = 16
@@ -60,7 +60,7 @@
 def masks(valid_ref, na, nb):
     lane = lax.broadcasted_iota(jnp.int32, (1, LANES), 1)
     place = lane % SLOT
-    first_row = (2 * lax.axis_index("chip") + lax.axis_index("core")) * na
+    first_row = lax.axis_index(("x", "zh", "core")) * na
     first_col = lax.axis_index("col") * nb
     cols = jnp.zeros((1, LANES), jnp.int32)
     for b in range(nb):
@@ -129,7 +129,7 @@
 
 
 def group_rows(depth, lo, col, row):
-    return pl.ds(depth * (16 * col + lo) + row, 8, stride=2 * depth)
+    return pl.ds(depth * (64 * lo + col) + row, 8, stride=8 * depth)
 
 
 def plane_rows(na, lo, t):
@@ -159,7 +159,9 @@
     core = core + theirs * (1 - 2 * core)
     lo = (place >= na).astype(jnp.int32)
     a = place - na * lo
-    return (token == SLOT * (row % 8) + na * (2 * lo + core) + a).astype(F32).astype(BF16)
+    hi = row % 8
+    found = SLOT * (4 * lo + hi // 2) + na * (2 * (hi % 2) + core) + a
+    return (token == found).astype(F32).astype(BF16)
 
 
 def sides_kernel(
@@ -414,13 +416,8 @@
                 back_proj_ref[rows, at] = (upstreams[tiles * side + t] * coef_ref[rows, at]).astype(BF16)
     term = matmul(normed_ref[...], back_proj_ref[0 : 4 * hidden, :], NT)
     for t in range(4):
-        for m in range(hidden // 8):
-            term_chunk_ref[weight_rows(m, t), :] = term[8 * m : 8 * m + 8, t * LANES : (t + 1) * LANES]
+        put_device_rows(term_chunk_ref, 4, t, term[:, t * LANES : (t + 1) * LANES])
     term_ref[...] = term_chunk_ref[...].astype(BF16)
-
-
-def weight_rows(chip, t):
-    return pl.ds(2 * (16 * chip + 8 * (t // 2)) + t % 2, 8, stride=2)
 
 
 def sum_kernel(full_len, parts_ref, out_ref):
@@ -439,8 +436,7 @@
 def grad_weight_kernel(sums_ref, gate_total_ref, out_ref, chunk_ref):
     chunk_ref[...] = sums_ref[...].astype(F32)
     for t in range(4):
-        for m in range(out_ref.shape[0] // 8):
-            out_ref[8 * m : 8 * m + 8, t * LANES : (t + 1) * LANES] = chunk_ref[weight_rows(m, t), :]
+        out_ref[:, t * LANES : (t + 1) * LANES] = device_rows(chunk_ref, 4, t)
     out_ref[:, 4 * LANES :] = gate_total_ref[...]
 
 
@@ -620,8 +616,8 @@
 
 def solution(mesh):
     rows, cols = mesh.devices.shape
-    split = Mesh(mesh.devices.reshape(rows // 2, 2, cols), ("chip", "core", "col"))
-    pairs = P(("chip", "core"), "col", None)
+    split = Mesh(mesh.devices.reshape(rows // 8, 4, 2, cols), ("x", "zh", "core", "col"))
+    pairs = P(("x", "zh", "core"), "col", None)
     return jax.shard_map(
         per_device,
         mesh=split,

time: 140 us -> 141 us (level)
  no operation moved by 1% of the time
where the time goes in v7:
time: 141 us
  blocking collectives  75.9 us (54%)
  starting transfers between devices  28.3 us (20%)
  waiting for transfers between devices  21.9 us (16%)
  Pallas kernels  13.8 us (10%)
    all_to_all x4, blocking collectives, exchange(): return lax.all_to_all(split, axes, 0, 0, tiled=True).reshape(chunks.shape)  75.9 us
    all_to_all x2, starting transfers between devices, exchange(): return lax.all_to_all(split, axes, 0, 0, tiled=True).reshape(chunks.shape)  22.1 us
    all_to_all x2, waiting for transfers between devices, exchange(): return lax.all_to_all(split, axes, 0, 0, tiled=True).reshape(chunks.shape)  20.7 us
    ppermute x2, starting transfers between devices, other_core(): return lax.ppermute(values, 'core', [(0, 1), (1, 0)])  6.26 us
    pallas_call x1, Pallas kernels, per_device(): local_call(ready_kernel, (array((channels, lanes)), array((hidden, lanes...  3.51 us
  transfers between devices with their start and end apart: 4, of which 4 were waited for; matrix products, arithmetic and copies ran while one was open for 0% of the time, Pallas kernels for 5%

profile of v7, /device:TPU:1, one launch (start us, length us, event | category | flops | bytes accessed | tf_op | source)
XLA Modules:
  0.0 140.8 jit_solution(18358123482298615654)
XLA Ops:
  0.6 2.6 %shard_map.94 = (bf16[1280,128]{1,0:T(8,128)(2,1)}, f32[1,768]{1,0:T(1,128)}) custom-call(s32[384]{0:T(512)} %valid_hbm.1, bf16[12,48,128]{2,1,0:T(8,128)(2,1)} %acts_ref.1, f32[1,128]{1,0:T(1,128)} %bitcast.30, bf16[128,640]{1,0:T(8,128)(2,1)} %weight_ref.1), custom_call_target="tpu_custom_call" | custom-call | flops 100000000 | bytes 2000000 | tf_op jit(solution)/shard_map/pallas_call | solution.py:494
  3.2 16.3 %all-to-all-start = ((bf16[128,5,2,128]{3,2,1,0:T(2,128)(2,1)}), bf16[128,5,2,128]{3,2,1,0:T(2,128)(2,1)S(1)}, u32[]{:S(2)}, u32[]{:S(2)}) async-start(bf16[128,5,2,128]{3,2,1,0:T(2,128)(2,1)} %bitcast.33), calls=%async_computation | async-start | bytes 655360 | tf_op jit(solution)/shard_map/all_to_all | solution.py:469
  19.5 0.2 shard_map.96.order_ref
  19.7 3.5 %shard_map.95 = (bf16[128,768]{1,0:T(8,128)(2,1)}, f32[128,1024]{1,0:T(8,128)}, f32[128,768]{1,0:T(8,128)}, f32[128,768]{1,0:T(8,128)}, f32[512,768]{1,0:T(8,128)}) custom-call(bf16[12,48,128]{2,1,0:T(8,128)(2,1)} %acts_ref.1, f32[1,128]{1,0:T(1,128)} %bitcast.31, bf16[128,640]{1,0:T(8,128)(2,1)} %weight_ref.1, bf16[12,48,128]{2,1,0:T(8,128)(2,1)} %cotangent_hbm.1, ...), custom_call_target="tpu_custom_call" | custom-call | flops 1000000000 | bytes 2000000 | tf_op jit(solution)/shard_map/pallas_call | solution.py:514
  23.3 10.0 %all-to-all-done = bf16[128,5,2,128]{3,2,1,0:T(2,128)(2,1)S(1)} async-done(((bf16[128,5,2,128]{3,2,1,0:T(2,128)(2,1)}), bf16[128,5,2,128]{3,2,1,0:T(2,128)(2,1)S(1)}, u32[]{:S(2)}, u32[]{:S(2)}) %all-to-all-start) | async-done | bytes 327712 | tf_op jit(solution)/shard_map/all_to_all | solution.py:469
  33.2 3.1 %collective-permute-start = (bf16[1280,128]{1,0:T(8,128)(2,1)S(1)}, bf16[1280,128]{1,0:T(8,128)(2,1)S(1)}, u32[]{:S(2)}, u32[]{:S(2)}) collective-permute-start(bf16[1280,128]{1,0:T(8,128)(2,1)S(1)} %bitcast.23), channel_id=1, source_target_pairs={{0,8},{8,0},{1,9},{9,1},{2,10},{10,2},{3,11},{11,3},{4,12},{12,4},... | collective-permute-start | bytes 983048 | tf_op jit(solution)/shard_map/ppermute | solution.py:473
  36.3 0.5 shard_map.97
  36.8 0.0 copy-start.1
  36.8 0.0 copy-start.2
  36.9 0.0 copy-start.3
  36.9 0.7 collective-permute-done.theirs_ref
  37.6 0.9 shard_map.98
  38.5 17.4 %all_to_all.30 = bf16[128,3,2,128]{3,2,1,0:T(2,128)(2,1)S(1)} all-to-all(bf16[128,3,2,128]{3,2,1,0:T(2,128)(2,1)S(1)} %bitcast.27), channel_id=1, replica_groups=mesh['x'=4,'zh'=4,'core'=2,'col'=8] {'x','zh','col'}, dimensions={0} | all-to-all | bytes 393216 | tf_op jit(solution)/shard_map/all_to_all | solution.py:469
  55.9 0.0 copy-done.1
  55.9 0.0 copy-done.2
  55.9 0.0 copy-done.3
  55.9 0.6 shard_map.99
  56.5 18.2 %all_to_all.31 = bf16[128,3,2,128]{3,2,1,0:T(2,128)(2,1)S(1)} all-to-all(bf16[128,3,2,128]{3,2,1,0:T(2,128)(2,1)S(1)} %bitcast.28), channel_id=1, replica_groups=mesh['x'=4,'zh'=4,'core'=2,'col'=8] {'x','zh','col'}, dimensions={0} | all-to-all | bytes 393216 | tf_op jit(solution)/shard_map/all_to_all | solution.py:469
  74.7 3.2 %collective-permute-start.1 = (bf16[768,128]{1,0:T(8,128)(2,1)S(1)}, bf16[768,128]{1,0:T(8,128)(2,1)S(1)}, u32[]{:S(2)}, u32[]{:S(2)}) collective-permute-start(bf16[768,128]{1,0:T(8,128)(2,1)S(1)} %bitcast.25), channel_id=1, source_target_pairs={{0,8},{8,0},{1,9},{9,1},{2,10},{10,2},{3,11},{11,3},{4,12},{12,4},... | collective-permute-start | bytes 589832 | tf_op jit(solution)/shard_map/ppermute | solution.py:473
  77.9 0.6 shard_map.101
  78.5 0.0 copy-start
  78.5 0.4 collective-permute-done.1.theirs_ref
  79.0 1.0 shard_map.102
  79.9 19.9 %all_to_all.32 = bf16[128,5,2,128]{3,2,1,0:T(2,128)(2,1)S(1)} all-to-all(bf16[128,5,2,128]{3,2,1,0:T(2,128)(2,1)S(1)} %bitcast.19), channel_id=1, replica_groups=mesh['x'=4,'zh'=4,'core'=2,'col'=8] {'x','zh','col'}, dimensions={0} | all-to-all | bytes 655360 | tf_op jit(solution)/shard_map/all_to_all | solution.py:469
  99.9 0.0 copy-start.7
  99.9 0.0 copy-done
  99.9 0.5 shard_map.103
  100.4 20.3 %all_to_all.33 = bf16[256,1,2,128]{3,2,1,0:T(2,128)(2,1)S(1)} all-to-all(bf16[256,1,2,128]{3,2,1,0:T(2,128)(2,1)S(1)} %bitcast.29), channel_id=1, replica_groups=mesh['x'=4,'zh'=4,'core'=2,'col'=8] {'zh','x','col','core'}, dimensions={0} | all-to-all | bytes 262144 | tf_op jit(solution)/shard_map/all_to_all | solution.py:469
  120.7 0.7 shard_map.105
  121.4 5.7 %all-to-all-start.5 = ((bf16[256,1,2,128]{3,2,1,0:T(2,128)(2,1)}), bf16[256,1,2,128]{3,2,1,0:T(2,128)(2,1)S(1)}, u32[]{:S(2)}, u32[]{:S(2)}) async-start(bf16[256,1,2,128]{3,2,1,0:T(2,128)(2,1)} %bitcast.14), calls=%async_computation.5 | async-start | bytes 262144 | tf_op jit(solution)/shard_map/all_to_all | solution.py:469
  127.1 0.0 copy-done.7
  127.1 0.0 copy-start.4
  127.2 0.0 copy-start.5
  127.2 0.0 copy-start.6
  127.2 0.8 shard_map.100
  128.0 0.1 copy-done.4
  128.1 0.1 copy-done.5
  128.1 0.0 copy-done.6
  128.1 1.1 shard_map.104
  129.3 10.8 %all-to-all-done.5 = bf16[256,1,2,128]{3,2,1,0:T(2,128)(2,1)S(1)} async-done(((bf16[256,1,2,128]{3,2,1,0:T(2,128)(2,1)}), bf16[256,1,2,128]{3,2,1,0:T(2,128)(2,1)S(1)}, u32[]{:S(2)}, u32[]{:S(2)}) %all-to-all-start.5) | async-done | bytes 131104 | tf_op jit(solution)/shard_map/all_to_all | solution.py:469
  140.1 0.8 shard_map.106
Async XLA Ops:
  3.2 30.0 %all-to-all-start = ((bf16[128,5,2,128]{3,2,1,0:T(2,128)(2,1)}), bf16[128,5,2,128]{3,2,1,0:T(2,128)(2,1)S(1)}, u32[]{:S(2)}, u32[]{:S(2)}) async-start(bf16[128,5,2,128]{3,2,1,0:T(2,128)(2,1)} %bitcast.33), calls=%async_computation | async-start | bytes 655360 | tf_op jit(solution)/shard_map/all_to_all | solution.py:469
  33.2 4.4 %collective-permute-start = (bf16[1280,128]{1,0:T(8,128)(2,1)S(1)}, bf16[1280,128]{1,0:T(8,128)(2,1)S(1)}, u32[]{:S(2)}, u32[]{:S(2)}) collective-permute-start(bf16[1280,128]{1,0:T(8,128)(2,1)S(1)} %bitcast.23), channel_id=1, source_target_pairs={{0,8},{8,0},{1,9},{9,1},{2,10},{10,2},{3,11},{11,3},{4,12},{12,4},... | collective-permute-start | bytes 983048 | tf_op jit(solution)/shard_map/ppermute | solution.py:473
  36.8 19.1 %copy-start.1 = (bf16[128,768]{1,0:T(8,128)(2,1)S(1)}, bf16[128,768]{1,0:T(8,128)(2,1)}, u32[]{:S(2)}) copy-start(bf16[128,768]{1,0:T(8,128)(2,1)} %get-tuple-element.36.normed_ref) | copy-start | bytes 589828
  36.8 19.1 %copy-start.2 = (f32[128,1024]{1,0:T(8,128)S(1)}, f32[128,1024]{1,0:T(8,128)}, u32[]{:S(2)}) copy-start(f32[128,1024]{1,0:T(8,128)} %get-tuple-element.37.back_norm_ref) | copy-start | bytes 1572868
  36.9 19.0 %copy-start.3 = (f32[128,768]{1,0:T(8,128)S(1)}, f32[128,768]{1,0:T(8,128)}, u32[]{:S(2)}) copy-start(f32[128,768]{1,0:T(8,128)} %get-tuple-element.38.gate_coef_ref) | copy-start | bytes 1179652
  74.7 4.2 %collective-permute-start.1 = (bf16[768,128]{1,0:T(8,128)(2,1)S(1)}, bf16[768,128]{1,0:T(8,128)(2,1)S(1)}, u32[]{:S(2)}, u32[]{:S(2)}) collective-permute-start(bf16[768,128]{1,0:T(8,128)(2,1)S(1)} %bitcast.25), channel_id=1, source_target_pairs={{0,8},{8,0},{1,9},{9,1},{2,10},{10,2},{3,11},{11,3},{4,12},{12,4},... | collective-permute-start | bytes 589832 | tf_op jit(solution)/shard_map/ppermute | solution.py:473
  78.5 21.4 %copy-start = (f32[512,768]{1,0:T(8,128)S(1)}, f32[512,768]{1,0:T(8,128)}, u32[]{:S(2)}) copy-start(f32[512,768]{1,0:T(8,128)} %get-tuple-element.46.coef_ref) | copy-start | bytes 4718596
  99.9 27.3 %copy-start.7 = (f32[128,768]{1,0:T(8,128)S(1)}, f32[128,768]{1,0:T(8,128)}, u32[]{:S(2)}) copy-start(f32[128,768]{1,0:T(8,128)} %get-tuple-element.28.gate_mask_ref) | copy-start | bytes 1179652
  121.4 18.7 %all-to-all-start.5 = ((bf16[256,1,2,128]{3,2,1,0:T(2,128)(2,1)}), bf16[256,1,2,128]{3,2,1,0:T(2,128)(2,1)S(1)}, u32[]{:S(2)}, u32[]{:S(2)}) async-start(bf16[256,1,2,128]{3,2,1,0:T(2,128)(2,1)} %bitcast.14), calls=%async_computation.5 | async-start | bytes 262144 | tf_op jit(solution)/shard_map/all_to_all | solution.py:469
  127.1 0.9 copy-start.4
  127.2 1.0 copy-start.5
  127.2 1.0 copy-start.6

commit v8 on v6

--- a/solution.py
+++ b/solution.py
@@ -254,39 +254,52 @@
     order_ref[...] = token_order(na, order_ref.shape[1])
 
 
-def side_planes(na, chunk_ref, left_ref, right_ref, first):
+def side_rows(chunk_ref, lo, pair):
+    return [
+        unpack_tiles([chunk_ref[group_rows(SIDE_ROWS, lo, col, t), :] for t in range(9)])
+        for col in (2 * pair, 2 * pair + 1)
+    ]
+
+
+def side_plane(na, chunk_ref, sides):
     tiles = na // 2
     for pair in range(4):
         at = slice(pair * LANES, (pair + 1) * LANES)
         for lo in range(2):
-            even, odd = [
-                unpack_tiles([chunk_ref[group_rows(SIDE_ROWS, lo, col, t), :] for t in range(9)])
-                for col in (2 * pair, 2 * pair + 1)
-            ]
-            for t in range(tiles):
-                rows = plane_rows(na, lo, t)
-                rows = slice(first + rows.start, first + rows.stop)
-                left_ref[rows, at] = plane_tile(even[t], odd[t]).astype(BF16)
-                right_ref[rows, at] = plane_tile(even[tiles + t], odd[tiles + t]).astype(BF16)
-
-
-def own_sides_kernel(na, mine_ref, left_ref, right_ref, chunk_ref):
+            even, odd = side_rows(chunk_ref, lo, pair)
+            for side, plane_ref in sides.items():
+                for t in range(tiles):
+                    tile = plane_tile(even[side * tiles + t], odd[side * tiles + t])
+                    plane_ref[plane_rows(na, lo, t), at] = tile.astype(BF16)
+
+
+def token_sums(left_ref, right_ref, order_ref, rows):
+    tri = matmul(left_ref[...], right_ref[...], NT).astype(BF16)
+    return matmul(tri, order_ref[rows, :])
+
+
+def own_sides_kernel(na, mine_ref, order_ref, left_ref, right_ref, tri_ref, chunk_ref):
     chunk_ref[...] = mine_ref[...].astype(F32)
-    side_planes(na, chunk_ref, left_ref, right_ref, 0)
+    side_plane(na, chunk_ref, {0: left_ref, 1: right_ref})
+    tri_ref[...] = token_sums(left_ref, right_ref, order_ref, slice(0, left_ref.shape[0]))
+
+
+def left_kernel(na, theirs_ref, left_ref, chunk_ref):
+    chunk_ref[...] = theirs_ref[...].astype(F32)
+    side_plane(na, chunk_ref, {0: left_ref})
 
 
 def tri_kernel(
-    na, theirs_ref, left_mine_ref, right_mine_ref, order_ref, tri_ref, left_ref, right_ref,
+    na, theirs_ref, left_ref, right_mine_ref, tri_mine_ref, order_ref, tri_ref, right_ref,
     chunk_ref, tri_chunk_ref,
 ):
     tiles = na // 2
-    half = left_mine_ref.shape[0]
+    half = left_ref.shape[0]
     chunk_ref[...] = theirs_ref[...].astype(F32)
-    left_ref[0:half, :] = left_mine_ref[...]
     right_ref[0:half, :] = right_mine_ref[...]
-    side_planes(na, chunk_ref, left_ref, right_ref, half)
-    tri = matmul(left_mine_ref[...], right_ref[...], NT).astype(BF16)
-    tri = matmul(tri, order_ref[...])
+    theirs = right_ref.at[half : 2 * half]
+    side_plane(na, chunk_ref, {1: theirs})
+    tri = tri_mine_ref[...] + token_sums(left_ref, theirs, order_ref, slice(half, 2 * half))
     for pair in range(4):
         for lo in range(2):
             for t in range(tiles):
@@ -362,26 +375,28 @@
 
 
 def own_back_kernel(
-    na, mine_ref, right_ref, order_ref, turned_ref, back_left_ref, total_ref, chunk_ref, plane_ref
+    na, mine_ref, left_ref, right_ref, order_ref, back_left_ref, back_right_ref, total_ref,
+    chunk_ref, plane_ref, turned_ref,
 ):
+    half = left_ref.shape[0]
     chunk_ref[...] = mine_ref[...].astype(F32)
     back_plane(na, chunk_ref, plane_ref)
     turned_ref[...] = matmul(plane_ref[...], order_ref[...], NT).astype(BF16)
     back_left_ref[...] = matmul(turned_ref[...], right_ref[...])
+    back_right_ref[...] = matmul(turned_ref[:, 0:half], left_ref[...], TN)
     total_ref[...] = gap_total(chunk_ref)
 
 
 def back_kernel(
-    na, theirs_ref, turned_mine_ref, back_left_ref, total_ref, left_ref, order_ref, out_ref,
+    na, theirs_ref, back_left_ref, back_right_ref, total_ref, left_ref, order_ref, out_ref,
     back_chunk_ref, chunk_ref, plane_ref, turned_ref,
 ):
     tiles = na // 2
-    half = turned_mine_ref.shape[0]
+    half = left_ref.shape[0]
     back_chunk_ref[...] = theirs_ref[...].astype(F32)
     back_plane(na, back_chunk_ref, plane_ref)
-    turned_ref[0:half, :] = turned_mine_ref[...]
-    turned_ref[half:, :] = matmul(plane_ref[...], order_ref[...], NT).astype(BF16)
-    back_right = matmul(turned_ref[:, 0:half], left_ref[...], TN)
+    turned_ref[...] = matmul(plane_ref[...], order_ref[0:half, :], NT).astype(BF16)
+    back_right = back_right_ref[...] + matmul(turned_ref[...], left_ref[...], TN)
     total = (total_ref[...] + gap_total(back_chunk_ref)) / (4 * 8 * na)
     for m in range(chunk_ref.shape[0] // (8 * SIDE_ROWS)):
         chunk_ref[pl.ds(8 * SIDE_ROWS * m + 9, 8, stride=SIDE_ROWS), :] = total
@@ -544,20 +559,20 @@
     mine, normed, order = lax.optimization_barrier((mine, normed, order))
     half_plane = (full_len // 2, plane[1])
     theirs = other_core(mine)
-    left_mine, right_mine = local_call(
+    left_mine, right_mine, tri_mine = local_call(
         functools.partial(own_sides_kernel, na),
-        (array(half_plane), array(half_plane)),
+        (array(half_plane), array(half_plane), array(half_plane, F32)),
         [pltpu.VMEM(sides_chunk, F32)],
         1_000_000_000,
-        1,
-    )(mine)
-    tri, left, right = local_call(
+        2,
+    )(mine, order)
+    tri, right = local_call(
         functools.partial(tri_kernel, na),
-        (array(tri_chunk), array(plane), array(plane)),
+        (array(tri_chunk), array(plane)),
         [pltpu.VMEM(sides_chunk, F32), pltpu.VMEM(tri_chunk, F32)],
         300_000_000,
-        4,
-    )(theirs, left_mine, right_mine, order)
+        5,
+    )(theirs, left_mine, right_mine, tri_mine, order)
     tri = exchange(tri, TRI_ROWS, CHANNEL_AXES)
     back, gate, out_proj = local_call(
         middle_kernel,
@@ -571,17 +586,29 @@
         4,
     )(tri, normed, back_norm, gate_coef)
     back = exchange(back, TRI_ROWS, CHANNEL_AXES)
+    side_theirs, back = lax.optimization_barrier((theirs, back))
     update = local_call(update_kernel, array(pair_acts.shape), [], 1_000_000_000, 2)(
         gate_mask, out_proj
     )
     theirs = other_core(back)
-    turned, back_left, total = local_call(
+    left_theirs = local_call(
+        functools.partial(left_kernel, na),
+        array(half_plane),
+        [pltpu.VMEM(sides_chunk, F32)],
+        1_000_000_000,
+        1,
+    )(side_theirs)
+    back_left, back_right, total = local_call(
         functools.partial(own_back_kernel, na),
-        (array((full_len // 2, full_len)), array(half_plane, F32), array((8, LANES), F32)),
-        [pltpu.VMEM(tri_chunk, F32), pltpu.VMEM(half_plane, BF16)],
+        (array(half_plane, F32), array(half_plane, F32), array((8, LANES), F32)),
+        [
+            pltpu.VMEM(tri_chunk, F32),
+            pltpu.VMEM(half_plane, BF16),
+            pltpu.VMEM((full_len // 2, full_len), BF16),
+        ],
         1_000_000_000,
-        3,
-    )(back, right, order)
+        4,
+    )(back, left_mine, right, order)
     back_sides = local_call(
         functools.partial(back_kernel, na),
         array(sides_chunk),
@@ -589,11 +616,11 @@
             pltpu.VMEM(tri_chunk, F32),
             pltpu.VMEM(sides_chunk, F32),
             pltpu.VMEM(half_plane, BF16),
-            pltpu.VMEM((full_len, full_len), BF16),
+            pltpu.VMEM((full_len // 2, full_len // 2), BF16),
         ],
         300_000_000,
         6,
-    )(theirs, turned, back_left, total, left, order)
+    )(theirs, back_left, back_right, total, left_theirs, order)
     back_sides = exchange(back_sides, SIDE_ROWS, CHANNEL_AXES)
     term, back_proj, gate_total = local_call(
         weight_kernel,

time: 140 us -> 140 us (level)
  no operation moved by 1% of the time
where the time goes in v8:
time: 140 us
  blocking collectives  75.6 us (54%)
  starting transfers between devices  28.1 us (20%)
  waiting for transfers between devices  21.3 us (15%)
  Pallas kernels  13.8 us (10%)
    all_to_all x4, blocking collectives, exchange(): return lax.all_to_all(split, axes, 0, 0, tiled=True).reshape(chunks.shape)  75.6 us
    all_to_all x2, starting transfers between devices, exchange(): return lax.all_to_all(split, axes, 0, 0, tiled=True).reshape(chunks.shape)  22.4 us
    all_to_all x2, waiting for transfers between devices, exchange(): return lax.all_to_all(split, axes, 0, 0, tiled=True).reshape(chunks.shape)  20.5 us
    ppermute x2, starting transfers between devices, other_core(): return lax.ppermute(values, 'core', [(0, 1), (1, 0)])  5.73 us
    pallas_call x1, Pallas kernels, per_device(): local_call(ready_kernel, (array((channels, lanes)), array((hidden, lanes...  3.51 us
  transfers between devices with their start and end apart: 4, of which 4 were waited for; matrix products, arithmetic and copies ran while one was open for 0% of the time, Pallas kernels for 5%

profile of v8, /device:TPU:1, one launch (start us, length us, event | category | flops | bytes accessed | tf_op | source)
XLA Modules:
  0.0 139.9 jit_solution(17511957389211795027)
XLA Ops:
  0.6 2.6 %shard_map.94 = (bf16[1280,128]{1,0:T(8,128)(2,1)}, f32[1,768]{1,0:T(1,128)}) custom-call(s32[384]{0:T(512)} %valid_hbm.1, bf16[12,48,128]{2,1,0:T(8,128)(2,1)} %acts_ref.1, f32[1,128]{1,0:T(1,128)} %bitcast.30, bf16[128,640]{1,0:T(8,128)(2,1)} %weight_ref.1), custom_call_target="tpu_custom_call" | custom-call | flops 100000000 | bytes 2000000 | tf_op jit(solution)/shard_map/pallas_call | solution.py:513
  3.2 16.3 %all-to-all-start = ((bf16[128,5,2,128]{3,2,1,0:T(2,128)(2,1)}), bf16[128,5,2,128]{3,2,1,0:T(2,128)(2,1)S(1)}, u32[]{:S(2)}, u32[]{:S(2)}) async-start(bf16[128,5,2,128]{3,2,1,0:T(2,128)(2,1)} %bitcast.33), calls=%async_computation | async-start | bytes 655360 | tf_op jit(solution)/shard_map/all_to_all | solution.py:488
  19.5 0.1 shard_map.96.order_ref
  19.7 3.5 %shard_map.95 = (bf16[128,768]{1,0:T(8,128)(2,1)}, f32[128,1024]{1,0:T(8,128)}, f32[128,768]{1,0:T(8,128)}, f32[128,768]{1,0:T(8,128)}, f32[512,768]{1,0:T(8,128)}) custom-call(bf16[12,48,128]{2,1,0:T(8,128)(2,1)} %acts_ref.1, f32[1,128]{1,0:T(1,128)} %bitcast.31, bf16[128,640]{1,0:T(8,128)(2,1)} %weight_ref.1, bf16[12,48,128]{2,1,0:T(8,128)(2,1)} %cotangent_hbm.1, ...), custom_call_target="tpu_custom_call" | custom-call | flops 1000000000 | bytes 2000000 | tf_op jit(solution)/shard_map/pallas_call | solution.py:533
  23.2 9.9 %all-to-all-done = bf16[128,5,2,128]{3,2,1,0:T(2,128)(2,1)S(1)} async-done(((bf16[128,5,2,128]{3,2,1,0:T(2,128)(2,1)}), bf16[128,5,2,128]{3,2,1,0:T(2,128)(2,1)S(1)}, u32[]{:S(2)}, u32[]{:S(2)}) %all-to-all-start) | async-done | bytes 327712 | tf_op jit(solution)/shard_map/all_to_all | solution.py:488
  33.1 2.6 %collective-permute-start = (bf16[1280,128]{1,0:T(8,128)(2,1)S(1)}, bf16[1280,128]{1,0:T(8,128)(2,1)S(1)}, u32[]{:S(2)}, u32[]{:S(2)}) collective-permute-start(bf16[1280,128]{1,0:T(8,128)(2,1)S(1)} %bitcast.23), channel_id=1, source_target_pairs={{0,8},{8,0},{1,9},{9,1},{2,10},{10,2},{3,11},{11,3},{4,12},{12,4},... | collective-permute-start | bytes 983048 | tf_op jit(solution)/shard_map/ppermute | solution.py:492
  35.7 0.7 shard_map.97
  36.4 0.0 copy-start.1
  36.4 0.0 copy-start.2
  36.4 0.0 copy-start.3
  36.5 0.5 collective-permute-done.theirs_ref
  37.0 0.7 shard_map.98
  37.8 17.9 %all_to_all.30 = bf16[128,3,2,128]{3,2,1,0:T(2,128)(2,1)S(1)} all-to-all(bf16[128,3,2,128]{3,2,1,0:T(2,128)(2,1)S(1)} %bitcast.28), channel_id=1, replica_groups=mesh['chip'=16,'core'=2,'col'=8] {'col','chip'}, dimensions={0} | all-to-all | bytes 393216 | tf_op jit(solution)/shard_map/all_to_all | solution.py:488
  55.6 0.0 copy-done.1
  55.6 0.0 copy-done.2
  55.6 0.0 copy-done.3
  55.6 0.6 shard_map.99
  56.3 17.8 %all_to_all.31 = bf16[128,3,2,128]{3,2,1,0:T(2,128)(2,1)S(1)} all-to-all(bf16[128,3,2,128]{3,2,1,0:T(2,128)(2,1)S(1)} %bitcast.27), channel_id=1, replica_groups=mesh['chip'=16,'core'=2,'col'=8] {'col','chip'}, dimensions={0} | all-to-all | bytes 393216 | tf_op jit(solution)/shard_map/all_to_all | solution.py:488
  74.0 3.1 %collective-permute-start.1 = (bf16[768,128]{1,0:T(8,128)(2,1)S(1)}, bf16[768,128]{1,0:T(8,128)(2,1)S(1)}, u32[]{:S(2)}, u32[]{:S(2)}) collective-permute-start(bf16[768,128]{1,0:T(8,128)(2,1)S(1)} %bitcast.25), channel_id=1, source_target_pairs={{0,8},{8,0},{1,9},{9,1},{2,10},{10,2},{3,11},{11,3},{4,12},{12,4},... | collective-permute-start | bytes 589832 | tf_op jit(solution)/shard_map/ppermute | solution.py:492
  77.1 0.1 shard_map.102.left_ref
  77.3 0.6 shard_map.101
  77.9 0.0 copy-start
  77.9 0.3 collective-permute-done.1.theirs_ref
  78.2 0.9 shard_map.103
  79.1 20.0 %all_to_all.32 = bf16[128,5,2,128]{3,2,1,0:T(2,128)(2,1)S(1)} all-to-all(bf16[128,5,2,128]{3,2,1,0:T(2,128)(2,1)S(1)} %bitcast.19), channel_id=1, replica_groups=mesh['chip'=16,'core'=2,'col'=8] {'col','chip'}, dimensions={0} | all-to-all | bytes 655360 | tf_op jit(solution)/shard_map/all_to_all | solution.py:488
  99.1 0.0 copy-start.7
  99.1 0.0 copy-done
  99.1 0.5 shard_map.104
  99.6 20.0 %all_to_all.33 = bf16[256,1,2,128]{3,2,1,0:T(2,128)(2,1)S(1)} all-to-all(bf16[256,1,2,128]{3,2,1,0:T(2,128)(2,1)S(1)} %bitcast.29), channel_id=1, replica_groups=mesh['chip'=16,'core'=2,'col'=8] {'chip','core','col'}, dimensions={0} | all-to-all | bytes 262144 | tf_op jit(solution)/shard_map/all_to_all | solution.py:488
  119.6 0.7 shard_map.106
  120.3 6.1 %all-to-all-start.5 = ((bf16[256,1,2,128]{3,2,1,0:T(2,128)(2,1)}), bf16[256,1,2,128]{3,2,1,0:T(2,128)(2,1)S(1)}, u32[]{:S(2)}, u32[]{:S(2)}) async-start(bf16[256,1,2,128]{3,2,1,0:T(2,128)(2,1)} %bitcast.14), calls=%async_computation.5 | async-start | bytes 262144 | tf_op jit(solution)/shard_map/all_to_all | solution.py:488
  126.4 0.0 copy-done.7
  126.4 0.0 copy-start.4
  126.4 0.0 copy-start.5
  126.4 0.0 copy-start.6
  126.4 0.8 shard_map.100
  127.2 0.1 copy-done.4
  127.3 0.1 copy-done.5
  127.4 0.0 copy-done.6
  127.4 1.1 shard_map.105
  128.5 10.6 %all-to-all-done.5 = bf16[256,1,2,128]{3,2,1,0:T(2,128)(2,1)S(1)} async-done(((bf16[256,1,2,128]{3,2,1,0:T(2,128)(2,1)}), bf16[256,1,2,128]{3,2,1,0:T(2,128)(2,1)S(1)}, u32[]{:S(2)}, u32[]{:S(2)}) %all-to-all-start.5) | async-done | bytes 131104 | tf_op jit(solution)/shard_map/all_to_all | solution.py:488
  139.1 0.8 shard_map.107
Async XLA Ops:
  3.2 29.9 %all-to-all-start = ((bf16[128,5,2,128]{3,2,1,0:T(2,128)(2,1)}), bf16[128,5,2,128]{3,2,1,0:T(2,128)(2,1)S(1)}, u32[]{:S(2)}, u32[]{:S(2)}) async-start(bf16[128,5,2,128]{3,2,1,0:T(2,128)(2,1)} %bitcast.33), calls=%async_computation | async-start | bytes 655360 | tf_op jit(solution)/shard_map/all_to_all | solution.py:488
  33.1 3.9 %collective-permute-start = (bf16[1280,128]{1,0:T(8,128)(2,1)S(1)}, bf16[1280,128]{1,0:T(8,128)(2,1)S(1)}, u32[]{:S(2)}, u32[]{:S(2)}) collective-permute-start(bf16[1280,128]{1,0:T(8,128)(2,1)S(1)} %bitcast.23), channel_id=1, source_target_pairs={{0,8},{8,0},{1,9},{9,1},{2,10},{10,2},{3,11},{11,3},{4,12},{12,4},... | collective-permute-start | bytes 983048 | tf_op jit(solution)/shard_map/ppermute | solution.py:492
  36.4 19.2 %copy-start.1 = (bf16[128,768]{1,0:T(8,128)(2,1)S(1)}, bf16[128,768]{1,0:T(8,128)(2,1)}, u32[]{:S(2)}) copy-start(bf16[128,768]{1,0:T(8,128)(2,1)} %get-tuple-element.39.normed_ref) | copy-start | bytes 589828
  36.4 19.2 %copy-start.2 = (f32[128,1024]{1,0:T(8,128)S(1)}, f32[128,1024]{1,0:T(8,128)}, u32[]{:S(2)}) copy-start(f32[128,1024]{1,0:T(8,128)} %get-tuple-element.40.back_norm_ref) | copy-start | bytes 1572868
  36.4 19.2 %copy-start.3 = (f32[128,768]{1,0:T(8,128)S(1)}, f32[128,768]{1,0:T(8,128)}, u32[]{:S(2)}) copy-start(f32[128,768]{1,0:T(8,128)} %get-tuple-element.41.gate_coef_ref) | copy-start | bytes 1179652
  74.0 4.2 %collective-permute-start.1 = (bf16[768,128]{1,0:T(8,128)(2,1)S(1)}, bf16[768,128]{1,0:T(8,128)(2,1)S(1)}, u32[]{:S(2)}, u32[]{:S(2)}) collective-permute-start(bf16[768,128]{1,0:T(8,128)(2,1)S(1)} %bitcast.25), channel_id=1, source_target_pairs={{0,8},{8,0},{1,9},{9,1},{2,10},{10,2},{3,11},{11,3},{4,12},{12,4},... | collective-permute-start | bytes 589832 | tf_op jit(solution)/shard_map/ppermute | solution.py:492
  77.9 21.2 %copy-start = (f32[512,768]{1,0:T(8,128)S(1)}, f32[512,768]{1,0:T(8,128)}, u32[]{:S(2)}) copy-start(f32[512,768]{1,0:T(8,128)} %get-tuple-element.50.coef_ref) | copy-start | bytes 4718596
  99.1 27.3 %copy-start.7 = (f32[128,768]{1,0:T(8,128)S(1)}, f32[128,768]{1,0:T(8,128)}, u32[]{:S(2)}) copy-start(f32[128,768]{1,0:T(8,128)} %get-tuple-element.30.gate_mask_ref) | copy-start | bytes 1179652
  120.3 18.8 %all-to-all-start.5 = ((bf16[256,1,2,128]{3,2,1,0:T(2,128)(2,1)}), bf16[256,1,2,128]{3,2,1,0:T(2,128)(2,1)S(1)}, u32[]{:S(2)}, u32[]{:S(2)}) async-start(bf16[256,1,2,128]{3,2,1,0:T(2,128)(2,1)} %bitcast.14), calls=%async_computation.5 | async-start | bytes 262144 | tf_op jit(solution)/shard_map/all_to_all | solution.py:488
  126.4 0.9 copy-start.4
  126.4 1.0 copy-start.5
  126.4 1.0 copy-start.6

commit v9 on v8

--- a/solution.py
+++ b/solution.py
@@ -46,8 +46,8 @@
 def spread(pairs_ref, spread_ref):
     na, nb, channels = pairs_ref.shape
     for a in range(na):
-        spread_ref[a * SLOT : a * SLOT + nb, :] = pairs_ref[a].astype(F32)
-        spread_ref[a * SLOT + nb : (a + 1) * SLOT, :] = jnp.zeros((SLOT - nb, channels), F32)
+        spread_ref[a * SLOT : a * SLOT + nb, :] = pairs_ref[a]
+        spread_ref[a * SLOT + nb : (a + 1) * SLOT, :] = jnp.zeros((SLOT - nb, channels), BF16)
 
 
 def store_pairs(out_ref, t, values):
@@ -90,7 +90,7 @@
     tiles = spread_ref.shape[0] // LANES
     for t in range(tiles):
         at = slice(t * LANES, (t + 1) * LANES)
-        scaled, _ = tile_norm(spread_ref[at, :].T)
+        scaled, _ = tile_norm(spread_ref[at, :].T.astype(F32))
         normed_ref[:, at] = (scaled * gain).astype(BF16)
 
 
@@ -232,7 +232,7 @@
         mask = mask_ref[:, at]
         gate = jax.nn.sigmoid(projected[4 * hidden :, at])
         gate_mask = gate * mask
-        cotangent = spread_ref[at, :].T
+        cotangent = spread_ref[at, :].T.astype(F32)
         gate_mask_ref[:, at] = gate_mask
         gate_coef_ref[:, at] = cotangent * gate_mask * (1.0 - gate)
         back_out_ref[:, at] = (cotangent * gate_mask).astype(BF16)
@@ -466,7 +466,7 @@
     back_normed = matmul(weight_ref[...], back_proj_ref[...])
     for t in range(na // 2):
         at = slice(t * LANES, (t + 1) * LANES)
-        scaled, inv = tile_norm(spread_ref[at, :].T)
+        scaled, inv = tile_norm(spread_ref[at, :].T.astype(F32))
         store_pairs(grad_pair_ref, t, tile_norm_grad(back_normed[:, at] * gain, scaled, inv))
 
 
@@ -508,7 +508,7 @@
     term_chunk = (4 * hidden, LANES)
     gain = norm_gain.reshape(1, channels)
     out_gain = out_gain.reshape(1, hidden)
-    spread_scratch = pltpu.VMEM((lanes, channels), F32)
+    spread_scratch = pltpu.VMEM((lanes, channels), BF16)
 
     sides, mask = local_call(
         sides_kernel,

time: 140 us -> 140 us (level)
  no operation moved by 1% of the time
where the time goes in v9:
time: 140 us
  blocking collectives  75.6 us (54%)
  starting transfers between devices  28.1 us (20%)
  waiting for transfers between devices  21.4 us (15%)
  Pallas kernels  13.7 us (10%)
    all_to_all x4, blocking collectives, exchange(): return lax.all_to_all(split, axes, 0, 0, tiled=True).reshape(chunks.shape)  75.6 us
    all_to_all x2, starting transfers between devices, exchange(): return lax.all_to_all(split, axes, 0, 0, tiled=True).reshape(chunks.shape)  22.4 us
    all_to_all x2, waiting for transfers between devices, exchange(): return lax.all_to_all(split, axes, 0, 0, tiled=True).reshape(chunks.shape)  20.5 us
    ppermute x2, starting transfers between devices, other_core(): return lax.ppermute(values, 'core', [(0, 1), (1, 0)])  5.73 us
    pallas_call x1, Pallas kernels, per_device(): local_call(ready_kernel, (array((channels, lanes)), array((hidden, lanes...  3.46 us
  transfers between devices with their start and end apart: 4, of which 4 were waited for; matrix products, arithmetic and copies ran while one was open for 0% of the time, Pallas kernels for 5%

profile of v9, /device:TPU:1, one launch (start us, length us, event | category | flops | bytes accessed | tf_op | source)
XLA Modules:
  0.0 139.9 jit_solution(1888490104524659208)
XLA Ops:
  0.6 2.5 %shard_map.94 = (bf16[1280,128]{1,0:T(8,128)(2,1)}, f32[1,768]{1,0:T(1,128)}) custom-call(s32[384]{0:T(512)} %valid_hbm.1, bf16[12,48,128]{2,1,0:T(8,128)(2,1)} %acts_ref.1, f32[1,128]{1,0:T(1,128)} %bitcast.30, bf16[128,640]{1,0:T(8,128)(2,1)} %weight_ref.1), custom_call_target="tpu_custom_call" | custom-call | flops 100000000 | bytes 2000000 | tf_op jit(solution)/shard_map/pallas_call | solution.py:513
  3.1 16.3 %all-to-all-start = ((bf16[128,5,2,128]{3,2,1,0:T(2,128)(2,1)}), bf16[128,5,2,128]{3,2,1,0:T(2,128)(2,1)S(1)}, u32[]{:S(2)}, u32[]{:S(2)}) async-start(bf16[128,5,2,128]{3,2,1,0:T(2,128)(2,1)} %bitcast.33), calls=%async_computation | async-start | bytes 655360 | tf_op jit(solution)/shard_map/all_to_all | solution.py:488
  19.5 0.1 shard_map.96.order_ref
  19.6 3.5 %shard_map.95 = (bf16[128,768]{1,0:T(8,128)(2,1)}, f32[128,1024]{1,0:T(8,128)}, f32[128,768]{1,0:T(8,128)}, f32[128,768]{1,0:T(8,128)}, f32[512,768]{1,0:T(8,128)}) custom-call(bf16[12,48,128]{2,1,0:T(8,128)(2,1)} %acts_ref.1, f32[1,128]{1,0:T(1,128)} %bitcast.31, bf16[128,640]{1,0:T(8,128)(2,1)} %weight_ref.1, bf16[12,48,128]{2,1,0:T(8,128)(2,1)} %cotangent_hbm.1, ...), custom_call_target="tpu_custom_call" | custom-call | flops 1000000000 | bytes 2000000 | tf_op jit(solution)/shard_map/pallas_call | solution.py:533
  23.1 10.0 %all-to-all-done = bf16[128,5,2,128]{3,2,1,0:T(2,128)(2,1)S(1)} async-done(((bf16[128,5,2,128]{3,2,1,0:T(2,128)(2,1)}), bf16[128,5,2,128]{3,2,1,0:T(2,128)(2,1)S(1)}, u32[]{:S(2)}, u32[]{:S(2)}) %all-to-all-start) | async-done | bytes 327712 | tf_op jit(solution)/shard_map/all_to_all | solution.py:488
  33.1 2.6 %collective-permute-start = (bf16[1280,128]{1,0:T(8,128)(2,1)S(1)}, bf16[1280,128]{1,0:T(8,128)(2,1)S(1)}, u32[]{:S(2)}, u32[]{:S(2)}) collective-permute-start(bf16[1280,128]{1,0:T(8,128)(2,1)S(1)} %bitcast.23), channel_id=1, source_target_pairs={{0,8},{8,0},{1,9},{9,1},{2,10},{10,2},{3,11},{11,3},{4,12},{12,4},... | collective-permute-start | bytes 983048 | tf_op jit(solution)/shard_map/ppermute | solution.py:492
  35.7 0.7 shard_map.97
  36.4 0.0 copy-start.1
  36.4 0.0 copy-start.2
  36.4 0.0 copy-start.3
  36.4 0.5 collective-permute-done.theirs_ref
  37.0 0.7 shard_map.98
  37.7 17.9 %all_to_all.30 = bf16[128,3,2,128]{3,2,1,0:T(2,128)(2,1)S(1)} all-to-all(bf16[128,3,2,128]{3,2,1,0:T(2,128)(2,1)S(1)} %bitcast.28), channel_id=1, replica_groups=mesh['chip'=16,'core'=2,'col'=8] {'col','chip'}, dimensions={0} | all-to-all | bytes 393216 | tf_op jit(solution)/shard_map/all_to_all | solution.py:488
  55.6 0.0 copy-done.1
  55.6 0.0 copy-done.2
  55.6 0.0 copy-done.3
  55.6 0.6 shard_map.99
  56.2 17.8 %all_to_all.31 = bf16[128,3,2,128]{3,2,1,0:T(2,128)(2,1)S(1)} all-to-all(bf16[128,3,2,128]{3,2,1,0:T(2,128)(2,1)S(1)} %bitcast.27), channel_id=1, replica_groups=mesh['chip'=16,'core'=2,'col'=8] {'col','chip'}, dimensions={0} | all-to-all | bytes 393216 | tf_op jit(solution)/shard_map/all_to_all | solution.py:488
  74.0 3.1 %collective-permute-start.1 = (bf16[768,128]{1,0:T(8,128)(2,1)S(1)}, bf16[768,128]{1,0:T(8,128)(2,1)S(1)}, u32[]{:S(2)}, u32[]{:S(2)}) collective-permute-start(bf16[768,128]{1,0:T(8,128)(2,1)S(1)} %bitcast.25), channel_id=1, source_target_pairs={{0,8},{8,0},{1,9},{9,1},{2,10},{10,2},{3,11},{11,3},{4,12},{12,4},... | collective-permute-start | bytes 589832 | tf_op jit(solution)/shard_map/ppermute | solution.py:492
  77.1 0.1 shard_map.102.left_ref
  77.2 0.6 shard_map.101
  77.9 0.0 copy-start
  77.9 0.3 collective-permute-done.1.theirs_ref
  78.2 0.9 shard_map.103
  79.0 20.0 %all_to_all.32 = bf16[128,5,2,128]{3,2,1,0:T(2,128)(2,1)S(1)} all-to-all(bf16[128,5,2,128]{3,2,1,0:T(2,128)(2,1)S(1)} %bitcast.19), channel_id=1, replica_groups=mesh['chip'=16,'core'=2,'col'=8] {'col','chip'}, dimensions={0} | all-to-all | bytes 655360 | tf_op jit(solution)/shard_map/all_to_all | solution.py:488
  99.0 0.0 copy-start.7
  99.0 0.0 copy-done
  99.0 0.5 shard_map.104
  99.6 20.0 %all_to_all.33 = bf16[256,1,2,128]{3,2,1,0:T(2,128)(2,1)S(1)} all-to-all(bf16[256,1,2,128]{3,2,1,0:T(2,128)(2,1)S(1)} %bitcast.29), channel_id=1, replica_groups=mesh['chip'=16,'core'=2,'col'=8] {'chip','core','col'}, dimensions={0} | all-to-all | bytes 262144 | tf_op jit(solution)/shard_map/all_to_all | solution.py:488
  119.5 0.7 shard_map.106
  120.3 6.1 %all-to-all-start.5 = ((bf16[256,1,2,128]{3,2,1,0:T(2,128)(2,1)}), bf16[256,1,2,128]{3,2,1,0:T(2,128)(2,1)S(1)}, u32[]{:S(2)}, u32[]{:S(2)}) async-start(bf16[256,1,2,128]{3,2,1,0:T(2,128)(2,1)} %bitcast.14), calls=%async_computation.5 | async-start | bytes 262144 | tf_op jit(solution)/shard_map/all_to_all | solution.py:488
  126.3 0.0 copy-done.7
  126.3 0.0 copy-start.4
  126.4 0.0 copy-start.5
  126.4 0.0 copy-start.6
  126.4 0.8 shard_map.100
  127.2 0.1 copy-done.4
  127.3 0.1 copy-done.5
  127.3 0.0 copy-done.6
  127.3 1.2 shard_map.105
  128.5 10.6 %all-to-all-done.5 = bf16[256,1,2,128]{3,2,1,0:T(2,128)(2,1)S(1)} async-done(((bf16[256,1,2,128]{3,2,1,0:T(2,128)(2,1)}), bf16[256,1,2,128]{3,2,1,0:T(2,128)(2,1)S(1)}, u32[]{:S(2)}, u32[]{:S(2)}) %all-to-all-start.5) | async-done | bytes 131104 | tf_op jit(solution)/shard_map/all_to_all | solution.py:488
  139.1 0.8 shard_map.107
Async XLA Ops:
  3.1 29.9 %all-to-all-start = ((bf16[128,5,2,128]{3,2,1,0:T(2,128)(2,1)}), bf16[128,5,2,128]{3,2,1,0:T(2,128)(2,1)S(1)}, u32[]{:S(2)}, u32[]{:S(2)}) async-start(bf16[128,5,2,128]{3,2,1,0:T(2,128)(2,1)} %bitcast.33), calls=%async_computation | async-start | bytes 655360 | tf_op jit(solution)/shard_map/all_to_all | solution.py:488
  33.1 3.9 %collective-permute-start = (bf16[1280,128]{1,0:T(8,128)(2,1)S(1)}, bf16[1280,128]{1,0:T(8,128)(2,1)S(1)}, u32[]{:S(2)}, u32[]{:S(2)}) collective-permute-start(bf16[1280,128]{1,0:T(8,128)(2,1)S(1)} %bitcast.23), channel_id=1, source_target_pairs={{0,8},{8,0},{1,9},{9,1},{2,10},{10,2},{3,11},{11,3},{4,12},{12,4},... | collective-permute-start | bytes 983048 | tf_op jit(solution)/shard_map/ppermute | solution.py:492
  36.4 19.2 %copy-start.1 = (bf16[128,768]{1,0:T(8,128)(2,1)S(1)}, bf16[128,768]{1,0:T(8,128)(2,1)}, u32[]{:S(2)}) copy-start(bf16[128,768]{1,0:T(8,128)(2,1)} %get-tuple-element.39.normed_ref) | copy-start | bytes 589828
  36.4 19.2 %copy-start.2 = (f32[128,1024]{1,0:T(8,128)S(1)}, f32[128,1024]{1,0:T(8,128)}, u32[]{:S(2)}) copy-start(f32[128,1024]{1,0:T(8,128)} %get-tuple-element.40.back_norm_ref) | copy-start | bytes 1572868
  36.4 19.2 %copy-start.3 = (f32[128,768]{1,0:T(8,128)S(1)}, f32[128,768]{1,0:T(8,128)}, u32[]{:S(2)}) copy-start(f32[128,768]{1,0:T(8,128)} %get-tuple-element.41.gate_coef_ref) | copy-start | bytes 1179652
  74.0 4.2 %collective-permute-start.1 = (bf16[768,128]{1,0:T(8,128)(2,1)S(1)}, bf16[768,128]{1,0:T(8,128)(2,1)S(1)}, u32[]{:S(2)}, u32[]{:S(2)}) collective-permute-start(bf16[768,128]{1,0:T(8,128)(2,1)S(1)} %bitcast.25), channel_id=1, source_target_pairs={{0,8},{8,0},{1,9},{9,1},{2,10},{10,2},{3,11},{11,3},{4,12},{12,4},... | collective-permute-start | bytes 589832 | tf_op jit(solution)/shard_map/ppermute | solution.py:492
  77.9 21.2 %copy-start = (f32[512,768]{1,0:T(8,128)S(1)}, f32[512,768]{1,0:T(8,128)}, u32[]{:S(2)}) copy-start(f32[512,768]{1,0:T(8,128)} %get-tuple-element.50.coef_ref) | copy-start | bytes 4718596
  99.0 27.3 %copy-start.7 = (f32[128,768]{1,0:T(8,128)S(1)}, f32[128,768]{1,0:T(8,128)}, u32[]{:S(2)}) copy-start(f32[128,768]{1,0:T(8,128)} %get-tuple-element.30.gate_mask_ref) | copy-start | bytes 1179652
  120.3 18.8 %all-to-all-start.5 = ((bf16[256,1,2,128]{3,2,1,0:T(2,128)(2,1)}), bf16[256,1,2,128]{3,2,1,0:T(2,128)(2,1)S(1)}, u32[]{:S(2)}, u32[]{:S(2)}) async-start(bf16[256,1,2,128]{3,2,1,0:T(2,128)(2,1)} %bitcast.14), calls=%async_computation.5 | async-start | bytes 262144 | tf_op jit(solution)/shard_map/all_to_all | solution.py:488
  126.3 0.9 copy-start.4
  126.4 1.0 copy-start.5
  126.4 1.0 copy-start.6

commit v10 on v9

--- a/solution.py
+++ b/solution.py
@@ -11,8 +11,8 @@
 EPSILON = 1e-05
 BF16 = jnp.bfloat16
 F32 = jnp.float32
-ALL_AXES = ("chip", "core", "col")
-CHANNEL_AXES = ("col", "chip")
+ALL_AXES = ("zh", "x", "col", "core")
+CHANNEL_AXES = ("col", "x", "zh")
 LANES = 128
 SLOT = 64
 PIECE = 16
@@ -60,7 +60,7 @@
 def masks(valid_ref, na, nb):
     lane = lax.broadcasted_iota(jnp.int32, (1, LANES), 1)
     place = lane % SLOT
-    first_row = (2 * lax.axis_index("chip") + lax.axis_index("core")) * na
+    first_row = lax.axis_index(("x", "zh", "core")) * na
     first_col = lax.axis_index("col") * nb
     cols = jnp.zeros((1, LANES), jnp.int32)
     for b in range(nb):
@@ -429,13 +429,8 @@
                 back_proj_ref[rows, at] = (upstreams[tiles * side + t] * coef_ref[rows, at]).astype(BF16)
     term = matmul(normed_ref[...], back_proj_ref[0 : 4 * hidden, :], NT)
     for t in range(4):
-        for m in range(hidden // 8):
-            term_chunk_ref[weight_rows(m, t), :] = term[8 * m : 8 * m + 8, t * LANES : (t + 1) * LANES]
+        put_device_rows(term_chunk_ref, 4, t, term[:, t * LANES : (t + 1) * LANES])
     term_ref[...] = term_chunk_ref[...].astype(BF16)
-
-
-def weight_rows(chip, t):
-    return pl.ds(2 * (16 * chip + 8 * (t // 2)) + t % 2, 8, stride=2)
 
 
 def sum_kernel(full_len, parts_ref, out_ref):
@@ -454,8 +449,7 @@
 def grad_weight_kernel(sums_ref, gate_total_ref, out_ref, chunk_ref):
     chunk_ref[...] = sums_ref[...].astype(F32)
     for t in range(4):
-        for m in range(out_ref.shape[0] // 8):
-            out_ref[8 * m : 8 * m + 8, t * LANES : (t + 1) * LANES] = chunk_ref[weight_rows(m, t), :]
+        out_ref[:, t * LANES : (t + 1) * LANES] = device_rows(chunk_ref, 4, t)
     out_ref[:, 4 * LANES :] = gate_total_ref[...]
 
 
@@ -647,8 +641,8 @@
 
 def solution(mesh):
     rows, cols = mesh.devices.shape
-    split = Mesh(mesh.devices.reshape(rows // 2, 2, cols), ("chip", "core", "col"))
-    pairs = P(("chip", "core"), "col", None)
+    split = Mesh(mesh.devices.reshape(rows // 8, 4, 2, cols), ("x", "zh", "core", "col"))
+    pairs = P(("x", "zh", "core"), "col", None)
     return jax.shard_map(
         per_device,
         mesh=split,

time: 140 us -> 140 us (level)
  no operation moved by 1% of the time
where the time goes in v10:
time: 140 us
  blocking collectives  75.8 us (54%)
  starting transfers between devices  27.8 us (20%)
  waiting for transfers between devices  21.6 us (15%)
  Pallas kernels  13.7 us (10%)
    all_to_all x4, blocking collectives, exchange(): return lax.all_to_all(split, axes, 0, 0, tiled=True).reshape(chunks.shape)  75.8 us
    all_to_all x2, starting transfers between devices, exchange(): return lax.all_to_all(split, axes, 0, 0, tiled=True).reshape(chunks.shape)  22.1 us
    all_to_all x2, waiting for transfers between devices, exchange(): return lax.all_to_all(split, axes, 0, 0, tiled=True).reshape(chunks.shape)  20.7 us
    ppermute x2, starting transfers between devices, other_core(): return lax.ppermute(values, 'core', [(0, 1), (1, 0)])  5.73 us
    pallas_call x1, Pallas kernels, per_device(): local_call(ready_kernel, (array((channels, lanes)), array((hidden, lanes...  3.46 us
  transfers between devices with their start and end apart: 4, of which 4 were waited for; matrix products, arithmetic and copies ran while one was open for 0% of the time, Pallas kernels for 5%

profile of v10, /device:TPU:1, one launch (start us, length us, event | category | flops | bytes accessed | tf_op | source)
XLA Modules:
  0.0 139.9 jit_solution(5660460973337456340)
XLA Ops:
  0.6 2.5 %shard_map.94 = (bf16[1280,128]{1,0:T(8,128)(2,1)}, f32[1,768]{1,0:T(1,128)}) custom-call(s32[384]{0:T(512)} %valid_hbm.1, bf16[12,48,128]{2,1,0:T(8,128)(2,1)} %acts_ref.1, f32[1,128]{1,0:T(1,128)} %bitcast.30, bf16[128,640]{1,0:T(8,128)(2,1)} %weight_ref.1), custom_call_target="tpu_custom_call" | custom-call | flops 100000000 | bytes 2000000 | tf_op jit(solution)/shard_map/pallas_call | solution.py:507
  3.1 16.3 %all-to-all-start = ((bf16[128,5,2,128]{3,2,1,0:T(2,128)(2,1)}), bf16[128,5,2,128]{3,2,1,0:T(2,128)(2,1)S(1)}, u32[]{:S(2)}, u32[]{:S(2)}) async-start(bf16[128,5,2,128]{3,2,1,0:T(2,128)(2,1)} %bitcast.33), calls=%async_computation | async-start | bytes 655360 | tf_op jit(solution)/shard_map/all_to_all | solution.py:482
  19.5 0.1 shard_map.96.order_ref
  19.6 3.5 %shard_map.95 = (bf16[128,768]{1,0:T(8,128)(2,1)}, f32[128,1024]{1,0:T(8,128)}, f32[128,768]{1,0:T(8,128)}, f32[128,768]{1,0:T(8,128)}, f32[512,768]{1,0:T(8,128)}) custom-call(bf16[12,48,128]{2,1,0:T(8,128)(2,1)} %acts_ref.1, f32[1,128]{1,0:T(1,128)} %bitcast.31, bf16[128,640]{1,0:T(8,128)(2,1)} %weight_ref.1, bf16[12,48,128]{2,1,0:T(8,128)(2,1)} %cotangent_hbm.1, ...), custom_call_target="tpu_custom_call" | custom-call | flops 1000000000 | bytes 2000000 | tf_op jit(solution)/shard_map/pallas_call | solution.py:527
  23.1 10.0 %all-to-all-done = bf16[128,5,2,128]{3,2,1,0:T(2,128)(2,1)S(1)} async-done(((bf16[128,5,2,128]{3,2,1,0:T(2,128)(2,1)}), bf16[128,5,2,128]{3,2,1,0:T(2,128)(2,1)S(1)}, u32[]{:S(2)}, u32[]{:S(2)}) %all-to-all-start) | async-done | bytes 327712 | tf_op jit(solution)/shard_map/all_to_all | solution.py:482
  33.1 2.6 %collective-permute-start = (bf16[1280,128]{1,0:T(8,128)(2,1)S(1)}, bf16[1280,128]{1,0:T(8,128)(2,1)S(1)}, u32[]{:S(2)}, u32[]{:S(2)}) collective-permute-start(bf16[1280,128]{1,0:T(8,128)(2,1)S(1)} %bitcast.23), channel_id=1, source_target_pairs={{0,8},{8,0},{1,9},{9,1},{2,10},{10,2},{3,11},{11,3},{4,12},{12,4},... | collective-permute-start | bytes 983048 | tf_op jit(solution)/shard_map/ppermute | solution.py:486
  35.7 0.7 shard_map.97
  36.4 0.0 copy-start.1
  36.4 0.0 copy-start.2
  36.4 0.0 copy-start.3
  36.4 0.5 collective-permute-done.theirs_ref
  37.0 0.7 shard_map.98
  37.7 17.9 %all_to_all.30 = bf16[128,3,2,128]{3,2,1,0:T(2,128)(2,1)S(1)} all-to-all(bf16[128,3,2,128]{3,2,1,0:T(2,128)(2,1)S(1)} %bitcast.28), channel_id=1, replica_groups=mesh['x'=4,'zh'=4,'core'=2,'col'=8] {'col','x','zh'}, dimensions={0} | all-to-all | bytes 393216 | tf_op jit(solution)/shard_map/all_to_all | solution.py:482
  55.6 0.0 copy-done.1
  55.6 0.0 copy-done.2
  55.6 0.0 copy-done.3
  55.6 0.6 shard_map.99
  56.2 17.8 %all_to_all.31 = bf16[128,3,2,128]{3,2,1,0:T(2,128)(2,1)S(1)} all-to-all(bf16[128,3,2,128]{3,2,1,0:T(2,128)(2,1)S(1)} %bitcast.27), channel_id=1, replica_groups=mesh['x'=4,'zh'=4,'core'=2,'col'=8] {'col','x','zh'}, dimensions={0} | all-to-all | bytes 393216 | tf_op jit(solution)/shard_map/all_to_all | solution.py:482
  74.0 3.1 %collective-permute-start.1 = (bf16[768,128]{1,0:T(8,128)(2,1)S(1)}, bf16[768,128]{1,0:T(8,128)(2,1)S(1)}, u32[]{:S(2)}, u32[]{:S(2)}) collective-permute-start(bf16[768,128]{1,0:T(8,128)(2,1)S(1)} %bitcast.25), channel_id=1, source_target_pairs={{0,8},{8,0},{1,9},{9,1},{2,10},{10,2},{3,11},{11,3},{4,12},{12,4},... | collective-permute-start | bytes 589832 | tf_op jit(solution)/shard_map/ppermute | solution.py:486
  77.1 0.1 shard_map.102.left_ref
  77.2 0.6 shard_map.101
  77.9 0.0 copy-start
  77.9 0.3 collective-permute-done.1.theirs_ref
  78.2 0.9 shard_map.103
  79.0 20.0 %all_to_all.32 = bf16[128,5,2,128]{3,2,1,0:T(2,128)(2,1)S(1)} all-to-all(bf16[128,5,2,128]{3,2,1,0:T(2,128)(2,1)S(1)} %bitcast.19), channel_id=1, replica_groups=mesh['x'=4,'zh'=4,'core'=2,'col'=8] {'col','x','zh'}, dimensions={0} | all-to-all | bytes 655360 | tf_op jit(solution)/shard_map/all_to_all | solution.py:482
  99.0 0.0 copy-start.7
  99.0 0.0 copy-done
  99.0 0.5 shard_map.104
  99.6 20.2 %all_to_all.33 = bf16[256,1,2,128]{3,2,1,0:T(2,128)(2,1)S(1)} all-to-all(bf16[256,1,2,128]{3,2,1,0:T(2,128)(2,1)S(1)} %bitcast.29), channel_id=1, replica_groups=mesh['x'=4,'zh'=4,'core'=2,'col'=8] {'zh','x','col','core'}, dimensions={0} | all-to-all | bytes 262144 | tf_op jit(solution)/shard_map/all_to_all | solution.py:482
  119.7 0.7 shard_map.106
  120.4 5.7 %all-to-all-start.5 = ((bf16[256,1,2,128]{3,2,1,0:T(2,128)(2,1)}), bf16[256,1,2,128]{3,2,1,0:T(2,128)(2,1)S(1)}, u32[]{:S(2)}, u32[]{:S(2)}) async-start(bf16[256,1,2,128]{3,2,1,0:T(2,128)(2,1)} %bitcast.14), calls=%async_computation.5 | async-start | bytes 262144 | tf_op jit(solution)/shard_map/all_to_all | solution.py:482
  126.2 0.0 copy-done.7
  126.2 0.0 copy-start.4
  126.2 0.0 copy-start.5
  126.2 0.0 copy-start.6
  126.2 0.8 shard_map.100
  127.0 0.1 copy-done.4
  127.1 0.1 copy-done.5
  127.2 0.0 copy-done.6
  127.2 1.2 shard_map.105
  128.3 10.8 %all-to-all-done.5 = bf16[256,1,2,128]{3,2,1,0:T(2,128)(2,1)S(1)} async-done(((bf16[256,1,2,128]{3,2,1,0:T(2,128)(2,1)}), bf16[256,1,2,128]{3,2,1,0:T(2,128)(2,1)S(1)}, u32[]{:S(2)}, u32[]{:S(2)}) %all-to-all-start.5) | async-done | bytes 131104 | tf_op jit(solution)/shard_map/all_to_all | solution.py:482
  139.1 0.8 shard_map.107
Async XLA Ops:
  3.1 29.9 %all-to-all-start = ((bf16[128,5,2,128]{3,2,1,0:T(2,128)(2,1)}), bf16[128,5,2,128]{3,2,1,0:T(2,128)(2,1)S(1)}, u32[]{:S(2)}, u32[]{:S(2)}) async-start(bf16[128,5,2,128]{3,2,1,0:T(2,128)(2,1)} %bitcast.33), calls=%async_computation | async-start | bytes 655360 | tf_op jit(solution)/shard_map/all_to_all | solution.py:482
  33.1 3.9 %collective-permute-start = (bf16[1280,128]{1,0:T(8,128)(2,1)S(1)}, bf16[1280,128]{1,0:T(8,128)(2,1)S(1)}, u32[]{:S(2)}, u32[]{:S(2)}) collective-permute-start(bf16[1280,128]{1,0:T(8,128)(2,1)S(1)} %bitcast.23), channel_id=1, source_target_pairs={{0,8},{8,0},{1,9},{9,1},{2,10},{10,2},{3,11},{11,3},{4,12},{12,4},... | collective-permute-start | bytes 983048 | tf_op jit(solution)/shard_map/ppermute | solution.py:486
  36.4 19.2 %copy-start.1 = (bf16[128,768]{1,0:T(8,128)(2,1)S(1)}, bf16[128,768]{1,0:T(8,128)(2,1)}, u32[]{:S(2)}) copy-start(bf16[128,768]{1,0:T(8,128)(2,1)} %get-tuple-element.39.normed_ref) | copy-start | bytes 589828
  36.4 19.2 %copy-start.2 = (f32[128,1024]{1,0:T(8,128)S(1)}, f32[128,1024]{1,0:T(8,128)}, u32[]{:S(2)}) copy-start(f32[128,1024]{1,0:T(8,128)} %get-tuple-element.40.back_norm_ref) | copy-start | bytes 1572868
  36.4 19.2 %copy-start.3 = (f32[128,768]{1,0:T(8,128)S(1)}, f32[128,768]{1,0:T(8,128)}, u32[]{:S(2)}) copy-start(f32[128,768]{1,0:T(8,128)} %get-tuple-element.41.gate_coef_ref) | copy-start | bytes 1179652
  74.0 4.2 %collective-permute-start.1 = (bf16[768,128]{1,0:T(8,128)(2,1)S(1)}, bf16[768,128]{1,0:T(8,128)(2,1)S(1)}, u32[]{:S(2)}, u32[]{:S(2)}) collective-permute-start(bf16[768,128]{1,0:T(8,128)(2,1)S(1)} %bitcast.25), channel_id=1, source_target_pairs={{0,8},{8,0},{1,9},{9,1},{2,10},{10,2},{3,11},{11,3},{4,12},{12,4},... | collective-permute-start | bytes 589832 | tf_op jit(solution)/shard_map/ppermute | solution.py:486
  77.9 21.2 %copy-start = (f32[512,768]{1,0:T(8,128)S(1)}, f32[512,768]{1,0:T(8,128)}, u32[]{:S(2)}) copy-start(f32[512,768]{1,0:T(8,128)} %get-tuple-element.50.coef_ref) | copy-start | bytes 4718596
  99.0 27.1 %copy-start.7 = (f32[128,768]{1,0:T(8,128)S(1)}, f32[128,768]{1,0:T(8,128)}, u32[]{:S(2)}) copy-start(f32[128,768]{1,0:T(8,128)} %get-tuple-element.30.gate_mask_ref) | copy-start | bytes 1179652
  120.4 18.7 %all-to-all-start.5 = ((bf16[256,1,2,128]{3,2,1,0:T(2,128)(2,1)}), bf16[256,1,2,128]{3,2,1,0:T(2,128)(2,1)S(1)}, u32[]{:S(2)}, u32[]{:S(2)}) async-start(bf16[256,1,2,128]{3,2,1,0:T(2,128)(2,1)} %bitcast.14), calls=%async_computation.5 | async-start | bytes 262144 | tf_op jit(solution)/shard_map/all_to_all | solution.py:482
  126.2 0.9 copy-start.4
  126.2 1.0 copy-start.5
  126.2 1.0 copy-start.6

commit v11 on v9

--- a/solution.py
+++ b/solution.py
@@ -633,6 +633,7 @@
         pair_kernel, array(pair_acts.shape), [spread_scratch], 1_000_000_000, 4
     )(pair_acts, gain, proj_weight, back_proj)
     parts = exchange(term, 2, ALL_AXES)
+    parts, grad_pair, update = lax.optimization_barrier((parts, grad_pair, update))
     sums = local_call(functools.partial(sum_kernel, full_len), array(term_chunk), [], 100_000, 1)(parts)
     sums = exchange(sums, 2, ALL_AXES)
     grad_weight = local_call(

time: 140 us -> 140 us (level)
  starting transfers between devices: 28.1 us -> 29.6 us
    all_to_all x2, starting transfers between devices: 22.4 us -> 23.8 us  [exchange(): return lax.all_to_all(split, axes, 0, 0, tiled=True).reshape(chunks.shape)]
where the time goes in v11:
time: 140 us
  blocking collectives  74.4 us (53%)
  starting transfers between devices  29.6 us (21%)
  waiting for transfers between devices  21.2 us (15%)
  Pallas kernels  13.8 us (10%)
    all_to_all x4, blocking collectives, exchange(): return lax.all_to_all(split, axes, 0, 0, tiled=True).reshape(chunks.shape)  74.4 us
    all_to_all x2, starting transfers between devices, exchange(): return lax.all_to_all(split, axes, 0, 0, tiled=True).reshape(chunks.shape)  23.8 us
    all_to_all x2, waiting for transfers between devices, exchange(): return lax.all_to_all(split, axes, 0, 0, tiled=True).reshape(chunks.shape)  20.4 us
    ppermute x2, starting transfers between devices, other_core(): return lax.ppermute(values, 'core', [(0, 1), (1, 0)])  5.73 us
    pallas_call x1, Pallas kernels, per_device(): local_call(ready_kernel, (array((channels, lanes)), array((hidden, lanes...  3.46 us
  transfers between devices with their start and end apart: 4, of which 4 were waited for; matrix products, arithmetic and copies ran while one was open for 0% of the time, Pallas kernels for 5%

profile of v11, /device:TPU:1, one launch (start us, length us, event | category | flops | bytes accessed | tf_op | source)
XLA Modules:
  0.0 139.9 jit_solution(3404569588148739722)
XLA Ops:
  0.6 2.5 %shard_map.94 = (bf16[1280,128]{1,0:T(8,128)(2,1)}, f32[1,768]{1,0:T(1,128)}) custom-call(s32[384]{0:T(512)} %valid_hbm.1, bf16[12,48,128]{2,1,0:T(8,128)(2,1)} %acts_ref.1, f32[1,128]{1,0:T(1,128)} %bitcast.30, bf16[128,640]{1,0:T(8,128)(2,1)} %weight_ref.1), custom_call_target="tpu_custom_call" | custom-call | flops 100000000 | bytes 2000000 | tf_op jit(solution)/shard_map/pallas_call | solution.py:513
  3.1 16.3 %all-to-all-start = ((bf16[128,5,2,128]{3,2,1,0:T(2,128)(2,1)}), bf16[128,5,2,128]{3,2,1,0:T(2,128)(2,1)S(1)}, u32[]{:S(2)}, u32[]{:S(2)}) async-start(bf16[128,5,2,128]{3,2,1,0:T(2,128)(2,1)} %bitcast.33), calls=%async_computation | async-start | bytes 655360 | tf_op jit(solution)/shard_map/all_to_all | solution.py:488
  19.5 0.1 shard_map.96.order_ref
  19.6 3.5 %shard_map.95 = (bf16[128,768]{1,0:T(8,128)(2,1)}, f32[128,1024]{1,0:T(8,128)}, f32[128,768]{1,0:T(8,128)}, f32[128,768]{1,0:T(8,128)}, f32[512,768]{1,0:T(8,128)}) custom-call(bf16[12,48,128]{2,1,0:T(8,128)(2,1)} %acts_ref.1, f32[1,128]{1,0:T(1,128)} %bitcast.31, bf16[128,640]{1,0:T(8,128)(2,1)} %weight_ref.1, bf16[12,48,128]{2,1,0:T(8,128)(2,1)} %cotangent_hbm.1, ...), custom_call_target="tpu_custom_call" | custom-call | flops 1000000000 | bytes 2000000 | tf_op jit(solution)/shard_map/pallas_call | solution.py:533
  23.1 10.0 %all-to-all-done = bf16[128,5,2,128]{3,2,1,0:T(2,128)(2,1)S(1)} async-done(((bf16[128,5,2,128]{3,2,1,0:T(2,128)(2,1)}), bf16[128,5,2,128]{3,2,1,0:T(2,128)(2,1)S(1)}, u32[]{:S(2)}, u32[]{:S(2)}) %all-to-all-start) | async-done | bytes 327712 | tf_op jit(solution)/shard_map/all_to_all | solution.py:488
  33.1 2.6 %collective-permute-start = (bf16[1280,128]{1,0:T(8,128)(2,1)S(1)}, bf16[1280,128]{1,0:T(8,128)(2,1)S(1)}, u32[]{:S(2)}, u32[]{:S(2)}) collective-permute-start(bf16[1280,128]{1,0:T(8,128)(2,1)S(1)} %bitcast.24), channel_id=1, source_target_pairs={{0,8},{8,0},{1,9},{9,1},{2,10},{10,2},{3,11},{11,3},{4,12},{12,4},... | collective-permute-start | bytes 983048 | tf_op jit(solution)/shard_map/ppermute | solution.py:492
  35.7 0.7 shard_map.97
  36.4 0.0 copy-start.1
  36.4 0.0 copy-start.2
  36.4 0.0 copy-start.3
  36.4 0.5 collective-permute-done.theirs_ref
  37.0 0.7 shard_map.98
  37.7 17.9 %all_to_all.30 = bf16[128,3,2,128]{3,2,1,0:T(2,128)(2,1)S(1)} all-to-all(bf16[128,3,2,128]{3,2,1,0:T(2,128)(2,1)S(1)} %bitcast.29), channel_id=1, replica_groups=mesh['chip'=16,'core'=2,'col'=8] {'col','chip'}, dimensions={0} | all-to-all | bytes 393216 | tf_op jit(solution)/shard_map/all_to_all | solution.py:488
  55.6 0.0 copy-done.1
  55.6 0.0 copy-done.2
  55.6 0.0 copy-done.3
  55.6 0.6 shard_map.99
  56.2 17.8 %all_to_all.31 = bf16[128,3,2,128]{3,2,1,0:T(2,128)(2,1)S(1)} all-to-all(bf16[128,3,2,128]{3,2,1,0:T(2,128)(2,1)S(1)} %bitcast.28), channel_id=1, replica_groups=mesh['chip'=16,'core'=2,'col'=8] {'col','chip'}, dimensions={0} | all-to-all | bytes 393216 | tf_op jit(solution)/shard_map/all_to_all | solution.py:488
  74.0 3.1 %collective-permute-start.1 = (bf16[768,128]{1,0:T(8,128)(2,1)S(1)}, bf16[768,128]{1,0:T(8,128)(2,1)S(1)}, u32[]{:S(2)}, u32[]{:S(2)}) collective-permute-start(bf16[768,128]{1,0:T(8,128)(2,1)S(1)} %bitcast.26), channel_id=1, source_target_pairs={{0,8},{8,0},{1,9},{9,1},{2,10},{10,2},{3,11},{11,3},{4,12},{12,4},... | collective-permute-start | bytes 589832 | tf_op jit(solution)/shard_map/ppermute | solution.py:492
  77.1 0.1 shard_map.101.left_ref
  77.2 0.6 shard_map.100
  77.9 0.0 copy-start
  77.9 0.3 collective-permute-done.1.theirs_ref
  78.2 0.9 shard_map.102
  79.0 0.0 copy-start.7
  79.0 20.1 %all_to_all.32 = bf16[128,5,2,128]{3,2,1,0:T(2,128)(2,1)S(1)} all-to-all(bf16[128,5,2,128]{3,2,1,0:T(2,128)(2,1)S(1)} %bitcast.19), channel_id=1, replica_groups=mesh['chip'=16,'core'=2,'col'=8] {'col','chip'}, dimensions={0} | all-to-all | bytes 655360 | tf_op jit(solution)/shard_map/all_to_all | solution.py:488
  99.2 0.0 copy-done
  99.2 1.2 shard_map.103
  100.4 7.5 %all-to-all-start.4 = ((bf16[256,1,2,128]{3,2,1,0:T(2,128)(2,1)}), bf16[256,1,2,128]{3,2,1,0:T(2,128)(2,1)S(1)}, u32[]{:S(2)}, u32[]{:S(2)}) async-start(bf16[256,1,2,128]{3,2,1,0:T(2,128)(2,1)} %bitcast.11), calls=%async_computation.4 | async-start | bytes 262144 | tf_op jit(solution)/shard_map/all_to_all | solution.py:488
  107.9 0.0 copy-done.7
  107.9 0.0 copy-start.4
  107.9 0.0 copy-start.5
  107.9 0.0 copy-start.6
  107.9 0.8 shard_map.105
  108.7 0.1 copy-done.4
  108.8 0.1 copy-done.5
  108.9 0.0 copy-done.6
  108.9 1.2 shard_map.104
  110.0 10.4 %all-to-all-done.4 = bf16[256,1,2,128]{3,2,1,0:T(2,128)(2,1)S(1)} async-done(((bf16[256,1,2,128]{3,2,1,0:T(2,128)(2,1)}), bf16[256,1,2,128]{3,2,1,0:T(2,128)(2,1)S(1)}, u32[]{:S(2)}, u32[]{:S(2)}) %all-to-all-start.4) | async-done | bytes 131104 | tf_op jit(solution)/shard_map/all_to_all | solution.py:488
  120.5 0.1 shard_map.106
  120.5 18.6 %all_to_all.33 = bf16[256,1,2,128]{3,2,1,0:T(2,128)(2,1)S(1)} all-to-all(bf16[256,1,2,128]{3,2,1,0:T(2,128)(2,1)S(1)} %bitcast.22), channel_id=1, replica_groups=mesh['chip'=16,'core'=2,'col'=8] {'chip','core','col'}, dimensions={0} | all-to-all | bytes 262144 | tf_op jit(solution)/shard_map/all_to_all | solution.py:488
  139.1 0.8 shard_map.107
Async XLA Ops:
  3.1 29.9 %all-to-all-start = ((bf16[128,5,2,128]{3,2,1,0:T(2,128)(2,1)}), bf16[128,5,2,128]{3,2,1,0:T(2,128)(2,1)S(1)}, u32[]{:S(2)}, u32[]{:S(2)}) async-start(bf16[128,5,2,128]{3,2,1,0:T(2,128)(2,1)} %bitcast.33), calls=%async_computation | async-start | bytes 655360 | tf_op jit(solution)/shard_map/all_to_all | solution.py:488
  33.1 3.9 %collective-permute-start = (bf16[1280,128]{1,0:T(8,128)(2,1)S(1)}, bf16[1280,128]{1,0:T(8,128)(2,1)S(1)}, u32[]{:S(2)}, u32[]{:S(2)}) collective-permute-start(bf16[1280,128]{1,0:T(8,128)(2,1)S(1)} %bitcast.24), channel_id=1, source_target_pairs={{0,8},{8,0},{1,9},{9,1},{2,10},{10,2},{3,11},{11,3},{4,12},{12,4},... | collective-permute-start | bytes 983048 | tf_op jit(solution)/shard_map/ppermute | solution.py:492
  36.4 19.2 %copy-start.1 = (bf16[128,768]{1,0:T(8,128)(2,1)S(1)}, bf16[128,768]{1,0:T(8,128)(2,1)}, u32[]{:S(2)}) copy-start(bf16[128,768]{1,0:T(8,128)(2,1)} %get-tuple-element.41.normed_ref) | copy-start | bytes 589828
  36.4 19.2 %copy-start.2 = (f32[128,1024]{1,0:T(8,128)S(1)}, f32[128,1024]{1,0:T(8,128)}, u32[]{:S(2)}) copy-start(f32[128,1024]{1,0:T(8,128)} %get-tuple-element.42.back_norm_ref) | copy-start | bytes 1572868
  36.4 19.2 %copy-start.3 = (f32[128,768]{1,0:T(8,128)S(1)}, f32[128,768]{1,0:T(8,128)}, u32[]{:S(2)}) copy-start(f32[128,768]{1,0:T(8,128)} %get-tuple-element.43.gate_coef_ref) | copy-start | bytes 1179652
  74.0 4.2 %collective-permute-start.1 = (bf16[768,128]{1,0:T(8,128)(2,1)S(1)}, bf16[768,128]{1,0:T(8,128)(2,1)S(1)}, u32[]{:S(2)}, u32[]{:S(2)}) collective-permute-start(bf16[768,128]{1,0:T(8,128)(2,1)S(1)} %bitcast.26), channel_id=1, source_target_pairs={{0,8},{8,0},{1,9},{9,1},{2,10},{10,2},{3,11},{11,3},{4,12},{12,4},... | collective-permute-start | bytes 589832 | tf_op jit(solution)/shard_map/ppermute | solution.py:492
  77.9 21.3 %copy-start = (f32[512,768]{1,0:T(8,128)S(1)}, f32[512,768]{1,0:T(8,128)}, u32[]{:S(2)}) copy-start(f32[512,768]{1,0:T(8,128)} %get-tuple-element.51.coef_ref) | copy-start | bytes 4718596
  79.0 28.8 %copy-start.7 = (f32[128,768]{1,0:T(8,128)S(1)}, f32[128,768]{1,0:T(8,128)}, u32[]{:S(2)}) copy-start(f32[128,768]{1,0:T(8,128)} %get-tuple-element.55.gate_mask_ref) | copy-start | bytes 1179652
  100.4 20.1 %all-to-all-start.4 = ((bf16[256,1,2,128]{3,2,1,0:T(2,128)(2,1)}), bf16[256,1,2,128]{3,2,1,0:T(2,128)(2,1)S(1)}, u32[]{:S(2)}, u32[]{:S(2)}) async-start(bf16[256,1,2,128]{3,2,1,0:T(2,128)(2,1)} %bitcast.11), calls=%async_computation.4 | async-start | bytes 262144 | tf_op jit(solution)/shard_map/all_to_all | solution.py:488
  107.9 0.9 copy-start.4
  107.9 1.0 copy-start.5
  107.9 1.0 copy-start.6

commit v12 on v9

--- a/solution.py
+++ b/solution.py
@@ -374,6 +374,11 @@
     return total
 
 
+def tile_rows(na, pair, lo, t, side):
+    start = 8 * (((2 * pair + lo) * (na // 2) + t) * 2 + side)
+    return slice(start, start + 8)
+
+
 def own_back_kernel(
     na, mine_ref, left_ref, right_ref, order_ref, back_left_ref, back_right_ref, total_ref,
     chunk_ref, plane_ref, turned_ref,
@@ -382,7 +387,13 @@
     chunk_ref[...] = mine_ref[...].astype(F32)
     back_plane(na, chunk_ref, plane_ref)
     turned_ref[...] = matmul(plane_ref[...], order_ref[...], NT).astype(BF16)
-    back_left_ref[...] = matmul(turned_ref[...], right_ref[...])
+    back_left = matmul(turned_ref[...], right_ref[...])
+    for pair in range(4):
+        for lo in range(2):
+            for t in range(na // 2):
+                rows = back_left[plane_rows(na, lo, t), pair * LANES : (pair + 1) * LANES]
+                for side, tile in enumerate(chunk_tiles(rows)):
+                    back_left_ref[tile_rows(na, pair, lo, t, side), :] = tile
     back_right_ref[...] = matmul(turned_ref[:, 0:half], left_ref[...], TN)
     total_ref[...] = gap_total(chunk_ref)
 
@@ -403,7 +414,10 @@
     for pair in range(4):
         at = slice(pair * LANES, (pair + 1) * LANES)
         for lo in range(2):
-            found = [chunk_tiles(back_left_ref[plane_rows(na, lo, t), at]) for t in range(tiles)]
+            found = [
+                [back_left_ref[tile_rows(na, pair, lo, t, side), :] for side in range(2)]
+                for t in range(tiles)
+            ]
             found += [chunk_tiles(back_right[plane_rows(na, lo, t), at]) for t in range(tiles)]
             for side in range(2):
                 for t, row in enumerate(pack_tiles([both[side] for both in found])):
@@ -600,7 +614,7 @@
     )(side_theirs)
     back_left, back_right, total = local_call(
         functools.partial(own_back_kernel, na),
-        (array(half_plane, F32), array(half_plane, F32), array((8, LANES), F32)),
+        (array(tri_chunk, F32), array(half_plane, F32), array((8, LANES), F32)),
         [
             pltpu.VMEM(tri_chunk, F32),
             pltpu.VMEM(half_plane, BF16),

time: 140 us -> 140 us (level)
  no operation moved by 1% of the time
where the time goes in v12:
time: 140 us
  blocking collectives  75.6 us (54%)
  starting transfers between devices  28.1 us (20%)
  waiting for transfers between devices  21.3 us (15%)
  Pallas kernels  13.8 us (10%)
    all_to_all x4, blocking collectives, exchange(): return lax.all_to_all(split, axes, 0, 0, tiled=True).reshape(chunks.shape)  75.6 us
    all_to_all x2, starting transfers between devices, exchange(): return lax.all_to_all(split, axes, 0, 0, tiled=True).reshape(chunks.shape)  22.4 us
    all_to_all x2, waiting for transfers between devices, exchange(): return lax.all_to_all(split, axes, 0, 0, tiled=True).reshape(chunks.shape)  20.5 us
    ppermute x2, starting transfers between devices, other_core(): return lax.ppermute(values, 'core', [(0, 1), (1, 0)])  5.73 us
    pallas_call x1, Pallas kernels, per_device(): local_call(ready_kernel, (array((channels, lanes)), array((hidden, lanes...  3.46 us
  transfers between devices with their start and end apart: 4, of which 4 were waited for; matrix products, arithmetic and copies ran while one was open for 0% of the time, Pallas kernels for 5%

profile of v12, /device:TPU:1, one launch (start us, length us, event | category | flops | bytes accessed | tf_op | source)
XLA Modules:
  0.0 139.8 jit_solution(15462261647620818836)
XLA Ops:
  0.6 2.5 %shard_map.94 = (bf16[1280,128]{1,0:T(8,128)(2,1)}, f32[1,768]{1,0:T(1,128)}) custom-call(s32[384]{0:T(512)} %valid_hbm.1, bf16[12,48,128]{2,1,0:T(8,128)(2,1)} %acts_ref.1, f32[1,128]{1,0:T(1,128)} %bitcast.30, bf16[128,640]{1,0:T(8,128)(2,1)} %weight_ref.1), custom_call_target="tpu_custom_call" | custom-call | flops 100000000 | bytes 2000000 | tf_op jit(solution)/shard_map/pallas_call | solution.py:527
  3.1 16.3 %all-to-all-start = ((bf16[128,5,2,128]{3,2,1,0:T(2,128)(2,1)}), bf16[128,5,2,128]{3,2,1,0:T(2,128)(2,1)S(1)}, u32[]{:S(2)}, u32[]{:S(2)}) async-start(bf16[128,5,2,128]{3,2,1,0:T(2,128)(2,1)} %bitcast.33), calls=%async_computation | async-start | bytes 655360 | tf_op jit(solution)/shard_map/all_to_all | solution.py:502
  19.5 0.1 shard_map.96.order_ref
  19.6 3.5 %shard_map.95 = (bf16[128,768]{1,0:T(8,128)(2,1)}, f32[128,1024]{1,0:T(8,128)}, f32[128,768]{1,0:T(8,128)}, f32[128,768]{1,0:T(8,128)}, f32[512,768]{1,0:T(8,128)}) custom-call(bf16[12,48,128]{2,1,0:T(8,128)(2,1)} %acts_ref.1, f32[1,128]{1,0:T(1,128)} %bitcast.31, bf16[128,640]{1,0:T(8,128)(2,1)} %weight_ref.1, bf16[12,48,128]{2,1,0:T(8,128)(2,1)} %cotangent_hbm.1, ...), custom_call_target="tpu_custom_call" | custom-call | flops 1000000000 | bytes 2000000 | tf_op jit(solution)/shard_map/pallas_call | solution.py:547
  23.1 10.0 %all-to-all-done = bf16[128,5,2,128]{3,2,1,0:T(2,128)(2,1)S(1)} async-done(((bf16[128,5,2,128]{3,2,1,0:T(2,128)(2,1)}), bf16[128,5,2,128]{3,2,1,0:T(2,128)(2,1)S(1)}, u32[]{:S(2)}, u32[]{:S(2)}) %all-to-all-start) | async-done | bytes 327712 | tf_op jit(solution)/shard_map/all_to_all | solution.py:502
  33.1 2.6 %collective-permute-start = (bf16[1280,128]{1,0:T(8,128)(2,1)S(1)}, bf16[1280,128]{1,0:T(8,128)(2,1)S(1)}, u32[]{:S(2)}, u32[]{:S(2)}) collective-permute-start(bf16[1280,128]{1,0:T(8,128)(2,1)S(1)} %bitcast.23), channel_id=1, source_target_pairs={{0,8},{8,0},{1,9},{9,1},{2,10},{10,2},{3,11},{11,3},{4,12},{12,4},... | collective-permute-start | bytes 983048 | tf_op jit(solution)/shard_map/ppermute | solution.py:506
  35.7 0.7 shard_map.97
  36.4 0.0 copy-start.1
  36.4 0.0 copy-start.2
  36.4 0.0 copy-start.3
  36.4 0.5 collective-permute-done.theirs_ref
  37.0 0.7 shard_map.98
  37.7 17.9 %all_to_all.30 = bf16[128,3,2,128]{3,2,1,0:T(2,128)(2,1)S(1)} all-to-all(bf16[128,3,2,128]{3,2,1,0:T(2,128)(2,1)S(1)} %bitcast.28), channel_id=1, replica_groups=mesh['chip'=16,'core'=2,'col'=8] {'col','chip'}, dimensions={0} | all-to-all | bytes 393216 | tf_op jit(solution)/shard_map/all_to_all | solution.py:502
  55.6 0.0 copy-done.1
  55.6 0.0 copy-done.2
  55.6 0.0 copy-done.3
  55.6 0.6 shard_map.99
  56.2 17.8 %all_to_all.31 = bf16[128,3,2,128]{3,2,1,0:T(2,128)(2,1)S(1)} all-to-all(bf16[128,3,2,128]{3,2,1,0:T(2,128)(2,1)S(1)} %bitcast.27), channel_id=1, replica_groups=mesh['chip'=16,'core'=2,'col'=8] {'col','chip'}, dimensions={0} | all-to-all | bytes 393216 | tf_op jit(solution)/shard_map/all_to_all | solution.py:502
  74.0 3.1 %collective-permute-start.1 = (bf16[768,128]{1,0:T(8,128)(2,1)S(1)}, bf16[768,128]{1,0:T(8,128)(2,1)S(1)}, u32[]{:S(2)}, u32[]{:S(2)}) collective-permute-start(bf16[768,128]{1,0:T(8,128)(2,1)S(1)} %bitcast.25), channel_id=1, source_target_pairs={{0,8},{8,0},{1,9},{9,1},{2,10},{10,2},{3,11},{11,3},{4,12},{12,4},... | collective-permute-start | bytes 589832 | tf_op jit(solution)/shard_map/ppermute | solution.py:506
  77.1 0.1 shard_map.102.left_ref
  77.2 0.7 shard_map.101
  77.9 0.0 copy-start
  77.9 0.3 collective-permute-done.1.theirs_ref
  78.2 0.9 shard_map.103
  79.0 20.0 %all_to_all.32 = bf16[128,5,2,128]{3,2,1,0:T(2,128)(2,1)S(1)} all-to-all(bf16[128,5,2,128]{3,2,1,0:T(2,128)(2,1)S(1)} %bitcast.19), channel_id=1, replica_groups=mesh['chip'=16,'core'=2,'col'=8] {'col','chip'}, dimensions={0} | all-to-all | bytes 655360 | tf_op jit(solution)/shard_map/all_to_all | solution.py:502
  99.0 0.0 copy-start.7
  99.0 0.0 copy-done
  99.0 0.5 shard_map.104
  99.6 20.0 %all_to_all.33 = bf16[256,1,2,128]{3,2,1,0:T(2,128)(2,1)S(1)} all-to-all(bf16[256,1,2,128]{3,2,1,0:T(2,128)(2,1)S(1)} %bitcast.29), channel_id=1, replica_groups=mesh['chip'=16,'core'=2,'col'=8] {'chip','core','col'}, dimensions={0} | all-to-all | bytes 262144 | tf_op jit(solution)/shard_map/all_to_all | solution.py:502
  119.5 0.7 shard_map.106
  120.2 6.1 %all-to-all-start.5 = ((bf16[256,1,2,128]{3,2,1,0:T(2,128)(2,1)}), bf16[256,1,2,128]{3,2,1,0:T(2,128)(2,1)S(1)}, u32[]{:S(2)}, u32[]{:S(2)}) async-start(bf16[256,1,2,128]{3,2,1,0:T(2,128)(2,1)} %bitcast.14), calls=%async_computation.5 | async-start | bytes 262144 | tf_op jit(solution)/shard_map/all_to_all | solution.py:502
  126.3 0.0 copy-done.7
  126.3 0.0 copy-start.4
  126.4 0.0 copy-start.5
  126.4 0.0 copy-start.6
  126.4 0.8 shard_map.100
  127.2 0.1 copy-done.4
  127.3 0.1 copy-done.5
  127.3 0.0 copy-done.6
  127.3 1.2 shard_map.105
  128.5 10.6 %all-to-all-done.5 = bf16[256,1,2,128]{3,2,1,0:T(2,128)(2,1)S(1)} async-done(((bf16[256,1,2,128]{3,2,1,0:T(2,128)(2,1)}), bf16[256,1,2,128]{3,2,1,0:T(2,128)(2,1)S(1)}, u32[]{:S(2)}, u32[]{:S(2)}) %all-to-all-start.5) | async-done | bytes 131104 | tf_op jit(solution)/shard_map/all_to_all | solution.py:502
  139.1 0.8 shard_map.107
Async XLA Ops:
  3.1 29.9 %all-to-all-start = ((bf16[128,5,2,128]{3,2,1,0:T(2,128)(2,1)}), bf16[128,5,2,128]{3,2,1,0:T(2,128)(2,1)S(1)}, u32[]{:S(2)}, u32[]{:S(2)}) async-start(bf16[128,5,2,128]{3,2,1,0:T(2,128)(2,1)} %bitcast.33), calls=%async_computation | async-start | bytes 655360 | tf_op jit(solution)/shard_map/all_to_all | solution.py:502
  33.1 3.9 %collective-permute-start = (bf16[1280,128]{1,0:T(8,128)(2,1)S(1)}, bf16[1280,128]{1,0:T(8,128)(2,1)S(1)}, u32[]{:S(2)}, u32[]{:S(2)}) collective-permute-start(bf16[1280,128]{1,0:T(8,128)(2,1)S(1)} %bitcast.23), channel_id=1, source_target_pairs={{0,8},{8,0},{1,9},{9,1},{2,10},{10,2},{3,11},{11,3},{4,12},{12,4},... | collective-permute-start | bytes 983048 | tf_op jit(solution)/shard_map/ppermute | solution.py:506
  36.4 19.2 %copy-start.1 = (bf16[128,768]{1,0:T(8,128)(2,1)S(1)}, bf16[128,768]{1,0:T(8,128)(2,1)}, u32[]{:S(2)}) copy-start(bf16[128,768]{1,0:T(8,128)(2,1)} %get-tuple-element.39.normed_ref) | copy-start | bytes 589828
  36.4 19.2 %copy-start.2 = (f32[128,1024]{1,0:T(8,128)S(1)}, f32[128,1024]{1,0:T(8,128)}, u32[]{:S(2)}) copy-start(f32[128,1024]{1,0:T(8,128)} %get-tuple-element.40.back_norm_ref) | copy-start | bytes 1572868
  36.4 19.2 %copy-start.3 = (f32[128,768]{1,0:T(8,128)S(1)}, f32[128,768]{1,0:T(8,128)}, u32[]{:S(2)}) copy-start(f32[128,768]{1,0:T(8,128)} %get-tuple-element.41.gate_coef_ref) | copy-start | bytes 1179652
  74.0 4.2 %collective-permute-start.1 = (bf16[768,128]{1,0:T(8,128)(2,1)S(1)}, bf16[768,128]{1,0:T(8,128)(2,1)S(1)}, u32[]{:S(2)}, u32[]{:S(2)}) collective-permute-start(bf16[768,128]{1,0:T(8,128)(2,1)S(1)} %bitcast.25), channel_id=1, source_target_pairs={{0,8},{8,0},{1,9},{9,1},{2,10},{10,2},{3,11},{11,3},{4,12},{12,4},... | collective-permute-start | bytes 589832 | tf_op jit(solution)/shard_map/ppermute | solution.py:506
  77.9 21.1 %copy-start = (f32[512,768]{1,0:T(8,128)S(1)}, f32[512,768]{1,0:T(8,128)}, u32[]{:S(2)}) copy-start(f32[512,768]{1,0:T(8,128)} %get-tuple-element.50.coef_ref) | copy-start | bytes 4718596
  99.0 27.3 %copy-start.7 = (f32[128,768]{1,0:T(8,128)S(1)}, f32[128,768]{1,0:T(8,128)}, u32[]{:S(2)}) copy-start(f32[128,768]{1,0:T(8,128)} %get-tuple-element.30.gate_mask_ref) | copy-start | bytes 1179652
  120.2 18.8 %all-to-all-start.5 = ((bf16[256,1,2,128]{3,2,1,0:T(2,128)(2,1)}), bf16[256,1,2,128]{3,2,1,0:T(2,128)(2,1)S(1)}, u32[]{:S(2)}, u32[]{:S(2)}) async-start(bf16[256,1,2,128]{3,2,1,0:T(2,128)(2,1)} %bitcast.14), calls=%async_computation.5 | async-start | bytes 262144 | tf_op jit(solution)/shard_map/all_to_all | solution.py:502
  126.3 0.9 copy-start.4
  126.4 1.0 copy-start.5
  126.4 1.0 copy-start.6
